TPU v7x, 128 devices: a whole 4x4x4 slice. The times are simulated.
128 devices in a mesh: atom: 16 (over x, z), aux: 8 (over y, core).
Axes of the slice: x: 4, y: 4, z: 4, core: 2. Of those that a mesh axis runs over, the one named last changes fastest.
Arguments:
- three_index: bfloat16 [256, 64, 128, 128], P('atom', 'aux'), may hold values from -6 to 6
- pair_mask: int32 [256, 8, 8], P('atom'), may hold values 0 or 1
- pair_owner: int32 [256, 1], P('atom'), may hold values from 0 to 15; in each aligned block of 16 rows (0 to 15, 16 to 31, ...) at most 2 rows name the same one
- pair_sub: int32 [256], P('atom'), may hold values from 0 to 3
- pair_nu: int32 [256], P('atom'), may hold values from 0 to 63
- live_count: int32 [16], P('atom'), may hold values from 1 to 16, 192 in all
- coefficients: bfloat16 [8192, 128], P('atom'), may hold values from -0.5 to 0.5
- fit_matrix: bfloat16 [64, 64], P('aux'), as said below
Outputs:
- exchange: float32 [8192, 8192], P('atom', 'aux')
Inputs may be any that keep to these rules, and one draw needn't show every extreme that they name: `pair_owner`: among the 16 slots of one atom index, at most 2 name the same owner, and in every draw some owner is named exactly 2 times by some atom index's slots. The first live_count[a] slots of atom index a are live; some atom index has all 16 slots live. `fit_matrix`: Symmetric.
All inputs are finite; a program needn't handle non-finite values. No bound on the sum of `pair_mask` or of `live_count` on one device may be relied on, other than what follows from the above.
Results may differ from a plain program's by a relative error of at most 0.012.
Values may be sent and summed in bfloat16 or wider, within the bound.
No kernel may reach another device: no remote copies, remote signals or barrier semaphores. Data moves between devices by JAX's collectives and lax.ppermute only.
A program may use at most 128 MiB of HBM per device.

v0:
```python
import jax
import jax.numpy as jnp
from jax import lax
from jax.sharding import PartitionSpec as P

CAP = 2


def per_device(
    three_index, pair_mask, pair_owner, pair_sub, pair_nu, live_count, coefficients, fit_matrix
):
    slot_count, aux_here, block_size, _ = three_index.shape
    rows_here, occupied = coefficients.shape
    blocks_here = rows_here // block_size
    atom_count = lax.axis_size("atom")
    aux_count = lax.axis_size("aux")
    aux_total = fit_matrix.shape[1]
    basis_total = rows_here * atom_count
    shell_size = block_size // pair_mask.shape[1]
    whole_orbitals = lax.all_gather(coefficients, "atom", axis=0, tiled=True)
    orbital_blocks = whole_orbitals.reshape(basis_total // block_size, block_size, occupied)[
        pair_nu
    ]
    expanded = jnp.repeat(jnp.repeat(pair_mask, shell_size, 1), shell_size, 2).astype(jnp.bfloat16)
    masked = three_index * expanded[:, None, :, :]
    halfway = jnp.einsum(
        "tpmn,tni->tpim", masked, orbital_blocks, preferred_element_type=jnp.float32
    )
    alive_mask = jnp.arange(slot_count) < live_count[0]
    halfway = jnp.where(alive_mask[:, None, None, None], halfway, 0.0).astype(jnp.bfloat16)
    owners = pair_owner[:, 0]
    owner_hits = (owners[:, None] == jnp.arange(atom_count)[None, :]).astype(jnp.int32)
    rank_within = jnp.sum(jnp.cumsum(owner_hits, 0) * owner_hits, 1) - 1
    placement = owners * CAP + rank_within
    routing = (jnp.arange(atom_count * CAP)[:, None] == placement[None, :]).astype(jnp.bfloat16)
    outgoing = jnp.dot(routing, halfway.reshape(slot_count, -1), preferred_element_type=jnp.float32)
    outgoing = outgoing.astype(jnp.bfloat16).reshape(
        atom_count, CAP, aux_here, occupied, block_size
    )
    sub_codes = jnp.dot(
        routing, (pair_sub + 1).astype(jnp.bfloat16)[:, None], preferred_element_type=jnp.float32
    )
    sub_codes = sub_codes.astype(jnp.bfloat16).reshape(atom_count, CAP)
    arrived, arrived_codes = (
        lax.all_to_all(outgoing, "atom", split_axis=0, concat_axis=0, tiled=True),
        lax.all_to_all(sub_codes, "atom", split_axis=0, concat_axis=0, tiled=True),
    )
    wanted = (jnp.arange(blocks_here) + 1).astype(jnp.float32)
    selector = (arrived_codes.reshape(1, -1).astype(jnp.float32) == wanted[:, None]).astype(
        jnp.bfloat16
    )
    gathered_rows = jnp.einsum(
        "sc,cpib->pisb",
        selector,
        arrived.reshape(atom_count * CAP, aux_here, occupied, block_size),
        preferred_element_type=jnp.float32,
    )
    local_rows = gathered_rows.reshape(aux_here, occupied, rows_here).astype(jnp.bfloat16)
    fitted_sum = jnp.einsum(
        "qp,pir->qir",
        fit_matrix,
        lax.all_gather(local_rows, "aux", axis=0, tiled=True),
        preferred_element_type=jnp.float32,
    )
    fitted = fitted_sum.astype(jnp.bfloat16)
    partial_value = lax.dot_general(
        local_rows,
        lax.all_gather(fitted, "atom", axis=2, tiled=True),
        (((0, 1), (0, 1)), ((), ())),
        preferred_element_type=jnp.float32,
    )
    columns_here = basis_total // aux_count
    everywhere = lax.psum(partial_value.astype(jnp.bfloat16), "aux").astype(jnp.float32)
    column_part = lax.dynamic_slice_in_dim(
        everywhere, lax.axis_index("aux") * columns_here, columns_here, 1
    )
    return column_part * (aux_total * occupied) ** (-0.5)


def solution(mesh):
    in_specs = (
        P("atom", "aux", None, None),
        P("atom", None, None),
        P("atom", None),
        P("atom"),
        P("atom"),
        P("atom"),
        P("atom", None),
        P("aux", None),
    )
    out_specs = P("atom", "aux")
    return jax.shard_map(
        per_device, mesh=mesh, in_specs=in_specs, out_specs=out_specs, check_vma=False
    )
```

profile of v0, /device:TPU:1, one launch (start us, length us, event | category | flops | bytes accessed | tf_op | source)
XLA Modules:
  0.0 580.0 jit_solution(9930203619096393487)
XLA Ops:
  6.5 0.0 copy-start
  6.5 0.0 all-gather.4.cloned.1.call-start
  6.5 0.7 all-gather.4.cloned.1.call-update
  7.3 0.7 fusion.25
  8.0 0.8 select_reduce_fusion
  8.9 0.7 add_add_fusion
  9.5 0.8 fusion.21
  10.3 0.7 all_to_all.12
  11.0 8.4 %all-to-all-start.1 = ((bf16[16,1,2]{2,1,0:T(2,128)(2,1)}), bf16[16,1,2]{2,1,0:T(2,128)(2,1)S(1)}, u32[]{:S(2)}, u32[]{:S(2)}) async-start(bf16[16,1,2]{2,1,0:T(2,128)(2,1)} %all_to_all.12), calls=%async_computation.1 | async-start | bytes 16384 | tf_op jit(solution)/shard_map/all_to_all | solution.py:46
  19.4 0.8 convert_element_type.76
  20.2 0.1 copy.17
  20.3 0.2 broadcast_in_dim.30
  20.5 0.2 convert_element_type.77
  20.7 0.1 broadcast_in_dim.31
  20.8 0.3 copy.18
  21.8 0.7 compare_select_fusion
  22.4 34.6 %all-gather.4.cloned.1.call-done = bf16[8192,128]{1,0:T(8,128)(2,1)} async-done(((bf16[512,128]{1,0:T(8,128)(2,1)}), bf16[8192,128]{1,0:T(8,128)(2,1)}) %all-gather.4.cloned.1.call-update) | async-done | bytes 2097168 | tf_op jit(solution)/shard_map/all_gather | solution.py:20
  57.0 2.2 gather_fusion
  59.3 4.0 select_convert_fusion
  63.3 6.1 %fusion.6 = bf16[4,8,1024,128]{3,1,2,0:T(8,128)(2,1)} fusion(bf16[2,8,1024,128]{3,2,1,0:T(8,128)(2,1)S(1)} %bitcast.51, s32[16]{0:T(128)S(1)} %add_add_fusion), kind=kOutput, calls=%fused_computation.8 | convolution fusion | flops 138412544 | bytes 12582976 | tf_op jit(solution)/shard_map/dot_general | solution.py:36
  69.3 8.6 %copy.31 = bf16[4,8,1024,128]{3,2,1,0:T(8,128)(2,1)} copy(bf16[4,8,1024,128]{3,1,2,0:T(8,128)(2,1)} %fusion.6) | data formatting | bytes 16777216
  77.9 0.0 all-to-all-done.1
  77.9 4.8 all-to-all-start
  82.7 0.0 all-gather.6.cloned.1.call-start
  82.8 0.1 reshape.65
  82.9 131.9 %all-to-all-done = bf16[16,2,8,128,128]{4,3,2,1,0:T(8,128)(2,1)} async-done(((bf16[16,2,8,128,128]{4,3,2,1,0:T(8,128)(2,1)}), bf16[16,2,8,128,128]{4,3,2,1,0:T(8,128)(2,1)}, u32[]{:S(2)}, u32[]{:S(2)}) %all-to-all-start) | async-done | bytes 8388640 | tf_op jit(solution)/shard_map/all_to_all | solution.py:45
  214.8 15.7 %copy.20 = bf16[16,2,8,128,128]{4,1,0,3,2:T(2,128)(2,1)S(1)} copy(bf16[16,2,8,128,128]{4,3,2,1,0:T(8,128)(2,1)} %all-to-all-done) | data formatting | bytes 16777216 | tf_op jit(solution)/shard_map/all_to_all | solution.py:45
  230.5 1.3 fusion.17
  231.7 1.2 convert_element_type.89
  232.9 0.0 copy-start.1
  232.9 0.0 all-gather.6.cloned.1.call-update
  233.0 0.2 all-gather.8.cloned.1.call-start
  233.2 57.2 %all-gather.6.cloned.1.call-done = bf16[64,128,512]{2,1,0:T(8,128)(2,1)} async-done(((bf16[8,128,512]{2,1,0:T(8,128)(2,1)}), bf16[64,128,512]{2,1,0:T(8,128)(2,1)}) %all-gather.6.cloned.1.call-update) | async-done | bytes 8388624 | tf_op jit(solution)/shard_map/all_gather | solution.py:62
  290.4 0.0 copy-done
  290.4 8.9 %fusion.18 = bf16[8,128,512]{2,0,1:T(8,128)(2,1)} fusion(bf16[64,128,512]{2,1,0:T(8,128)(2,1)} %all-gather.6.cloned.1.call-done, bf16[8,64]{1,0:T(8,128)(2,1)S(1)} %copy-done), kind=kOutput, calls=%fused_computation.18 | convolution fusion | flops 67633152 | bytes 9438208 | tf_op jit(solution)/shard_map/qp,pir->qir/dot_general | solution.py:59
  299.3 0.0 all-gather.8.cloned.1.call-update
  299.3 0.0 all-reduce.2.cloned.1.call-start
  299.4 120.1 %all-gather.8.cloned.1.call-done = bf16[8,128,8192]{2,0,1:T(8,128)(2,1)} async-done(((bf16[8,128,512]{2,0,1:T(8,128)(2,1)}), bf16[8,128,8192]{2,0,1:T(8,128)(2,1)}) %all-gather.8.cloned.1.call-update) | async-done | bytes 16777232 | tf_op jit(solution)/shard_map/all_gather | solution.py:68
  419.5 0.0 copy-done.1
  419.5 47.3 %bitcast_convert_fusion = bf16[512,8192]{1,0:T(8,128)(2,1)} fusion(bf16[8,128,512]{2,1,0:T(8,128)(2,1)S(1)} %copy-done.1, bf16[8,128,8192]{2,0,1:T(8,128)(2,1)} %all-gather.8.cloned.1.call-done), kind=kOutput, calls=%fused_computation.2 | convolution fusion | flops 8594128896 | bytes 26214400 | tf_op jit(solution)/shard_map/dot_general | solution.py:66
  466.8 0.0 all-reduce.2.cloned.1.call-update
  466.8 103.9 %all-reduce.2.cloned.1.call-done = bf16[512,8192]{1,0:T(8,128)(2,1)} async-done(((bf16[512,8192]{1,0:T(8,128)(2,1)}), bf16[512,8192]{1,0:T(8,128)(2,1)}) %all-reduce.2.cloned.1.call-update) | async-done | bytes 8388624 | tf_op jit(solution)/shard_map/psum | solution.py:73
  570.7 2.8 convert_multiply_fusion
  (5 shorter events, 0.1 us)
Async XLA Ops:
  6.5 283.9 %copy-start = (bf16[8,64]{1,0:T(8,128)(2,1)S(1)}, bf16[8,64]{1,0:T(8,128)(2,1)}, u32[]{:S(2)}) copy-start(bf16[8,64]{1,0:T(8,128)(2,1)} %param.15) | copy-start | bytes 3076
  6.5 50.5 %all-gather.4.cloned.1.call-start = ((), (), s32[]{:S(2)}) async-start(), calls=%async_computation.2 | async-start | bytes 2228224 | tf_op jit(solution)/shard_map/all_gather | solution.py:20
  11.0 66.9 %all-to-all-start.1 = ((bf16[16,1,2]{2,1,0:T(2,128)(2,1)}), bf16[16,1,2]{2,1,0:T(2,128)(2,1)S(1)}, u32[]{:S(2)}, u32[]{:S(2)}) async-start(bf16[16,1,2]{2,1,0:T(2,128)(2,1)} %all_to_all.12), calls=%async_computation.1 | async-start | bytes 16384 | tf_op jit(solution)/shard_map/all_to_all | solution.py:46
  77.9 136.8 %all-to-all-start = ((bf16[16,2,8,128,128]{4,3,2,1,0:T(8,128)(2,1)}), bf16[16,2,8,128,128]{4,3,2,1,0:T(8,128)(2,1)}, u32[]{:S(2)}, u32[]{:S(2)}) async-start(bf16[16,2,8,128,128]{4,3,2,1,0:T(8,128)(2,1)} %bitcast.49), calls=%async_computation | async-start | bytes 16777216 | tf_op jit(solution)/shard_map/all_to_all | solution.py:45
  82.7 207.7 %all-gather.6.cloned.1.call-start = ((), (), s32[]{:S(2)}) async-start(), calls=%async_computation.3 | async-start | bytes 9437184 | tf_op jit(solution)/shard_map/all_gather | solution.py:62
  232.9 186.6 %copy-start.1 = (bf16[8,128,512]{2,1,0:T(8,128)(2,1)S(1)}, bf16[8,128,512]{2,1,0:T(8,128)(2,1)}, u32[]{:S(2)}) copy-start(bf16[8,128,512]{2,1,0:T(8,128)(2,1)} %convert_element_type.89) | copy-start | bytes 3145732
  233.0 186.5 %all-gather.8.cloned.1.call-start = ((), (), s32[]{:S(2)}) async-start(), calls=%async_computation.4 | async-start | bytes 17825792 | tf_op jit(solution)/shard_map/all_gather | solution.py:68
  299.3 271.3 %all-reduce.2.cloned.1.call-start = ((), (), s32[]{:S(2)}) async-start(), calls=%async_computation.5 | async-start | bytes 16777216 | tf_op jit(solution)/shard_map/psum | solution.py:73
Sparse Core Ops, SparseCore 0:
  9.5 47.4 all-gather.3
  233.1 57.2 all-gather.5
  299.5 120.0 all-gather.7
  466.9 103.6 all-reduce.1
where the time goes:
time: 581 us; the launch traced here: 580 us
  waiting for transfers between devices  448 us (77%)
  matrix products  68.3 us (12%)
  local copies, waits for them, and re-layouts  29.4 us (5%)
  between operations  13.9 us (2%)
  starting transfers between devices  13.5 us (2%)
  other arithmetic  6.56 us (1%)
    all_to_all x1, waiting for transfers between devices, per_device(): lax.all_to_all(outgoing, 'atom', split_axis=0, concat_axis=0, tiled=True)  132 us
    all_gather x1, waiting for transfers between devices, per_device(): lax.all_gather(fitted, 'atom', axis=2, tiled=True)  120 us
    psum x1, waiting for transfers between devices, per_device(): lax.psum(partial_value.astype(jnp.bfloat16), 'aux').astype(jnp.float32)  104 us
    all_gather x1, waiting for transfers between devices, per_device(): lax.all_gather(local_rows, 'aux', axis=0, tiled=True)  57.2 us
    dot_general x1, matrix products, per_device(): lax.dot_general(local_rows, lax.all_gather(fitted, 'atom', axis=2, tiled=...  47.3 us
    all_gather x1, waiting for transfers between devices, per_device(): whole_orbitals = lax.all_gather(coefficients, 'atom', axis=0, tiled=True)  34.6 us
    all_to_all x1, local copies, waits for them, and re-layouts, per_device(): lax.all_to_all(outgoing, 'atom', split_axis=0, concat_axis=0, tiled=True)  15.7 us
  transfers between devices with their start and end apart: 6, of which 5 were waited for; matrix products, arithmetic and copies ran while one was open for 5% of the time, Pallas kernels for 0%

commit v1 on v0

v1 whole, which is shorter than its diff:
```python
import functools

import jax
import jax.numpy as jnp
from jax import lax
from jax.experimental import pallas as pl
from jax.experimental.pallas import tpu as pltpu
from jax.sharding import Mesh
from jax.sharding import PartitionSpec as P

CAP = 2
SIDE = 4
BF = jnp.bfloat16
F32 = jnp.float32
VMEM = 48 * 1024 * 1024


def shifted(value, axis, shift):
    return lax.ppermute(value, axis, [(i, (i + shift) % SIDE) for i in range(SIDE)])


def params():
    return pltpu.CompilerParams(vmem_limit_bytes=VMEM)


def cost(flops, bytes_accessed):
    return pl.CostEstimate(flops=flops, bytes_accessed=bytes_accessed, transcendentals=0)


def transform_kernel(src, valid, blk, sel, tile_ref, mask_ref, own_ref, other_ref, out_ref):
    j = pl.program_id(0)
    count = tile_ref.shape[1]

    def fill(orbitals):
        masked = tile_ref[0] * mask_ref[0][None]
        masked = masked.reshape(count * 128, 128)
        product = lax.dot_general(
            orbitals, masked, (((1,), (1,)), ((), ())), preferred_element_type=F32
        ).astype(BF)
        for p in range(count):
            out_ref[0, p] = product[:, p * 128 : (p + 1) * 128]

    @pl.when(jnp.logical_and(valid[j] > 0, sel[j] == 0))
    def _():
        fill(own_ref[blk[j]])

    @pl.when(jnp.logical_and(valid[j] > 0, sel[j] != 0))
    def _():
        fill(other_ref[blk[j]])

    @pl.when(valid[j] == 0)
    def _():
        out_ref[0] = jnp.zeros(out_ref.shape[1:], BF)


def transform(half, order, pair_nu, core, tiles, mask, own, other):
    positions = order.shape[0]
    valid = (order > 0).astype(jnp.int32)
    last = lax.cummax(jnp.where(order > 0, jnp.arange(positions), 0))
    src = jnp.maximum(order[last] - 1, 0)
    block = pair_nu[src]
    sel = jnp.where((block % 4) // 2 == core, 0, 1)
    blk = (block // 4) * 2 + block % 2
    grid_spec = pltpu.PrefetchScalarGridSpec(
        num_scalar_prefetch=4,
        grid=(positions,),
        in_specs=[
            pl.BlockSpec((1, 4, 128, 128), lambda j, src, *_: (src[j], half, 0, 0)),
            pl.BlockSpec((1, 128, 128), lambda j, src, *_: (src[j], 0, 0)),
            pl.BlockSpec((32, 128, 128), lambda j, *_: (0, 0, 0)),
            pl.BlockSpec((32, 128, 128), lambda j, *_: (0, 0, 0)),
        ],
        out_specs=pl.BlockSpec((1, 4, 128, 128), lambda j, *_: (j, 0, 0, 0)),
    )
    return pl.pallas_call(
        transform_kernel,
        grid_spec=grid_spec,
        out_shape=jax.ShapeDtypeStruct((positions, 4, 128, 128), BF),
        compiler_params=params(),
        cost_estimate=cost(2 * 16 * 4 * 128**3, 8 * 2**20),
        name="transform",
    )(src, valid, blk, sel, tiles, mask, own, other)


def collect_kernel(codes, place, a_ref, b_ref, c_ref, d_ref, out_ref, acc):
    j = pl.program_id(0)
    acc[...] = jnp.zeros(acc.shape, F32)
    for k, ref in enumerate((a_ref, b_ref, c_ref, d_ref)):
        for r in range(CAP):
            code = codes[(k * SIDE + j) * CAP + r]

            @pl.when(code > 0)
            def _(ref=ref, r=r, code=code):
                acc[code - 1] += ref[0, r].astype(F32)

    for s in range(4):
        out_ref[0, :, :, s * 128 : (s + 1) * 128] = acc[s].astype(BF)


def collect(codes, place, pieces, offsets):
    block = (1, CAP, 4, 128, 128)
    specs = [
        pl.BlockSpec(block, functools.partial(lambda o, j, *_: (o + j, 0, 0, 0, 0), o))
        for o in offsets
    ]
    grid_spec = pltpu.PrefetchScalarGridSpec(
        num_scalar_prefetch=2,
        grid=(SIDE,),
        in_specs=specs,
        out_specs=pl.BlockSpec((1, 4, 128, 512), lambda j, codes, place: (place[j], 0, 0, 0)),
        scratch_shapes=[pltpu.VMEM((4, 4, 128, 128), F32)],
    )
    return pl.pallas_call(
        collect_kernel,
        grid_spec=grid_spec,
        out_shape=jax.ShapeDtypeStruct((SIDE, 4, 128, 512), BF),
        compiler_params=params(),
        cost_estimate=cost(2**22, 6 * 2**20),
        name="collect",
    )(codes, place, *pieces)


def finish_kernel(*refs):
    out_ref = refs[-1]
    for half in range(2):
        total = refs[4 * half][0].astype(F32)
        for k in range(1, 4):
            total += refs[4 * half + k][0].astype(F32)
        out_ref[0, 4 * half : 4 * half + 4] = total.astype(BF)


def finish(pieces, offsets):
    specs = [
        pl.BlockSpec((1, 4, 16, 512), functools.partial(lambda o, g: (o, 0, g, 0), o))
        for o in offsets
    ]
    return pl.pallas_call(
        finish_kernel,
        grid=(8,),
        in_specs=specs,
        out_specs=pl.BlockSpec((1, 8, 16, 512), lambda g: (g, 0, 0, 0)),
        out_shape=jax.ShapeDtypeStruct((8, 8, 16, 512), BF),
        compiler_params=params(),
        cost_estimate=cost(2**21, 5 * 2**20),
        name="finish",
    )(*pieces)


def product_kernel(has_add, zsel, psel, left_ref, f0, f1, f2, f3, *rest):
    out_ref = rest[-1]
    x2 = pl.program_id(1)
    for s, ref in enumerate((f0, f1, f2, f3)):

        @pl.when(psel[x2] == s)
        def _(ref=ref):
            value = jnp.dot(left_ref[0], ref[...], preferred_element_type=F32)
            if has_add:
                value += rest[0][0, 0].astype(F32)
            out_ref[0, 0] = value.astype(BF)


def product(zsel, psel, left, columns, add=None):
    whole = pl.BlockSpec((1024, 512), lambda l, x2, *_: (0, 0))
    tile = pl.BlockSpec((1, 1, 512, 512), lambda l, x2, *_: (x2, l, 0, 0))
    specs = [pl.BlockSpec((1, 512, 1024), lambda l, x2, zsel, psel: (zsel[l], 0, 0))] + [whole] * 4
    operands = [left, *columns]
    if add is not None:
        specs.append(tile)
        operands.append(add)
    grid_spec = pltpu.PrefetchScalarGridSpec(
        num_scalar_prefetch=2, grid=(2, SIDE), in_specs=specs, out_specs=tile
    )
    return pl.pallas_call(
        functools.partial(product_kernel, add is not None),
        grid_spec=grid_spec,
        out_shape=jax.ShapeDtypeStruct((SIDE, 2, 512, 512), BF),
        compiler_params=params(),
        cost_estimate=cost(8 * 2 * 512 * 512 * 1024, 10 * 2**20),
        name="product",
    )(zsel, psel, *operands)


def per_device(
    three_index, pair_mask, pair_owner, pair_sub, pair_nu, live_count, coefficients, fit_matrix
):
    slots = three_index.shape[0]
    x, z, y, c = (lax.axis_index(name) for name in ("x", "z", "y", "c"))

    blocks = coefficients.reshape(4, 128, 128).transpose(0, 2, 1)
    half_blocks = lax.dynamic_slice_in_dim(blocks, c * 2, 2, 0)
    own = lax.all_to_all(
        jnp.broadcast_to(half_blocks[None], (16, 2, 128, 128)), ("x", "z"), 0, 0, tiled=True
    ).reshape(32, 128, 128)
    other = lax.ppermute(own, "c", [(0, 1), (1, 0)])

    alive = jnp.arange(slots) < live_count[0]
    code = jnp.where(alive, pair_owner[:, 0] * 4 + pair_sub, -1).astype(jnp.int32)
    codes = lax.all_gather(code, ("x", "z"), axis=0, tiled=True).reshape(16, slots)

    def table(code, value):
        owner = jnp.where(code >= 0, code // 4, -1)
        hits = (owner[..., None] == jnp.arange(16)).astype(jnp.int32)
        rank = jnp.sum(
            (owner[..., None, :] == owner[..., :, None])
            & (jnp.arange(slots)[None, :] < jnp.arange(slots)[:, None]),
            -1,
        )
        ranks = (rank[..., None] == jnp.arange(CAP)).astype(jnp.int32)
        return jnp.sum(
            hits[..., :, None] * ranks[..., None, :] * value[..., None, None], -3
        )

    outgoing = table(code, jnp.arange(1, slots + 1, dtype=jnp.int32)).reshape(4, 4, CAP)
    arriving = table(codes, codes % 4 + 1).reshape(4, 4, 4, 4, CAP)
    order_a = outgoing.transpose(1, 0, 2).reshape(-1)
    order_b = outgoing[(x + jnp.arange(4)) % 4].reshape(-1)
    codes_a = arriving[x][:, :, z].reshape(-1)
    codes_b = arriving[:, z, x][(x - jnp.arange(4)) % 4].reshape(-1)

    mask = jnp.repeat(jnp.repeat(pair_mask, 16, 1), 16, 2).astype(BF)

    out_a = transform(0, order_a, pair_nu, c, three_index, mask, own, other)
    got_a = lax.all_to_all(
        out_a.reshape(4, 8, 4, 128, 128), "z", 0, 0, tiled=True
    ).reshape(16, CAP, 4, 128, 128)
    out_b = transform(1, order_b, pair_nu, c, three_index, mask, own, other)
    out_b = out_b.reshape(4, 4, CAP, 4, 128, 128)
    got_b = [out_b[0]] + [shifted(out_b[s], "x", s) for s in (1, 2, 3)]
    sum_a = collect(codes_a, jnp.arange(4, dtype=jnp.int32), [got_a] * 4, (0, 4, 8, 12))
    last_a = lax.all_to_all(sum_a, "x", 0, 0, tiled=True)
    sum_b = collect(codes_b, ((jnp.arange(4) - z) % 4).astype(jnp.int32), got_b, (0,) * 4)
    last_b = [sum_b[:1]] + [shifted(sum_b[s : s + 1], "z", s) for s in (1, 2, 3)]
    cut = finish([last_a] * 4 + last_b, (0, 1, 2, 3, 0, 0, 0, 0))

    rows = lax.all_to_all(cut, ("y", "c"), 0, 0, tiled=True).reshape(1024, 512)

    fit = lax.all_gather(fit_matrix, ("y", "c"), axis=0, tiled=True)
    spread = (jnp.arange(1024)[:, None] // 16 == jnp.arange(64)[None, :]).astype(BF)
    mixing = jnp.dot(jnp.dot(spread, fit, preferred_element_type=F32).astype(BF), spread.T)
    same = jnp.arange(1024)[:, None] % 16 == jnp.arange(1024)[None, :] % 16
    mixing = jnp.where(same, mixing, 0).astype(BF)

    fitted = jnp.dot(mixing, rows, preferred_element_type=F32).astype(BF)
    left = lax.all_to_all(
        jnp.broadcast_to(rows.T[None], (4, 512, 1024)), "z", 0, 0, tiled=True
    )
    columns = [fitted] + [shifted(fitted, "x", s) for s in (1, 2, 3)]

    psel = ((x - jnp.arange(4)) % 4).astype(jnp.int32)
    pair = jnp.arange(2, dtype=jnp.int32)
    theirs = product(2 * (1 - c) + pair, psel, left, columns)
    theirs = lax.ppermute(theirs, "c", [(0, 1), (1, 0)])
    partial = product(2 * c + pair, psel, left, columns, theirs)

    parts = lax.all_to_all(partial, "y", 0, 0, tiled=True)
    got = []
    for t in range(2):
        tile = lax.dynamic_index_in_dim(parts, (z + t) % 2, 1, keepdims=False)
        tile = jnp.sum(tile.astype(F32), 0).astype(BF)
        pairs = [
            (zz * 2 + k, (2 * k + (zz + t) % 2) * 2 + zz // 2) for zz in range(4) for k in range(2)
        ]
        got.append(lax.ppermute(tile, ("z", "c"), pairs).astype(F32))
    scale = 8192 ** (-0.5)
    even = z % 2 == 0
    first = jnp.where(even, got[0], got[1]) * scale
    second = jnp.where(even, got[1], got[0]) * scale
    return jnp.concatenate([first, second], 1)


def solution(mesh):
    grid = Mesh(mesh.devices.reshape(4, 4, 4, 2), ("x", "z", "y", "c"))
    atom, aux = ("x", "z"), ("y", "c")
    in_specs = (
        P(atom, aux, None, None),
        P(atom, None, None),
        P(atom, None),
        P(atom),
        P(atom),
        P(atom),
        P(atom, None),
        P(aux, None),
    )
    return jax.shard_map(
        per_device, mesh=grid, in_specs=in_specs, out_specs=P(atom, aux), check_vma=False
    )
```

time: 581 us -> 425 us (0.73)
  waiting for transfers between devices: 448 us -> 178 us
  blocking collectives: 0 us -> 90.1 us
  matrix products: 68.3 us -> 2.34 us
  Pallas kernels: 0 us -> 64 us
  starting transfers between devices: 13.5 us -> 53.4 us
  between operations: 13.9 us -> 1.8 us
    all_gather x3 -> x0, waiting for transfers between devices: 212 us -> none  [the longest x1 120 us: per_device(): lax.all_gather(fitted, 'atom', axis=2, tiled=True)]
    ppermute x0 -> x13, waiting for transfers between devices: none -> 117 us  [the longest x9 96.4 us: shifted(): lax.ppermute(value, axis, [(i, (i + shift) % SIDE) for i in range(SIDE)])]
    psum x1 -> x0, waiting for transfers between devices: 104 us -> none  [per_device(): lax.psum(partial_value.astype(jnp.bfloat16), 'aux').astype(jnp.float32)]
    all_to_all x2 -> x5, waiting for transfers between devices: 132 us -> 60.7 us  [the longest x1 48.6 us: per_device(): parts = lax.all_to_all(partial, 'y', 0, 0, tiled=True)]
    dot_general x6 -> x2, matrix products: 68.3 us -> 2.34 us  [the longest x1 1.96 us: per_device(): fitted = jnp.dot(mixing, rows, preferred_element_type=F32).astype(BF)]
    pallas_call x0 -> x7, Pallas kernels: none -> 64 us  [the longest x2 33.4 us: transform(): pl.pallas_call(transform_kernel, grid_spec=grid_spec, out_shape=jax.Shape...]
    unnamed x0 -> x1, blocking collectives: none -> 53.7 us
    ppermute x0 -> x13, starting transfers between devices: none -> 26.5 us  [the longest x9 16 us: shifted(): lax.ppermute(value, axis, [(i, (i + shift) % SIDE) for i in range(SIDE)])]
  transfers between devices with their start and end apart: 6 -> 18, of which waited for: 5 -> 13; matrix products, arithmetic and copies ran while one was open for 5% -> 4% of each run, Pallas kernels for 0% -> 6%
where the time goes in v1:
time: 425 us; the launch traced here: 422 us
  waiting for transfers between devices  178 us (42%)
  blocking collectives  90.1 us (21%)
  Pallas kernels  64 us (15%)
  starting transfers between devices  53.4 us (13%)
  local copies, waits for them, and re-layouts  25.3 us (6%)
  other arithmetic  6.94 us (2%)
    ppermute x9, waiting for transfers between devices, shifted(): lax.ppermute(value, axis, [(i, (i + shift) % SIDE) for i in range(SIDE)])  96.4 us
    unnamed x1, blocking collectives  53.7 us
    all_to_all x1, waiting for transfers between devices, per_device(): parts = lax.all_to_all(partial, 'y', 0, 0, tiled=True)  48.6 us
    pallas_call x2, Pallas kernels, transform(): pl.pallas_call(transform_kernel, grid_spec=grid_spec, out_shape=jax.Shape...  33.4 us
    all_to_all x1, blocking collectives, per_device(): rows = lax.all_to_all(cut, ('y', 'c'), 0, 0, tiled=True).reshape(1024, 512)  24.3 us
    pallas_call x2, Pallas kernels, product(): pl.pallas_call(functools.partial(product_kernel, add is not None), grid_s...  20.7 us
    ppermute x9, starting transfers between devices, shifted(): lax.ppermute(value, axis, [(i, (i + shift) % SIDE) for i in range(SIDE)])  16 us
    ppermute x2, waiting for transfers between devices, per_device(): got.append(lax.ppermute(tile, ('z', 'c'), pairs).astype(F32))  13.9 us
  transfers between devices with their start and end apart: 18, of which 13 were waited for; matrix products, arithmetic and copies ran while one was open for 4% of the time, Pallas kernels for 6%

profile of v1, /device:TPU:1, one launch (start us, length us, event | category | flops | bytes accessed | tf_op | source)
XLA Modules:
  0.0 421.9 jit_solution(15350476430273751774)
XLA Ops:
  0.0 0.9 copy-done
  1.0 1.2 broadcast_in_dim.27
  2.3 8.6 %all-to-all-start = ((bf16[16,2,128,128]{3,2,1,0:T(8,128)(2,1)}), bf16[16,2,128,128]{3,2,1,0:T(8,128)(2,1)S(1)}, u32[]{:S(2)}, u32[]{:S(2)}) async-start(bf16[16,2,128,128]{3,2,1,0:T(8,128)(2,1)} %broadcast_in_dim.27), calls=%async_computation | async-start | bytes 2097152 | tf_op jit(solution)/shard_map/all_to_all | solution.py:191
  12.1 0.6 gather_fusion.3
  13.5 0.7 gather_fusion.4
  14.2 12.1 %all-to-all-done = bf16[16,2,128,128]{3,2,1,0:T(8,128)(2,1)S(1)} async-done(((bf16[16,2,128,128]{3,2,1,0:T(8,128)(2,1)}), bf16[16,2,128,128]{3,2,1,0:T(8,128)(2,1)S(1)}, u32[]{:S(2)}, u32[]{:S(2)}) %all-to-all-start) | async-done | bytes 1048608 | tf_op jit(solution)/shard_map/all_to_all | solution.py:191
  26.3 3.1 collective-permute-start
  29.7 0.7 gather_fusion.5
  30.6 0.7 gather_fusion
  31.3 0.7 gather_fusion.1
  32.9 16.6 %transform.3 = bf16[32,4,128,128]{3,2,1,0:T(8,128)(2,1)} custom-call(s32[32]{0:T(128)S(1)} %add_maximum_fusion.1.src, s32[32]{0:T(128)S(1)} %get-tuple-element.28.valid, s32[32]{0:T(128)S(1)} %get-tuple-element.25.blk, s32[32]{0:T(128)S(1)} %get-tuple-element.26.sel, bf16[16,8,128,128]{3,2,1,0:T(8,128)(2,1)} %tile_ref.3, ...), custom_call_target="tpu_custom_call" | custom-call | flops 268435456 | bytes 8388608 | tf_op jit(solution)/shard_map/transform/pallas_call | solution.py:75
  49.6 5.0 %all-to-all-start.1 = ((bf16[4,8,4,128,128]{4,3,2,1,0:T(8,128)(2,1)}), bf16[4,8,4,128,128]{4,3,2,1,0:T(8,128)(2,1)}, u32[]{:S(2)}, u32[]{:S(2)}) async-start(bf16[4,8,4,128,128]{4,3,2,1,0:T(8,128)(2,1)} %bitcast.47), calls=%async_computation.1 | async-start | bytes 8388608 | tf_op jit(solution)/shard_map/all_to_all | solution.py:223
  54.6 0.6 dynamic-slice.6
  56.0 53.7 %all-reduce = s32[256]{0:T(256)S(1)} all-reduce(s32[256]{0:T(256)S(1)} %dynamic-update-slice), channel_id=1, replica_groups=mesh['x'=4,'z'=4,'y'=4,'c'=2] {'x','z'}, use_global_device_ids=true, to_apply=%add | all-reduce | flops 256 | bytes 2048
  109.9 0.4 convert_reduce_fusion
  110.4 16.8 %transform.6 = bf16[32,4,128,128]{3,2,1,0:T(8,128)(2,1)} custom-call(s32[32]{0:T(128)S(1)} %add_maximum_fusion.src, s32[32]{0:T(128)S(1)} %get-tuple-element.27.valid, s32[32]{0:T(128)S(1)} %get-tuple-element.22.blk, s32[32]{0:T(128)S(1)} %get-tuple-element.21.sel, bf16[16,8,128,128]{3,2,1,0:T(8,128)(2,1)} %tile_ref.3, ...), custom_call_target="tpu_custom_call" | custom-call | flops 268435456 | bytes 8388608 | tf_op jit(solution)/shard_map/transform/pallas_call | solution.py:75
  127.2 4.0 fusion.34
  131.2 1.8 collective-permute-start.1
  133.0 0.4 collective-permute-start.2
  133.4 2.1 collective-permute-start.3
  136.2 4.0 collect.2
  140.2 1.3 copy-done.2
  141.5 3.6 all-to-all-start.2
  145.2 0.6 gather_fusion.2
  146.0 8.7 %collective-permute-done.1.b_ref = bf16[4,2,4,128,128]{4,3,2,1,0:T(8,128)(2,1)} collective-permute-done((bf16[4,2,4,128,128]{4,3,2,1,0:T(8,128)(2,1)}, bf16[4,2,4,128,128]{4,3,2,1,0:T(8,128)(2,1)}, u32[]{:S(2)}, u32[]{:S(2)}) %collective-permute-start.1) | collective-permute-done | bytes 1048608 | tf_op jit(solution)/shard_map/ppermute | solution.py:19
  154.7 21.4 %collective-permute-done.2.c_ref = bf16[4,2,4,128,128]{4,3,2,1,0:T(8,128)(2,1)} collective-permute-done((bf16[4,2,4,128,128]{4,3,2,1,0:T(8,128)(2,1)}, bf16[4,2,4,128,128]{4,3,2,1,0:T(8,128)(2,1)}, u32[]{:S(2)}, u32[]{:S(2)}) %collective-permute-start.2) | collective-permute-done | bytes 1048608 | tf_op jit(solution)/shard_map/ppermute | solution.py:19
  176.1 3.7 collective-permute-done.3.d_ref
  179.8 4.9 %collect.3 = bf16[4,4,128,512]{3,2,1,0:T(8,128)(2,1)} custom-call(s32[32]{0:T(128)S(1)} %reshape.485.codes, s32[4]{0:T(128)S(1)} %and_select_fusion.5.place, bf16[4,2,4,128,128]{4,3,2,1,0:T(8,128)(2,1)S(1)} %bitcast.46, bf16[4,2,4,128,128]{4,3,2,1,0:T(8,128)(2,1)} %collective-permute-done.1.b_ref, bf16[4,2,4,128,128]{4,3,2,1,0:T(8,128)(2,1)} %collective-permute-done.2.c_ref, ...), custom_call_target="tpu_custom_call" | custom-call | flops 4194304 | bytes 6291456 | tf_op jit(solution)/shard_map/collect/pallas_call | solution.py:113
  184.8 1.7 fusion.35
  186.4 3.1 collective-permute-start.4
  189.5 2.0 collective-permute-start.5
  191.5 2.0 collective-permute-start.6
  193.4 3.0 collective-permute-done.4.refs_5_
  196.4 12.2 %collective-permute-done.5.refs_6_ = bf16[1,4,128,512]{3,2,1,0:T(8,128)(2,1)S(1)} collective-permute-done((bf16[1,4,128,512]{3,2,1,0:T(8,128)(2,1)S(1)}, bf16[1,4,128,512]{3,2,1,0:T(8,128)(2,1)S(1)}, u32[]{:S(2)}, u32[]{:S(2)}) %collective-permute-start.5) | collective-permute-done | bytes 524320 | tf_op jit(solution)/shard_map/ppermute | solution.py:19
  208.7 0.8 copy-done.3
  209.5 1.8 collective-permute-done.6.refs_7_
  211.3 0.8 copy-done.5
  212.1 1.0 copy-done.4
  213.1 1.0 copy-done.6
  214.2 1.1 finish.1
  215.2 24.3 %all_to_all.30 = bf16[8,8,16,512]{3,2,1,0:T(8,128)(2,1)S(1)} all-to-all(bf16[8,8,16,512]{3,2,1,0:T(8,128)(2,1)S(1)} %finish.1), channel_id=1, replica_groups=mesh['x'=4,'z'=4,'y'=4,'c'=2] {'y','c'}, dimensions={0} | all-to-all | bytes 2097152 | tf_op jit(solution)/shard_map/all_to_all | solution.py:235
  239.6 0.5 copy.70
  240.1 2.5 broadcast_in_dim.28
  242.6 5.0 %all-to-all-start.4 = ((bf16[4,512,1024]{2,1,0:T(8,128)(2,1)}), bf16[4,512,1024]{2,1,0:T(8,128)(2,1)}, u32[]{:S(2)}, u32[]{:S(2)}) async-start(bf16[4,512,1024]{2,1,0:T(8,128)(2,1)} %broadcast_in_dim.28), calls=%async_computation.4 | async-start | bytes 8388608 | tf_op jit(solution)/shard_map/all_to_all | solution.py:244
  247.6 12.1 %all_gather.7 = bf16[64,64]{1,0:T(8,128)(2,1)S(1)} all-gather(bf16[8,64]{1,0:T(8,128)(2,1)S(1)} %copy-done.10), channel_id=1, replica_groups=mesh['x'=4,'z'=4,'y'=4,'c'=2] {'y','c'}, dimensions={0}, use_global_device_ids=true | all-gather | bytes 9216 | tf_op jit(solution)/shard_map/all_gather | solution.py:237
  259.7 0.4 convolution_convert_fusion
  260.0 2.0 fusion.5.f0
  262.0 1.4 collective-permute-start.7
  263.4 3.3 collective-permute-start.8
  266.7 22.3 %collective-permute-done.7.f1 = bf16[1024,512]{1,0:T(8,128)(2,1)S(1)} collective-permute-done((bf16[1024,512]{1,0:T(8,128)(2,1)S(1)}, bf16[1024,512]{1,0:T(8,128)(2,1)S(1)}, u32[]{:S(2)}, u32[]{:S(2)}) %collective-permute-start.7) | collective-permute-done | bytes 1048608 | tf_op jit(solution)/shard_map/ppermute | solution.py:19
  289.0 23.2 %collective-permute-done.8.f2 = bf16[1024,512]{1,0:T(8,128)(2,1)S(1)} collective-permute-done((bf16[1024,512]{1,0:T(8,128)(2,1)S(1)}, bf16[1024,512]{1,0:T(8,128)(2,1)S(1)}, u32[]{:S(2)}, u32[]{:S(2)}) %collective-permute-start.8) | collective-permute-done | bytes 1048608 | tf_op jit(solution)/shard_map/ppermute | solution.py:19
  312.3 9.7 %product.2 = bf16[4,2,512,512]{3,2,1,0:T(8,128)(2,1)} custom-call(s32[2]{0:T(128)S(1)} %iota_add_fusion.zsel, s32[4]{0:T(128)S(1)} %and_select_fusion.12.psel, bf16[4,512,1024]{2,1,0:T(8,128)(2,1)} %all-to-all-done.4.left_ref, bf16[1024,512]{1,0:T(8,128)(2,1)S(1)} %fusion.5.f0, bf16[1024,512]{1,0:T(8,128)(2,1)S(1)} %collective-permute-done.7.f1, ...), custom_call_target="tpu_custom_call" | custom-call | flops 4294967296 | bytes 10485760 | tf_op jit(solution)/shard_map/product/pallas_call | solution.py:173
  322.0 1.0 collective-permute-start.10
  323.0 7.0 %collective-permute-done.10.rest_0_ = bf16[4,2,512,512]{3,2,1,0:T(8,128)(2,1)S(1)} collective-permute-done((bf16[4,2,512,512]{3,2,1,0:T(8,128)(2,1)}, bf16[4,2,512,512]{3,2,1,0:T(8,128)(2,1)S(1)}, u32[]{:S(2)}, u32[]{:S(2)}) %collective-permute-start.10) | collective-permute-done | bytes 4194336 | tf_op jit(solution)/shard_map/ppermute | solution.py:252
  330.0 2.0 copy-done.8
  331.9 11.0 %product.3 = bf16[4,2,512,512]{3,2,1,0:T(8,128)(2,1)} custom-call(s32[2]{0:T(128)S(1)} %iota_add_fusion.2.zsel, s32[4]{0:T(128)S(1)} %and_select_fusion.12.psel, bf16[4,512,1024]{2,1,0:T(8,128)(2,1)} %all-to-all-done.4.left_ref, bf16[1024,512]{1,0:T(8,128)(2,1)S(1)} %fusion.5.f0, bf16[1024,512]{1,0:T(8,128)(2,1)S(1)} %collective-permute-done.7.f1, ...), custom_call_target="tpu_custom_call" | custom-call | flops 4294967296 | bytes 10485760 | tf_op jit(solution)/shard_map/product/pallas_call | solution.py:173
  342.9 4.8 %all-to-all-start.5 = ((bf16[4,2,512,512]{3,2,1,0:T(8,128)(2,1)}), bf16[4,2,512,512]{3,2,1,0:T(8,128)(2,1)}, u32[]{:S(2)}, u32[]{:S(2)}) async-start(bf16[4,2,512,512]{3,2,1,0:T(8,128)(2,1)} %product.3), calls=%async_computation.5 | async-start | bytes 8388608 | tf_op jit(solution)/shard_map/all_to_all | solution.py:255
  347.8 48.6 %all-to-all-done.5 = bf16[4,2,512,512]{3,2,1,0:T(8,128)(2,1)} async-done(((bf16[4,2,512,512]{3,2,1,0:T(8,128)(2,1)}), bf16[4,2,512,512]{3,2,1,0:T(8,128)(2,1)}, u32[]{:S(2)}, u32[]{:S(2)}) %all-to-all-start.5) | async-done | bytes 4194336 | tf_op jit(solution)/shard_map/all_to_all | solution.py:255
  396.4 3.5 dynamic-slice_reduce_fusion
  399.9 6.2 %collective-permute-start.11 = (bf16[512,512]{1,0:T(8,128)(2,1)S(1)}, bf16[512,512]{1,0:T(8,128)(2,1)S(1)}, u32[]{:S(2)}, u32[]{:S(2)}) collective-permute-start(bf16[512,512]{1,0:T(8,128)(2,1)S(1)} %get-tuple-element.6), channel_id=1, source_target_pairs={{0,0},{1,16},{8,8},{9,24},{16,1},{17,17},{24,9},{25,25},{2,2},{3,1... | collective-permute-start | bytes 1572872 | tf_op jit(solution)/shard_map/ppermute | solution.py:263
  406.3 10.8 %collective-permute-done.11 = bf16[512,512]{1,0:T(8,128)(2,1)S(1)} collective-permute-done((bf16[512,512]{1,0:T(8,128)(2,1)S(1)}, bf16[512,512]{1,0:T(8,128)(2,1)S(1)}, u32[]{:S(2)}, u32[]{:S(2)}) %collective-permute-start.11) | collective-permute-done | bytes 524320 | tf_op jit(solution)/shard_map/ppermute | solution.py:263
  417.1 3.1 collective-permute-done.12
  420.1 0.3 fusion.6
  420.5 1.5 pad_maximum_fusion
  (97 shorter events, 4.4 us)
Async XLA Ops:
  0.0 0.9 copy-start
  0.0 11.5 %copy-start.12 = (s32[16,1]{0,1:T(1,128)S(1)}, s32[16,1]{0,1:T(1,128)}, u32[]{:S(2)}) copy-start(s32[16,1]{0,1:T(1,128)} %param.10) | copy-start | bytes 196
  0.0 11.5 %copy-start.11 = (s32[16]{0:T(128)S(1)}, s32[16]{0:T(128)}, u32[]{:S(2)}) copy-start(s32[16]{0:T(128)} %param.11) | copy-start | bytes 196
  0.9 28.8 %copy-start.7 = (s32[16]{0:T(128)S(1)}, s32[16]{0:T(128)}, u32[]{:S(2)}) copy-start(s32[16]{0:T(128)} %param.12) | copy-start | bytes 196
  2.3 29.7 %copy-start.9 = (s32[16,8,8]{0,2,1:T(8,128)S(1)}, s32[16,8,8]{0,2,1:T(8,128)}, u32[]{:S(2)}) copy-start(s32[16,8,8]{0,2,1:T(8,128)} %param.9) | copy-start | bytes 12292
  2.3 24.1 %all-to-all-start = ((bf16[16,2,128,128]{3,2,1,0:T(8,128)(2,1)}), bf16[16,2,128,128]{3,2,1,0:T(8,128)(2,1)S(1)}, u32[]{:S(2)}, u32[]{:S(2)}) async-start(bf16[16,2,128,128]{3,2,1,0:T(8,128)(2,1)} %broadcast_in_dim.27), calls=%async_computation | async-start | bytes 2097152 | tf_op jit(solution)/shard_map/all_to_all | solution.py:191
  26.3 6.6 %collective-permute-start = (bf16[32,128,128]{2,1,0:T(8,128)(2,1)S(1)}, bf16[32,128,128]{2,1,0:T(8,128)(2,1)S(1)}, u32[]{:S(2)}, u32[]{:S(2)}) collective-permute-start(bf16[32,128,128]{2,1,0:T(8,128)(2,1)S(1)} %bitcast.43), channel_id=1, source_target_pairs={{0,1},{1,0},{2,3},{3,2},{4,5},{5,4},{6,7},{7,6},{8,9},{9,8},{10,11... | collective-permute-start | bytes 3145736 | tf_op jit(solution)/shard_map/ppermute | solution.py:194
  49.6 5.0 %copy-start.13 = (u32[128]{0:T(128)S(1)}, u32[128]{0:T(128)}, u32[]{:S(2)}) copy-start(u32[128]{0:T(128)} %constant.243) | copy-start | bytes 1540
  49.6 86.7 %all-to-all-start.1 = ((bf16[4,8,4,128,128]{4,3,2,1,0:T(8,128)(2,1)}), bf16[4,8,4,128,128]{4,3,2,1,0:T(8,128)(2,1)}, u32[]{:S(2)}, u32[]{:S(2)}) async-start(bf16[4,8,4,128,128]{4,3,2,1,0:T(8,128)(2,1)} %bitcast.47), calls=%async_computation.1 | async-start | bytes 8388608 | tf_op jit(solution)/shard_map/all_to_all | solution.py:223
  131.2 23.5 %collective-permute-start.1 = (bf16[4,2,4,128,128]{4,3,2,1,0:T(8,128)(2,1)}, bf16[4,2,4,128,128]{4,3,2,1,0:T(8,128)(2,1)}, u32[]{:S(2)}, u32[]{:S(2)}) collective-permute-start(bf16[4,2,4,128,128]{4,3,2,1,0:T(8,128)(2,1)} %bitcast.15), channel_id=1, source_target_pairs={{0,32},{32,64},{64,96},{96,0},{1,33},{33,65},{65,97},{97,1},{2,34}... | collective-permute-start | bytes 3145736 | tf_op jit(solution)/shard_map/ppermute | solution.py:19
  133.0 43.1 %collective-permute-start.2 = (bf16[4,2,4,128,128]{4,3,2,1,0:T(8,128)(2,1)}, bf16[4,2,4,128,128]{4,3,2,1,0:T(8,128)(2,1)}, u32[]{:S(2)}, u32[]{:S(2)}) collective-permute-start(bf16[4,2,4,128,128]{4,3,2,1,0:T(8,128)(2,1)} %bitcast.16), channel_id=1, source_target_pairs={{0,64},{32,96},{64,0},{96,32},{1,65},{33,97},{65,1},{97,33},{2,66}... | collective-permute-start | bytes 3145736 | tf_op jit(solution)/shard_map/ppermute | solution.py:19
  133.4 46.4 %collective-permute-start.3 = (bf16[4,2,4,128,128]{4,3,2,1,0:T(8,128)(2,1)}, bf16[4,2,4,128,128]{4,3,2,1,0:T(8,128)(2,1)}, u32[]{:S(2)}, u32[]{:S(2)}) collective-permute-start(bf16[4,2,4,128,128]{4,3,2,1,0:T(8,128)(2,1)} %bitcast.17), channel_id=1, source_target_pairs={{0,96},{32,0},{64,32},{96,64},{1,97},{33,1},{65,33},{97,65},{2,98}... | collective-permute-start | bytes 3145736 | tf_op jit(solution)/shard_map/ppermute | solution.py:19
  140.2 1.3 copy-start.2
  141.5 70.6 %all-to-all-start.2 = ((bf16[4,4,128,512]{3,2,1,0:T(8,128)(2,1)}), bf16[4,4,128,512]{3,2,1,0:T(8,128)(2,1)S(1)}, u32[]{:S(2)}, u32[]{:S(2)}) async-start(bf16[4,4,128,512]{3,2,1,0:T(8,128)(2,1)} %copy-done.2), calls=%async_computation.2 | async-start | bytes 4194304 | tf_op jit(solution)/shard_map/all_to_all | solution.py:230
  186.4 10.0 %collective-permute-start.4 = (bf16[1,4,128,512]{3,2,1,0:T(8,128)(2,1)S(1)}, bf16[1,4,128,512]{3,2,1,0:T(8,128)(2,1)S(1)}, u32[]{:S(2)}, u32[]{:S(2)}) collective-permute-start(bf16[1,4,128,512]{3,2,1,0:T(8,128)(2,1)S(1)} %get-tuple-element.15), channel_id=1, source_target_pairs={{0,8},{8,16},{16,24},{24,0},{1,9},{9,17},{17,25},{25,1},{2,10},{10... | collective-permute-start | bytes 1572872 | tf_op jit(solution)/shard_map/ppermute | solution.py:19
  189.5 19.2 %collective-permute-start.5 = (bf16[1,4,128,512]{3,2,1,0:T(8,128)(2,1)S(1)}, bf16[1,4,128,512]{3,2,1,0:T(8,128)(2,1)S(1)}, u32[]{:S(2)}, u32[]{:S(2)}) collective-permute-start(bf16[1,4,128,512]{3,2,1,0:T(8,128)(2,1)S(1)} %get-tuple-element.14), channel_id=1, source_target_pairs={{0,16},{8,24},{16,0},{24,8},{1,17},{9,25},{17,1},{25,9},{2,18},{10... | collective-permute-start | bytes 1572872 | tf_op jit(solution)/shard_map/ppermute | solution.py:19
  191.5 19.8 %collective-permute-start.6 = (bf16[1,4,128,512]{3,2,1,0:T(8,128)(2,1)S(1)}, bf16[1,4,128,512]{3,2,1,0:T(8,128)(2,1)S(1)}, u32[]{:S(2)}, u32[]{:S(2)}) collective-permute-start(bf16[1,4,128,512]{3,2,1,0:T(8,128)(2,1)S(1)} %get-tuple-element.13), channel_id=1, source_target_pairs={{0,24},{8,0},{16,8},{24,16},{1,25},{9,1},{17,9},{25,17},{2,26},{10... | collective-permute-start | bytes 1572872 | tf_op jit(solution)/shard_map/ppermute | solution.py:19
  208.7 0.8 copy-start.3
  211.3 0.8 copy-start.5
  212.1 1.0 copy-start.4
  213.1 1.0 copy-start.6
  242.6 5.0 %copy-start.10 = (bf16[8,64]{1,0:T(8,128)(2,1)S(1)}, bf16[8,64]{1,0:T(8,128)(2,1)}, u32[]{:S(2)}) copy-start(bf16[8,64]{1,0:T(8,128)(2,1)} %param.15) | copy-start | bytes 3076
  242.6 69.7 %all-to-all-start.4 = ((bf16[4,512,1024]{2,1,0:T(8,128)(2,1)}), bf16[4,512,1024]{2,1,0:T(8,128)(2,1)}, u32[]{:S(2)}, u32[]{:S(2)}) async-start(bf16[4,512,1024]{2,1,0:T(8,128)(2,1)} %broadcast_in_dim.28), calls=%async_computation.4 | async-start | bytes 8388608 | tf_op jit(solution)/shard_map/all_to_all | solution.py:244
  262.0 27.0 %collective-permute-start.7 = (bf16[1024,512]{1,0:T(8,128)(2,1)S(1)}, bf16[1024,512]{1,0:T(8,128)(2,1)S(1)}, u32[]{:S(2)}, u32[]{:S(2)}) collective-permute-start(bf16[1024,512]{1,0:T(8,128)(2,1)S(1)} %fusion.5.f0), channel_id=1, source_target_pairs={{0,32},{32,64},{64,96},{96,0},{1,33},{33,65},{65,97},{97,1},{2,34}... | collective-permute-start | bytes 3145736 | tf_op jit(solution)/shard_map/ppermute | solution.py:19
  263.4 48.8 %collective-permute-start.8 = (bf16[1024,512]{1,0:T(8,128)(2,1)S(1)}, bf16[1024,512]{1,0:T(8,128)(2,1)S(1)}, u32[]{:S(2)}, u32[]{:S(2)}) collective-permute-start(bf16[1024,512]{1,0:T(8,128)(2,1)S(1)} %fusion.5.f0), channel_id=1, source_target_pairs={{0,64},{32,96},{64,0},{96,32},{1,65},{33,97},{65,1},{97,33},{2,66}... | collective-permute-start | bytes 3145736 | tf_op jit(solution)/shard_map/ppermute | solution.py:19
  266.7 45.6 %collective-permute-start.9 = (bf16[1024,512]{1,0:T(8,128)(2,1)S(1)}, bf16[1024,512]{1,0:T(8,128)(2,1)}, u32[]{:S(2)}, u32[]{:S(2)}) collective-permute-start(bf16[1024,512]{1,0:T(8,128)(2,1)S(1)} %fusion.5.f0), channel_id=1, source_target_pairs={{0,96},{32,0},{64,32},{96,64},{1,97},{33,1},{65,33},{97,65},{2,98}... | collective-permute-start | bytes 3145736 | tf_op jit(solution)/shard_map/ppermute | solution.py:19
  322.0 8.0 %collective-permute-start.10 = (bf16[4,2,512,512]{3,2,1,0:T(8,128)(2,1)}, bf16[4,2,512,512]{3,2,1,0:T(8,128)(2,1)S(1)}, u32[]{:S(2)}, u32[]{:S(2)}) collective-permute-start(bf16[4,2,512,512]{3,2,1,0:T(8,128)(2,1)} %product.2), channel_id=1, source_target_pairs={{0,1},{1,0},{2,3},{3,2},{4,5},{5,4},{6,7},{7,6},{8,9},{9,8},{10,11... | collective-permute-start | bytes 12582920 | tf_op jit(solution)/shard_map/ppermute | solution.py:252
  330.0 2.0 copy-start.8
  342.9 53.5 %all-to-all-start.5 = ((bf16[4,2,512,512]{3,2,1,0:T(8,128)(2,1)}), bf16[4,2,512,512]{3,2,1,0:T(8,128)(2,1)}, u32[]{:S(2)}, u32[]{:S(2)}) async-start(bf16[4,2,512,512]{3,2,1,0:T(8,128)(2,1)} %product.3), calls=%async_computation.5 | async-start | bytes 8388608 | tf_op jit(solution)/shard_map/all_to_all | solution.py:255
  399.9 17.1 %collective-permute-start.11 = (bf16[512,512]{1,0:T(8,128)(2,1)S(1)}, bf16[512,512]{1,0:T(8,128)(2,1)S(1)}, u32[]{:S(2)}, u32[]{:S(2)}) collective-permute-start(bf16[512,512]{1,0:T(8,128)(2,1)S(1)} %get-tuple-element.6), channel_id=1, source_target_pairs={{0,0},{1,16},{8,8},{9,24},{16,1},{17,17},{24,9},{25,25},{2,2},{3,1... | collective-permute-start | bytes 1572872 | tf_op jit(solution)/shard_map/ppermute | solution.py:263
  406.1 14.0 %collective-permute-start.12 = (bf16[512,512]{1,0:T(8,128)(2,1)S(1)}, bf16[512,512]{1,0:T(8,128)(2,1)S(1)}, u32[]{:S(2)}, u32[]{:S(2)}) collective-permute-start(bf16[512,512]{1,0:T(8,128)(2,1)S(1)} %get-tuple-element.5), channel_id=1, source_target_pairs={{0,8},{1,24},{8,0},{9,16},{16,9},{17,25},{24,1},{25,17},{2,10},{3,... | collective-permute-start | bytes 1572872 | tf_op jit(solution)/shard_map/ppermute | solution.py:263
  420.4 1.5 copy-start.1

commit v2 on v1

v2 whole, which is shorter than its diff:
```python
import functools

import jax
import jax.numpy as jnp
from jax import lax
from jax.experimental import pallas as pl
from jax.experimental.pallas import tpu as pltpu
from jax.sharding import Mesh
from jax.sharding import PartitionSpec as P

CAP = 2
SIDE = 4
BF = jnp.bfloat16
F32 = jnp.float32
VMEM = 48 * 1024 * 1024


def shifted(value, axis, shift):
    return lax.ppermute(value, axis, [(i, (i + shift) % SIDE) for i in range(SIDE)])


def params():
    return pltpu.CompilerParams(vmem_limit_bytes=VMEM)


def cost(flops, bytes_accessed):
    return pl.CostEstimate(flops=flops, bytes_accessed=bytes_accessed, transcendentals=0)


def plan_kernel(where, owner, nu, out, count):
    x, z, c = where[0], where[1], where[2]
    for o in range(16):
        count[o] = 0
    for j in range(16):
        target = owner[j, 0]
        rank = jnp.minimum(count[target], CAP - 1)
        count[target] = rank + 1
        to_x, to_z = target // 4, target % 4
        out[0, j] = to_z * 8 + to_x * 2 + rank
        out[1, j] = to_z * 2 + rank
        out[2, j] = (to_x - x + 4) % 4
        out[6, j] = nu[j] // 4
        out[7, j] = (nu[j] % 2) * 128
        out[8, j] = jnp.where((nu[j] % 4) // 2 == c, 0, 1)


def plan(where, owner, nu):
    smem = pl.BlockSpec(memory_space=pltpu.SMEM)
    return pl.pallas_call(
        plan_kernel,
        in_specs=[smem] * 3,
        out_specs=smem,
        out_shape=jax.ShapeDtypeStruct((9, 16), jnp.int32),
        scratch_shapes=[pltpu.SMEM((16,), jnp.int32)],
        name="plan",
    )(where, owner, nu)


def transform_kernel(
    meta, live, tile_hbm, mask_ref, own_hbm, other_hbm, a_hbm, b0_hbm, b1_hbm, b2_hbm, b3_hbm,
    tile, orb, result, tile_sem, orb_sem, a_sem, b_sem,
):
    def tile_copy(j):
        return pltpu.make_async_copy(tile_hbm.at[j], tile.at[j], tile_sem.at[j])

    def orb_copy(j, source):
        rows = pl.ds(pl.multiple_of(meta[7, j], 128), 128)
        return pltpu.make_async_copy(source.at[meta[6, j], rows], orb.at[j], orb_sem.at[j])

    def a_copy(j):
        return pltpu.make_async_copy(
            result.at[j, pl.ds(0, 4)], a_hbm.at[meta[0, j]], a_sem.at[j]
        )

    def b_copy(j, target):
        return pltpu.make_async_copy(
            result.at[j, pl.ds(4, 4)], target.at[meta[1, j]], b_sem.at[j]
        )

    def begin(j, carry):
        tile_copy(j).start()

        @pl.when(meta[8, j] == 0)
        def _():
            orb_copy(j, own_hbm).start()

        @pl.when(meta[8, j] != 0)
        def _():
            orb_copy(j, other_hbm).start()

        return carry

    def work(j, carry):
        tile_copy(j).wait()
        orb_copy(j, own_hbm).wait()
        masked = (tile[j] * mask_ref[j][None]).reshape(8 * 128, 128)
        product = jnp.dot(masked, orb[j], preferred_element_type=F32).astype(BF)
        result[j] = product.reshape(8, 128, 128)
        a_copy(j).start()
        for s, target in enumerate((b0_hbm, b1_hbm, b2_hbm, b3_hbm)):

            @pl.when(meta[2, j] == s)
            def _(target=target):
                b_copy(j, target).start()

        return carry

    def end(j, carry):
        a_copy(j).wait()
        b_copy(j, b0_hbm).wait()
        return carry

    lax.fori_loop(0, live[0], begin, 0)
    lax.fori_loop(0, live[0], work, 0)
    lax.fori_loop(0, live[0], end, 0)


def transform(meta, live, tiles, mask, own, other):
    smem = pl.BlockSpec(memory_space=pltpu.SMEM)
    hbm = pl.BlockSpec(memory_space=pl.ANY)
    vmem = pl.BlockSpec(memory_space=pltpu.VMEM)
    sems = pltpu.SemaphoreType.DMA((16,))
    return pl.pallas_call(
        transform_kernel,
        in_specs=[smem, smem, hbm, vmem, hbm, hbm],
        out_specs=[hbm] * 5,
        out_shape=[jax.ShapeDtypeStruct((32, 4, 128, 128), BF)]
        + [jax.ShapeDtypeStruct((8, 4, 128, 128), BF)] * 4,
        scratch_shapes=[
            pltpu.VMEM((16, 8, 128, 128), BF),
            pltpu.VMEM((16, 128, 128), BF),
            pltpu.VMEM((16, 8, 128, 128), BF),
            sems,
            sems,
            sems,
            sems,
        ],
        compiler_params=params(),
        cost_estimate=cost(2 * 16 * 8 * 128**3, 10 * 2**20),
        name="transform",
    )(meta, live, tiles, mask, own, other)


def collect_kernel(
    along_x, codes, source, place, mine, a_ref, b_ref, c_ref, d_ref, out_ref, acc, table, count
):
    j = pl.program_id(0)

    @pl.when(j == 0)
    def _():
        for k in range(SIDE):
            for t in range(SIDE):
                count[t] = 0
                for r in range(CAP):
                    table[(k * SIDE + t) * CAP + r] = 0
            row = source[k]

            def visit(slot, carry):
                code = codes[row, slot]
                owner = code // 4
                fixed, free = (owner // 4, owner % 4) if along_x else (owner % 4, owner // 4)

                @pl.when(jnp.logical_and(code >= 0, fixed == mine[0]))
                def _():
                    rank = jnp.minimum(count[free], CAP - 1)
                    table[(k * SIDE + free) * CAP + rank] = code % 4 + 1
                    count[free] = rank + 1

                return carry

            lax.fori_loop(0, 16, visit, 0)

    acc[...] = jnp.zeros(acc.shape, F32)
    for k, ref in enumerate((a_ref, b_ref, c_ref, d_ref)):
        for r in range(CAP):
            code = table[(k * SIDE + j) * CAP + r]

            @pl.when(code > 0)
            def _(ref=ref, r=r, code=code):
                acc[code - 1] += ref[0, r].astype(F32)

    for s in range(4):
        out_ref[0, :, s * 128 : (s + 1) * 128, :] = acc[s].astype(BF)


def collect(along_x, codes, source, place, mine, pieces, offsets):
    block = (1, CAP, 4, 128, 128)
    specs = [
        pl.BlockSpec(block, functools.partial(lambda o, j, *_: (o + j, 0, 0, 0, 0), o))
        for o in offsets
    ]
    grid_spec = pltpu.PrefetchScalarGridSpec(
        num_scalar_prefetch=4,
        grid=(SIDE,),
        in_specs=specs,
        out_specs=pl.BlockSpec(
            (1, 4, 512, 128), lambda j, codes, source, place, mine: (place[j], 0, 0, 0)
        ),
        scratch_shapes=[
            pltpu.VMEM((4, 4, 128, 128), F32),
            pltpu.SMEM((4 * SIDE * CAP,), jnp.int32),
            pltpu.SMEM((SIDE,), jnp.int32),
        ],
    )
    return pl.pallas_call(
        functools.partial(collect_kernel, along_x),
        grid_spec=grid_spec,
        out_shape=jax.ShapeDtypeStruct((SIDE, 4, 512, 128), BF),
        compiler_params=params(),
        cost_estimate=cost(2**22, 6 * 2**20),
        name="collect",
    )(codes, source, place, mine, *pieces)


def finish_kernel(*refs):
    out_ref = refs[-1]
    for half in range(2):
        total = refs[4 * half][0].astype(F32)
        for k in range(1, 4):
            total += refs[4 * half + k][0].astype(F32)
        for p in range(4):
            turned = total[p].T.astype(BF)
            out_ref[:, 4 * half + p] = turned.reshape(8, 16, 128)


def finish(pieces, offsets):
    specs = [
        pl.BlockSpec((1, 4, 128, 128), functools.partial(lambda o, m: (o, 0, m, 0), o))
        for o in offsets
    ]
    return pl.pallas_call(
        finish_kernel,
        grid=(4,),
        in_specs=specs,
        out_specs=pl.BlockSpec((8, 8, 16, 128), lambda m: (0, 0, 0, m)),
        out_shape=jax.ShapeDtypeStruct((8, 8, 16, 512), BF),
        compiler_params=params(),
        cost_estimate=cost(2**21, 5 * 2**20),
        name="finish",
    )(*pieces)


def product_kernel(has_add, zsel, psel, left_ref, f0, f1, f2, f3, *rest):
    out_ref = rest[-1]
    x2 = pl.program_id(0)
    for s, ref in enumerate((f0, f1, f2, f3)):

        @pl.when(psel[x2] == s)
        def _(ref=ref):
            value = jnp.dot(left_ref[0], ref[...], preferred_element_type=F32)
            if has_add:
                value += rest[0][0].astype(F32)
            out_ref[0] = value.astype(BF)


def product(zsel, psel, left, columns, add=None):
    whole = pl.BlockSpec((1024, 512), lambda x2, *_: (0, 0))
    tile = pl.BlockSpec((1, 512, 512), lambda x2, *_: (x2, 0, 0))
    specs = [pl.BlockSpec((1, 512, 1024), lambda x2, zsel, psel: (zsel[0], 0, 0))] + [whole] * 4
    operands = [left, *columns]
    if add is not None:
        specs.append(tile)
        operands.append(add)
    grid_spec = pltpu.PrefetchScalarGridSpec(
        num_scalar_prefetch=2, grid=(SIDE,), in_specs=specs, out_specs=tile
    )
    return pl.pallas_call(
        functools.partial(product_kernel, add is not None),
        grid_spec=grid_spec,
        out_shape=jax.ShapeDtypeStruct((SIDE, 512, 512), BF),
        compiler_params=params(),
        cost_estimate=cost(4 * 2 * 512 * 512 * 1024, 7 * 2**20),
        name="product",
    )(zsel, psel, *operands)


def per_device(
    three_index, pair_mask, pair_owner, pair_sub, pair_nu, live_count, coefficients, fit_matrix
):
    slots = three_index.shape[0]
    x, z, y, c = (lax.axis_index(name) for name in ("x", "z", "y", "c"))

    swapped_fit = lax.ppermute(fit_matrix, "c", [(0, 1), (1, 0)])
    pair_fit = jnp.where(
        c == 0,
        jnp.concatenate([fit_matrix, swapped_fit], 0),
        jnp.concatenate([swapped_fit, fit_matrix], 0),
    )
    fits = jnp.stack([pair_fit] + [shifted(pair_fit, "y", s) for s in (1, 2, 3)])
    fit = fits[(y - jnp.arange(4)) % 4].reshape(64, 64)

    alive = jnp.arange(slots) < live_count[0]
    code = jnp.where(alive, pair_owner[:, 0] * 4 + pair_sub, -1).astype(BF)
    half_blocks = lax.dynamic_slice_in_dim(coefficients, c * 256, 256, 0)
    code_rows = jnp.broadcast_to(jnp.pad(code, (0, 112))[None], (16, 128))
    sent = jnp.concatenate([half_blocks, code_rows], 0)
    own = lax.all_to_all(
        jnp.broadcast_to(sent[None], (16, 272, 128)), ("x", "z"), 0, 0, tiled=True
    )
    other = lax.ppermute(own, "c", [(0, 1), (1, 0)])
    codes = own[:, 256, :slots].astype(jnp.int32)

    where = jnp.stack([x, z, c]).astype(jnp.int32)
    meta = plan(where, pair_owner, pair_nu)
    mask = jnp.repeat(jnp.repeat(pair_mask, 16, 1), 16, 2).astype(BF)

    out_a, *out_b = transform(meta, live_count, three_index, mask, own, other)
    got_a = lax.all_to_all(
        out_a.reshape(4, 8, 4, 128, 128), "z", 0, 0, tiled=True
    ).reshape(16, CAP, 4, 128, 128)
    out_b = [piece.reshape(4, CAP, 4, 128, 128) for piece in out_b]
    got_b = [out_b[0]] + [shifted(out_b[s], "x", s) for s in (1, 2, 3)]
    steps = jnp.arange(4, dtype=jnp.int32)
    sum_a = collect(False, codes, x * 4 + steps, steps, z[None], [got_a] * 4, (0, 4, 8, 12))
    last_a = lax.all_to_all(sum_a, "x", 0, 0, tiled=True)
    sum_b = collect(
        True, codes, (x - steps) % 4 * 4 + z, (steps - z) % 4, x[None], got_b, (0,) * 4
    )
    last_b = [sum_b[:1]] + [shifted(sum_b[s : s + 1], "z", s) for s in (1, 2, 3)]
    cut = finish([last_a] * 4 + last_b, (0, 1, 2, 3, 0, 0, 0, 0))

    rows = lax.all_to_all(cut, ("y", "c"), 0, 0, tiled=True).reshape(1024, 512)

    spread = (jnp.arange(1024)[:, None] // 16 == jnp.arange(64)[None, :]).astype(BF)
    mixing = jnp.dot(jnp.dot(spread, fit, preferred_element_type=F32).astype(BF), spread.T)
    same = jnp.arange(1024)[:, None] % 16 == jnp.arange(1024)[None, :] % 16
    mixing = jnp.where(same, mixing, 0).astype(BF)

    fitted = jnp.dot(mixing, rows, preferred_element_type=F32).astype(BF)
    left = lax.all_to_all(
        jnp.broadcast_to(rows.T[None], (4, 512, 1024)), "z", 0, 0, tiled=True
    )
    columns = [fitted] + [shifted(fitted, "x", s) for s in (1, 2, 3)]

    psel = ((x - jnp.arange(4)) % 4).astype(jnp.int32)
    swap = [(0, 1), (1, 0)]
    turns = [((z + t) % 2)[None] for t in range(2)]
    theirs = [product(2 * (1 - c) + turn, psel, left, columns) for turn in turns]
    theirs = [lax.ppermute(part, "c", swap) for part in theirs]
    got = []
    for t in range(2):
        partial = product(2 * c + turns[t], psel, left, columns, theirs[t])
        parts = lax.all_to_all(partial, "y", 0, 0, tiled=True)
        tile = jnp.sum(parts.astype(F32), 0).astype(BF)
        pairs = [
            (zz * 2 + k, (2 * k + (zz + t) % 2) * 2 + zz // 2) for zz in range(4) for k in range(2)
        ]
        got.append(lax.ppermute(tile, ("z", "c"), pairs).astype(F32))
    scale = 8192 ** (-0.5)
    even = z % 2 == 0
    first = jnp.where(even, got[0], got[1]) * scale
    second = jnp.where(even, got[1], got[0]) * scale
    return jnp.concatenate([first, second], 1)


def solution(mesh):
    grid = Mesh(mesh.devices.reshape(4, 4, 4, 2), ("x", "z", "y", "c"))
    atom, aux = ("x", "z"), ("y", "c")
    in_specs = (
        P(atom, aux, None, None),
        P(atom, None, None),
        P(atom, None),
        P(atom),
        P(atom),
        P(atom),
        P(atom, None),
        P(aux, None),
    )
    return jax.shard_map(
        per_device, mesh=grid, in_specs=in_specs, out_specs=P(atom, aux), check_vma=False
    )
```

time: 425 us -> 332 us (0.78)
  blocking collectives: 90.1 us -> 46.3 us
  waiting for transfers between devices: 178 us -> 161 us
  Pallas kernels: 64 us -> 47.2 us
  local copies, waits for them, and re-layouts: 25.3 us -> 15.1 us
    unnamed x1 -> x0, blocking collectives: 53.7 us -> none
    all_to_all x1, waiting for transfers between devices: 0.01 us -> 45.3 us  [per_device(): lax.all_to_all(out_a.reshape(4, 8, 4, 128, 128), 'z', 0, 0, tiled=True)]
    ppermute x9 -> x12, waiting for transfers between devices: 96.4 us -> 69.3 us  [shifted(): lax.ppermute(value, axis, [(i, (i + shift) % SIDE) for i in range(SIDE)])]
    all_to_all x0 -> x1, blocking collectives: none -> 24.9 us  [per_device(): lax.all_to_all(jnp.broadcast_to(sent[None], (16, 272, 128)), ('x', 'z'),...]
    pallas_call x5, Pallas kernels: 43.3 us -> 22.3 us  [the longest x2 10.6 us: collect(): pl.pallas_call(functools.partial(collect_kernel, along_x), grid_spec=grid...]
    all_to_all x1 -> x0, waiting for transfers between devices: 12.1 us -> none  [per_device(): lax.all_to_all(jnp.broadcast_to(half_blocks[None], (16, 2, 128, 128)), ('...]
    all_gather x1 -> x0, blocking collectives: 12.1 us -> none  [per_device(): fit = lax.all_gather(fit_matrix, ('y', 'c'), axis=0, tiled=True)]
    all_to_all x1 -> x2, waiting for transfers between devices: 48.6 us -> 38 us  [per_device(): parts = lax.all_to_all(partial, 'y', 0, 0, tiled=True)]
  transfers between devices with their start and end apart: 18 -> 23, of which waited for: 13 -> 13; matrix products, arithmetic and copies ran while one was open for 4% -> 3% of each run, Pallas kernels for 6% -> 10%
where the time goes in v2:
time: 332 us; the launch traced here: 331 us
  waiting for transfers between devices  161 us (48%)
  starting transfers between devices  51.8 us (16%)
  Pallas kernels  47.2 us (14%)
  blocking collectives  46.3 us (14%)
  local copies, waits for them, and re-layouts  15.1 us (5%)
  other arithmetic  6.57 us (2%)
    ppermute x12, waiting for transfers between devices, shifted(): lax.ppermute(value, axis, [(i, (i + shift) % SIDE) for i in range(SIDE)])  69.3 us
    all_to_all x1, waiting for transfers between devices, per_device(): lax.all_to_all(out_a.reshape(4, 8, 4, 128, 128), 'z', 0, 0, tiled=True)  45.3 us
    all_to_all x2, waiting for transfers between devices, per_device(): parts = lax.all_to_all(partial, 'y', 0, 0, tiled=True)  38 us
    pallas_call x4, Pallas kernels, product(): pl.pallas_call(functools.partial(product_kernel, add is not None), grid_s...  25 us
    all_to_all x1, blocking collectives, per_device(): lax.all_to_all(jnp.broadcast_to(sent[None], (16, 272, 128)), ('x', 'z'),...  24.9 us
    all_to_all x1, blocking collectives, per_device(): rows = lax.all_to_all(cut, ('y', 'c'), 0, 0, tiled=True).reshape(1024, 512)  21.4 us
    ppermute x12, starting transfers between devices, shifted(): lax.ppermute(value, axis, [(i, (i + shift) % SIDE) for i in range(SIDE)])  13.7 us
    ppermute x2, starting transfers between devices, per_device(): got.append(lax.ppermute(tile, ('z', 'c'), pairs).astype(F32))  11.2 us
  transfers between devices with their start and end apart: 23, of which 13 were waited for; matrix products, arithmetic and copies ran while one was open for 3% of the time, Pallas kernels for 10%

profile of v2, /device:TPU:1, one launch (start us, length us, event | category | flops | bytes accessed | tf_op | source)
XLA Modules:
  0.0 331.0 jit_solution(6357744318797205858)
XLA Ops:
  0.7 0.7 fusion.18
  1.6 24.9 %all_to_all.35.own_hbm = bf16[16,272,128]{2,1,0:T(8,128)(2,1)S(1)} all-to-all(bf16[16,272,128]{2,1,0:T(8,128)(2,1)S(1)} %broadcast_in_dim.22), channel_id=1, replica_groups=mesh['x'=4,'z'=4,'y'=4,'c'=2] {'x','z'}, dimensions={0} | all-to-all | bytes 2228224 | tf_op jit(solution)/shard_map/all_to_all | solution.py:297
  26.5 2.2 collective-permute-start
  28.7 0.7 copy.21.owner
  30.3 0.6 pad_add_fusion.where
  30.9 1.9 plan.1.meta
  32.8 0.7 copy-done.7
  33.5 8.4 %transform.1 = (bf16[32,4,128,128]{3,2,1,0:T(8,128)(2,1)}, bf16[8,4,128,128]{3,2,1,0:T(8,128)(2,1)S(1)}, bf16[8,4,128,128]{3,2,1,0:T(8,128)(2,1)S(1)}, bf16[8,4,...) custom-call(s32[9,16]{1,0:T(8,128)S(1)} %copy-done.7, s32[1]{0:T(128)} %copy.29.live, ...), custom_call_target="tpu_custom_call" | custom-call | flops 536870912 | bytes 10485760 | tf_op jit(solution)/shard_map/transform/pallas_call | solution.py:123
  41.9 1.0 copy-done.8
  42.9 1.0 copy-done.9
  43.9 0.4 copy-done.10
  44.3 4.9 %all-to-all-start.1 = ((bf16[4,8,4,128,128]{4,3,2,1,0:T(8,128)(2,1)}), bf16[4,8,4,128,128]{4,3,2,1,0:T(8,128)(2,1)}, u32[]{:S(2)}, u32[]{:S(2)}) async-start(bf16[4,8,4,128,128]{4,3,2,1,0:T(8,128)(2,1)} %bitcast.47), calls=%async_computation.1 | async-start | bytes 8388608 | tf_op jit(solution)/shard_map/all_to_all | solution.py:308
  49.2 1.2 collective-permute-start.1
  50.4 1.7 collective-permute-start.2
  52.1 0.7 collective-permute-start.3
  52.9 45.3 %all-to-all-done.1 = bf16[4,8,4,128,128]{4,3,2,1,0:T(8,128)(2,1)} async-done(((bf16[4,8,4,128,128]{4,3,2,1,0:T(8,128)(2,1)}), bf16[4,8,4,128,128]{4,3,2,1,0:T(8,128)(2,1)}, u32[]{:S(2)}, u32[]{:S(2)}) %all-to-all-start.1) | async-done | bytes 4194336 | tf_op jit(solution)/shard_map/all_to_all | solution.py:308
  98.2 4.8 %collect.2 = bf16[4,4,512,128]{3,2,1,0:T(8,128)(2,1)S(1)} custom-call(s32[16,16]{1,0:T(8,128)S(1)} %fusion.13.codes, s32[4]{0:T(128)S(1)} %iota_add_fusion.source, s32[4]{0:T(128)S(1)} %iota.42.place, s32[1]{0:T(128)} %bitcast.4.mine, bf16[16,2,4,128,128]{4,3,2,1,0:T(8,128)(2,1)} %bitcast.9.a_ref.b_ref.c_ref.d_ref, ...), custom_call_target="tpu_custom_call" | custom-call | flops 4194304 | bytes 6291456 | tf_op jit(solution)/shard_map/collect/pallas_call | solution.py:205
  103.0 1.3 copy-done.2
  104.3 3.6 %all-to-all-start.2 = ((bf16[4,4,512,128]{3,2,1,0:T(8,128)(2,1)}), bf16[4,4,512,128]{3,2,1,0:T(8,128)(2,1)S(1)}, u32[]{:S(2)}, u32[]{:S(2)}) async-start(bf16[4,4,512,128]{3,2,1,0:T(8,128)(2,1)} %copy-done.2), calls=%async_computation.2 | async-start | bytes 4194304 | tf_op jit(solution)/shard_map/all_to_all | solution.py:315
  108.0 5.9 %collect.3 = bf16[4,4,512,128]{3,2,1,0:T(8,128)(2,1)} custom-call(s32[16,16]{1,0:T(8,128)S(1)} %fusion.13.codes, s32[4]{0:T(128)S(1)} %get-tuple-element.22.source, s32[4]{0:T(128)S(1)} %get-tuple-element.21.place, s32[1]{0:T(128)} %bitcast.5.mine, bf16[4,2,4,128,128]{4,3,2,1,0:T(8,128)(2,1)S(1)} %bitcast.42, ...), custom_call_target="tpu_custom_call" | custom-call | flops 4194304 | bytes 6291456 | tf_op jit(solution)/shard_map/collect/pallas_call | solution.py:205
  113.9 1.7 fusion.24
  115.9 1.9 collective-permute-start.5
  117.8 0.6 collective-permute-start.6
  118.4 11.6 %collective-permute-done.4.refs_5_ = bf16[1,4,512,128]{3,2,1,0:T(8,128)(2,1)S(1)} collective-permute-done((bf16[1,4,512,128]{3,2,1,0:T(8,128)(2,1)S(1)}, bf16[1,4,512,128]{3,2,1,0:T(8,128)(2,1)S(1)}, u32[]{:S(2)}, u32[]{:S(2)}) %collective-permute-start.4) | collective-permute-done | bytes 524320 | tf_op jit(solution)/shard_map/ppermute | solution.py:19
  130.0 10.3 %collective-permute-done.5.refs_6_ = bf16[1,4,512,128]{3,2,1,0:T(8,128)(2,1)S(1)} collective-permute-done((bf16[1,4,512,128]{3,2,1,0:T(8,128)(2,1)S(1)}, bf16[1,4,512,128]{3,2,1,0:T(8,128)(2,1)S(1)}, u32[]{:S(2)}, u32[]{:S(2)}) %collective-permute-start.5) | collective-permute-done | bytes 524320 | tf_op jit(solution)/shard_map/ppermute | solution.py:19
  140.3 0.8 copy-done.3
  141.1 0.8 copy-done.5
  141.9 1.0 copy-done.4
  142.9 1.0 copy-done.6
  144.0 1.3 finish.1
  145.3 21.4 %all_to_all.36 = bf16[8,8,16,512]{3,2,1,0:T(8,128)(2,1)S(1)} all-to-all(bf16[8,8,16,512]{3,2,1,0:T(8,128)(2,1)S(1)} %finish.1), channel_id=1, replica_groups=mesh['x'=4,'z'=4,'y'=4,'c'=2] {'y','c'}, dimensions={0} | all-to-all | bytes 2097152 | tf_op jit(solution)/shard_map/all_to_all | solution.py:322
  166.7 0.5 copy.24
  167.3 2.6 broadcast_in_dim.26
  169.8 5.0 %all-to-all-start.4 = ((bf16[4,512,1024]{2,1,0:T(8,128)(2,1)}), bf16[4,512,1024]{2,1,0:T(8,128)(2,1)}, u32[]{:S(2)}, u32[]{:S(2)}) async-start(bf16[4,512,1024]{2,1,0:T(8,128)(2,1)} %broadcast_in_dim.26), calls=%async_computation.4 | async-start | bytes 8388608 | tf_op jit(solution)/shard_map/all_to_all | solution.py:330
  174.8 1.1 collective-permute-start.7
  176.0 0.8 collective-permute-done.7
  176.8 0.9 collective-permute-start.10
  177.7 1.2 collective-permute-start.9
  178.9 0.8 collective-permute-done.10
  179.6 2.0 collective-permute-done.9
  181.6 1.3 collective-permute-done.8
  182.9 0.6 gather_fusion
  183.9 2.0 fusion.5.f0
  185.8 1.6 collective-permute-start.11
  187.4 2.3 collective-permute-start.12
  189.8 1.2 collective-permute-start.13
  190.9 19.3 %collective-permute-done.11.f1 = bf16[1024,512]{1,0:T(8,128)(2,1)S(1)} collective-permute-done((bf16[1024,512]{1,0:T(8,128)(2,1)S(1)}, bf16[1024,512]{1,0:T(8,128)(2,1)S(1)}, u32[]{:S(2)}, u32[]{:S(2)}) %collective-permute-start.11) | collective-permute-done | bytes 1048608 | tf_op jit(solution)/shard_map/ppermute | solution.py:19
  210.2 23.5 %collective-permute-done.12.f2 = bf16[1024,512]{1,0:T(8,128)(2,1)S(1)} collective-permute-done((bf16[1024,512]{1,0:T(8,128)(2,1)S(1)}, bf16[1024,512]{1,0:T(8,128)(2,1)S(1)}, u32[]{:S(2)}, u32[]{:S(2)}) %collective-permute-start.12) | collective-permute-done | bytes 1048608 | tf_op jit(solution)/shard_map/ppermute | solution.py:19
  233.8 0.5 collective-permute-done.13.f3
  234.3 5.9 %product.6 = bf16[4,512,512]{2,1,0:T(8,128)(2,1)} custom-call(s32[1]{0:T(128)} %bitcast.26.zsel, s32[4]{0:T(128)S(1)} %and_select_fusion.2.psel, bf16[4,512,1024]{2,1,0:T(8,128)(2,1)} %all-to-all-done.4.left_ref, bf16[1024,512]{1,0:T(8,128)(2,1)S(1)} %fusion.5.f0, bf16[1024,512]{1,0:T(8,128)(2,1)S(1)} %collective-permute-done.11.f1, ...), custom_call_target="tpu_custom_call" | custom-call | flops 2147483648 | bytes 7340032 | tf_op jit(solution)/shard_map/product/pallas_call | solution.py:267
  240.2 2.0 collective-permute-start.16
  242.2 5.9 %product.4 = bf16[4,512,512]{2,1,0:T(8,128)(2,1)} custom-call(s32[1]{0:T(128)} %bitcast.24.zsel, s32[4]{0:T(128)S(1)} %and_select_fusion.2.psel, bf16[4,512,1024]{2,1,0:T(8,128)(2,1)} %all-to-all-done.4.left_ref, bf16[1024,512]{1,0:T(8,128)(2,1)S(1)} %fusion.5.f0, bf16[1024,512]{1,0:T(8,128)(2,1)S(1)} %collective-permute-done.11.f1, ...), custom_call_target="tpu_custom_call" | custom-call | flops 2147483648 | bytes 7340032 | tf_op jit(solution)/shard_map/product/pallas_call | solution.py:267
  248.2 6.6 %product.7 = bf16[4,512,512]{2,1,0:T(8,128)(2,1)} custom-call(s32[1]{0:T(128)} %bitcast.25.zsel, s32[4]{0:T(128)S(1)} %and_select_fusion.2.psel, bf16[4,512,1024]{2,1,0:T(8,128)(2,1)} %all-to-all-done.4.left_ref, bf16[1024,512]{1,0:T(8,128)(2,1)S(1)} %fusion.5.f0, bf16[1024,512]{1,0:T(8,128)(2,1)S(1)} %collective-permute-done.11.f1, ...), custom_call_target="tpu_custom_call" | custom-call | flops 2147483648 | bytes 7340032 | tf_op jit(solution)/shard_map/product/pallas_call | solution.py:267
  254.7 4.5 %all-to-all-start.6 = ((bf16[4,512,512]{2,1,0:T(8,128)(2,1)}), bf16[4,512,512]{2,1,0:T(8,128)(2,1)}, u32[]{:S(2)}, u32[]{:S(2)}) async-start(bf16[4,512,512]{2,1,0:T(8,128)(2,1)} %product.7), calls=%async_computation.6 | async-start | bytes 4194304 | tf_op jit(solution)/shard_map/all_to_all | solution.py:343
  259.3 6.6 %product.5 = bf16[4,512,512]{2,1,0:T(8,128)(2,1)} custom-call(s32[1]{0:T(128)} %bitcast.zsel, s32[4]{0:T(128)S(1)} %and_select_fusion.2.psel, bf16[4,512,1024]{2,1,0:T(8,128)(2,1)} %all-to-all-done.4.left_ref, bf16[1024,512]{1,0:T(8,128)(2,1)S(1)} %fusion.5.f0, bf16[1024,512]{1,0:T(8,128)(2,1)S(1)} %collective-permute-done.11.f1, ...), custom_call_target="tpu_custom_call" | custom-call | flops 2147483648 | bytes 7340032 | tf_op jit(solution)/shard_map/product/pallas_call | solution.py:267
  265.9 19.4 %all-to-all-done.6 = bf16[4,512,512]{2,1,0:T(8,128)(2,1)} async-done(((bf16[4,512,512]{2,1,0:T(8,128)(2,1)}), bf16[4,512,512]{2,1,0:T(8,128)(2,1)}, u32[]{:S(2)}, u32[]{:S(2)}) %all-to-all-start.6) | async-done | bytes 2097184 | tf_op jit(solution)/shard_map/all_to_all | solution.py:343
  285.2 3.6 %all-to-all-start.5 = ((bf16[4,512,512]{2,1,0:T(8,128)(2,1)}), bf16[4,512,512]{2,1,0:T(8,128)(2,1)S(1)}, u32[]{:S(2)}, u32[]{:S(2)}) async-start(bf16[4,512,512]{2,1,0:T(8,128)(2,1)} %product.5), calls=%async_computation.5 | async-start | bytes 4194304 | tf_op jit(solution)/shard_map/all_to_all | solution.py:343
  288.9 2.2 reduce_sum.25
  291.0 4.1 %collective-permute-start.17 = (bf16[512,512]{1,0:T(8,128)(2,1)S(1)}, bf16[512,512]{1,0:T(8,128)(2,1)S(1)}, u32[]{:S(2)}, u32[]{:S(2)}) collective-permute-start(bf16[512,512]{1,0:T(8,128)(2,1)S(1)} %reduce_sum.25), channel_id=1, source_target_pairs={{0,8},{1,24},{8,0},{9,16},{16,9},{17,25},{24,1},{25,17},{2,10},{3,... | collective-permute-start | bytes 1572872 | tf_op jit(solution)/shard_map/ppermute | solution.py:348
  295.2 18.7 %all-to-all-done.5 = bf16[4,512,512]{2,1,0:T(8,128)(2,1)S(1)} async-done(((bf16[4,512,512]{2,1,0:T(8,128)(2,1)}), bf16[4,512,512]{2,1,0:T(8,128)(2,1)S(1)}, u32[]{:S(2)}, u32[]{:S(2)}) %all-to-all-start.5) | async-done | bytes 2097184 | tf_op jit(solution)/shard_map/all_to_all | solution.py:343
  313.8 1.2 reduce_sum.24
  315.1 7.1 %collective-permute-start.15 = (bf16[512,512]{1,0:T(8,128)(2,1)}, bf16[512,512]{1,0:T(8,128)(2,1)S(1)}, u32[]{:S(2)}, u32[]{:S(2)}) collective-permute-start(bf16[512,512]{1,0:T(8,128)(2,1)} %reduce_sum.24), channel_id=1, source_target_pairs={{0,0},{1,16},{8,8},{9,24},{16,1},{17,17},{24,9},{25,25},{2,2},{3,1... | collective-permute-start | bytes 1572872 | tf_op jit(solution)/shard_map/ppermute | solution.py:348
  322.2 7.0 %collective-permute-done.15 = bf16[512,512]{1,0:T(8,128)(2,1)S(1)} collective-permute-done((bf16[512,512]{1,0:T(8,128)(2,1)}, bf16[512,512]{1,0:T(8,128)(2,1)S(1)}, u32[]{:S(2)}, u32[]{:S(2)}) %collective-permute-start.15) | collective-permute-done | bytes 524320 | tf_op jit(solution)/shard_map/ppermute | solution.py:348
  329.5 1.5 pad_maximum_fusion
  (58 shorter events, 2.3 us)
Async XLA Ops:
  0.0 1.4 copy-start
  0.0 28.7 %copy-start.13 = (s32[16,1]{0,1:T(1,128)S(1)}, s32[16,1]{0,1:T(1,128)}, u32[]{:S(2)}) copy-start(s32[16,1]{0,1:T(1,128)} %param.10) | copy-start | bytes 196
  0.0 29.4 %copy-start.11 = (s32[16,8,8]{0,2,1:T(8,128)S(1)}, s32[16,8,8]{0,2,1:T(8,128)}, u32[]{:S(2)}) copy-start(s32[16,8,8]{0,2,1:T(8,128)} %param.9) | copy-start | bytes 12292
  26.5 6.3 %collective-permute-start = (bf16[16,272,128]{2,1,0:T(8,128)(2,1)S(1)}, bf16[16,272,128]{2,1,0:T(8,128)(2,1)}, u32[]{:S(2)}, u32[]{:S(2)}) collective-permute-start(bf16[16,272,128]{2,1,0:T(8,128)(2,1)S(1)} %all_to_all.35.own_hbm), channel_id=1, source_target_pairs={{0,1},{1,0},{2,3},{3,2},{4,5},{5,4},{6,7},{7,6},{8,9},{9,8},{10,11... | collective-permute-start | bytes 3342344 | tf_op jit(solution)/shard_map/ppermute | solution.py:300
  32.8 0.7 copy-start.7
  41.9 1.0 copy-start.8
  42.9 1.0 copy-start.9
  42.9 1.4 copy-start.10
  44.3 53.9 %all-to-all-start.1 = ((bf16[4,8,4,128,128]{4,3,2,1,0:T(8,128)(2,1)}), bf16[4,8,4,128,128]{4,3,2,1,0:T(8,128)(2,1)}, u32[]{:S(2)}, u32[]{:S(2)}) async-start(bf16[4,8,4,128,128]{4,3,2,1,0:T(8,128)(2,1)} %bitcast.47), calls=%async_computation.1 | async-start | bytes 8388608 | tf_op jit(solution)/shard_map/all_to_all | solution.py:308
  49.2 58.8 %collective-permute-start.1 = (bf16[4,2,4,128,128]{4,3,2,1,0:T(8,128)(2,1)}, bf16[4,2,4,128,128]{4,3,2,1,0:T(8,128)(2,1)}, u32[]{:S(2)}, u32[]{:S(2)}) collective-permute-start(bf16[4,2,4,128,128]{4,3,2,1,0:T(8,128)(2,1)} %bitcast.45), channel_id=1, source_target_pairs={{0,32},{32,64},{64,96},{96,0},{1,33},{33,65},{65,97},{97,1},{2,34}... | collective-permute-start | bytes 3145736 | tf_op jit(solution)/shard_map/ppermute | solution.py:19
  50.4 57.6 %collective-permute-start.2 = (bf16[4,2,4,128,128]{4,3,2,1,0:T(8,128)(2,1)}, bf16[4,2,4,128,128]{4,3,2,1,0:T(8,128)(2,1)}, u32[]{:S(2)}, u32[]{:S(2)}) collective-permute-start(bf16[4,2,4,128,128]{4,3,2,1,0:T(8,128)(2,1)} %bitcast.44), channel_id=1, source_target_pairs={{0,64},{32,96},{64,0},{96,32},{1,65},{33,97},{65,1},{97,33},{2,66}... | collective-permute-start | bytes 3145736 | tf_op jit(solution)/shard_map/ppermute | solution.py:19
  52.1 55.9 %collective-permute-start.3 = (bf16[4,2,4,128,128]{4,3,2,1,0:T(8,128)(2,1)}, bf16[4,2,4,128,128]{4,3,2,1,0:T(8,128)(2,1)}, u32[]{:S(2)}, u32[]{:S(2)}) collective-permute-start(bf16[4,2,4,128,128]{4,3,2,1,0:T(8,128)(2,1)} %bitcast.43), channel_id=1, source_target_pairs={{0,96},{32,0},{64,32},{96,64},{1,97},{33,1},{65,33},{97,65},{2,98}... | collective-permute-start | bytes 3145736 | tf_op jit(solution)/shard_map/ppermute | solution.py:19
  103.0 1.3 copy-start.2
  104.3 37.6 %all-to-all-start.2 = ((bf16[4,4,512,128]{3,2,1,0:T(8,128)(2,1)}), bf16[4,4,512,128]{3,2,1,0:T(8,128)(2,1)S(1)}, u32[]{:S(2)}, u32[]{:S(2)}) async-start(bf16[4,4,512,128]{3,2,1,0:T(8,128)(2,1)} %copy-done.2), calls=%async_computation.2 | async-start | bytes 4194304 | tf_op jit(solution)/shard_map/all_to_all | solution.py:315
  115.5 14.5 %collective-permute-start.4 = (bf16[1,4,512,128]{3,2,1,0:T(8,128)(2,1)S(1)}, bf16[1,4,512,128]{3,2,1,0:T(8,128)(2,1)S(1)}, u32[]{:S(2)}, u32[]{:S(2)}) collective-permute-start(bf16[1,4,512,128]{3,2,1,0:T(8,128)(2,1)S(1)} %get-tuple-element.17), channel_id=1, source_target_pairs={{0,8},{8,16},{16,24},{24,0},{1,9},{9,17},{17,25},{25,1},{2,10},{10... | collective-permute-start | bytes 1572872 | tf_op jit(solution)/shard_map/ppermute | solution.py:19
  115.9 24.4 %collective-permute-start.5 = (bf16[1,4,512,128]{3,2,1,0:T(8,128)(2,1)S(1)}, bf16[1,4,512,128]{3,2,1,0:T(8,128)(2,1)S(1)}, u32[]{:S(2)}, u32[]{:S(2)}) collective-permute-start(bf16[1,4,512,128]{3,2,1,0:T(8,128)(2,1)S(1)} %get-tuple-element.16), channel_id=1, source_target_pairs={{0,16},{8,24},{16,0},{24,8},{1,17},{9,25},{17,1},{25,9},{2,18},{10... | collective-permute-start | bytes 1572872 | tf_op jit(solution)/shard_map/ppermute | solution.py:19
  117.8 23.3 %collective-permute-start.6 = (bf16[1,4,512,128]{3,2,1,0:T(8,128)(2,1)S(1)}, bf16[1,4,512,128]{3,2,1,0:T(8,128)(2,1)S(1)}, u32[]{:S(2)}, u32[]{:S(2)}) collective-permute-start(bf16[1,4,512,128]{3,2,1,0:T(8,128)(2,1)S(1)} %get-tuple-element.15), channel_id=1, source_target_pairs={{0,24},{8,0},{16,8},{24,16},{1,25},{9,1},{17,9},{25,17},{2,26},{10... | collective-permute-start | bytes 1572872 | tf_op jit(solution)/shard_map/ppermute | solution.py:19
  140.3 0.8 copy-start.3
  141.1 0.8 copy-start.5
  141.9 1.0 copy-start.4
  142.9 1.0 copy-start.6
  169.8 5.0 %copy-start.12 = (bf16[8,64]{1,0:T(8,128)(2,1)S(1)}, bf16[8,64]{1,0:T(8,128)(2,1)}, u32[]{:S(2)}) copy-start(bf16[8,64]{1,0:T(8,128)(2,1)} %param.15) | copy-start | bytes 3076
  169.8 64.5 %all-to-all-start.4 = ((bf16[4,512,1024]{2,1,0:T(8,128)(2,1)}), bf16[4,512,1024]{2,1,0:T(8,128)(2,1)}, u32[]{:S(2)}, u32[]{:S(2)}) async-start(bf16[4,512,1024]{2,1,0:T(8,128)(2,1)} %broadcast_in_dim.26), calls=%async_computation.4 | async-start | bytes 8388608 | tf_op jit(solution)/shard_map/all_to_all | solution.py:330
  174.8 1.9 collective-permute-start.7
  176.8 2.9 collective-permute-start.10
  177.7 4.0 %collective-permute-start.9 = (bf16[16,64]{1,0:T(8,128)(2,1)S(1)}, bf16[16,64]{1,0:T(8,128)(2,1)S(1)}, u32[]{:S(2)}, u32[]{:S(2)}) collective-permute-start(bf16[16,64]{1,0:T(8,128)(2,1)S(1)} %maximum_select_fusion.1), channel_id=1, source_target_pairs={{0,4},{2,6},{4,0},{6,2},{1,5},{3,7},{5,1},{7,3},{8,12},{10,14},{12... | collective-permute-start | bytes 6152 | tf_op jit(solution)/shard_map/ppermute | solution.py:19
  178.9 4.1 %collective-permute-start.8 = (bf16[16,64]{1,0:T(8,128)(2,1)S(1)}, bf16[16,64]{1,0:T(8,128)(2,1)S(1)}, u32[]{:S(2)}, u32[]{:S(2)}) collective-permute-start(bf16[16,64]{1,0:T(8,128)(2,1)S(1)} %maximum_select_fusion.1), channel_id=1, source_target_pairs={{0,2},{2,4},{4,6},{6,0},{1,3},{3,5},{5,7},{7,1},{8,10},{10,12},{12... | collective-permute-start | bytes 6152 | tf_op jit(solution)/shard_map/ppermute | solution.py:19
  185.8 24.4 %collective-permute-start.11 = (bf16[1024,512]{1,0:T(8,128)(2,1)S(1)}, bf16[1024,512]{1,0:T(8,128)(2,1)S(1)}, u32[]{:S(2)}, u32[]{:S(2)}) collective-permute-start(bf16[1024,512]{1,0:T(8,128)(2,1)S(1)} %fusion.5.f0), channel_id=1, source_target_pairs={{0,32},{32,64},{64,96},{96,0},{1,33},{33,65},{65,97},{97,1},{2,34}... | collective-permute-start | bytes 3145736 | tf_op jit(solution)/shard_map/ppermute | solution.py:19
  187.4 46.3 %collective-permute-start.12 = (bf16[1024,512]{1,0:T(8,128)(2,1)S(1)}, bf16[1024,512]{1,0:T(8,128)(2,1)S(1)}, u32[]{:S(2)}, u32[]{:S(2)}) collective-permute-start(bf16[1024,512]{1,0:T(8,128)(2,1)S(1)} %fusion.5.f0), channel_id=1, source_target_pairs={{0,64},{32,96},{64,0},{96,32},{1,65},{33,97},{65,1},{97,33},{2,66}... | collective-permute-start | bytes 3145736 | tf_op jit(solution)/shard_map/ppermute | solution.py:19
  189.8 44.6 %collective-permute-start.13 = (bf16[1024,512]{1,0:T(8,128)(2,1)S(1)}, bf16[1024,512]{1,0:T(8,128)(2,1)}, u32[]{:S(2)}, u32[]{:S(2)}) collective-permute-start(bf16[1024,512]{1,0:T(8,128)(2,1)S(1)} %fusion.5.f0), channel_id=1, source_target_pairs={{0,96},{32,0},{64,32},{96,64},{1,97},{33,1},{65,33},{97,65},{2,98}... | collective-permute-start | bytes 3145736 | tf_op jit(solution)/shard_map/ppermute | solution.py:19
  240.2 8.0 %collective-permute-start.16 = (bf16[4,512,512]{2,1,0:T(8,128)(2,1)}, bf16[4,512,512]{2,1,0:T(8,128)(2,1)}, u32[]{:S(2)}, u32[]{:S(2)}) collective-permute-start(bf16[4,512,512]{2,1,0:T(8,128)(2,1)} %product.6), channel_id=1, source_target_pairs={{0,1},{1,0},{2,3},{3,2},{4,5},{5,4},{6,7},{7,6},{8,9},{9,8},{10,11... | collective-permute-start | bytes 6291464 | tf_op jit(solution)/shard_map/ppermute | solution.py:339
  248.2 11.1 %collective-permute-start.14 = (bf16[4,512,512]{2,1,0:T(8,128)(2,1)}, bf16[4,512,512]{2,1,0:T(8,128)(2,1)}, u32[]{:S(2)}, u32[]{:S(2)}) collective-permute-start(bf16[4,512,512]{2,1,0:T(8,128)(2,1)} %product.4), channel_id=1, source_target_pairs={{0,1},{1,0},{2,3},{3,2},{4,5},{5,4},{6,7},{7,6},{8,9},{9,8},{10,11... | collective-permute-start | bytes 6291464 | tf_op jit(solution)/shard_map/ppermute | solution.py:339
  254.7 30.5 %all-to-all-start.6 = ((bf16[4,512,512]{2,1,0:T(8,128)(2,1)}), bf16[4,512,512]{2,1,0:T(8,128)(2,1)}, u32[]{:S(2)}, u32[]{:S(2)}) async-start(bf16[4,512,512]{2,1,0:T(8,128)(2,1)} %product.7), calls=%async_computation.6 | async-start | bytes 4194304 | tf_op jit(solution)/shard_map/all_to_all | solution.py:343
  285.2 28.6 %all-to-all-start.5 = ((bf16[4,512,512]{2,1,0:T(8,128)(2,1)}), bf16[4,512,512]{2,1,0:T(8,128)(2,1)S(1)}, u32[]{:S(2)}, u32[]{:S(2)}) async-start(bf16[4,512,512]{2,1,0:T(8,128)(2,1)} %product.5), calls=%async_computation.5 | async-start | bytes 4194304 | tf_op jit(solution)/shard_map/all_to_all | solution.py:343
  291.0 31.1 %collective-permute-start.17 = (bf16[512,512]{1,0:T(8,128)(2,1)S(1)}, bf16[512,512]{1,0:T(8,128)(2,1)S(1)}, u32[]{:S(2)}, u32[]{:S(2)}) collective-permute-start(bf16[512,512]{1,0:T(8,128)(2,1)S(1)} %reduce_sum.25), channel_id=1, source_target_pairs={{0,8},{1,24},{8,0},{9,16},{16,9},{17,25},{24,1},{25,17},{2,10},{3,... | collective-permute-start | bytes 1572872 | tf_op jit(solution)/shard_map/ppermute | solution.py:348
  315.1 14.1 %collective-permute-start.15 = (bf16[512,512]{1,0:T(8,128)(2,1)}, bf16[512,512]{1,0:T(8,128)(2,1)S(1)}, u32[]{:S(2)}, u32[]{:S(2)}) collective-permute-start(bf16[512,512]{1,0:T(8,128)(2,1)} %reduce_sum.24), channel_id=1, source_target_pairs={{0,0},{1,16},{8,8},{9,24},{16,1},{17,17},{24,9},{25,25},{2,2},{3,1... | collective-permute-start | bytes 1572872 | tf_op jit(solution)/shard_map/ppermute | solution.py:348
  329.5 1.5 copy-start.1

commit v3 on v2

v3 whole, which is shorter than its diff:
```python
import functools

import jax
import jax.numpy as jnp
from jax import lax
from jax.experimental import pallas as pl
from jax.experimental.pallas import tpu as pltpu
from jax.sharding import Mesh
from jax.sharding import PartitionSpec as P

CAP = 2
SIDE = 4
MAIN = 6
CHUNKS = 1
BF = jnp.bfloat16
F32 = jnp.float32
VMEM = 60 * 1024 * 1024


def shifted(value, axis, shift):
    return lax.ppermute(value, axis, [(i, (i + shift) % SIDE) for i in range(SIDE)])


def params():
    return pltpu.CompilerParams(vmem_limit_bytes=VMEM)


def cost(flops, bytes_accessed):
    return pl.CostEstimate(flops=flops, bytes_accessed=bytes_accessed, transcendentals=0)


def plan_kernel(where, owner, nu, out, count):
    x, z, c = where[0], where[1], where[2]
    for o in range(2 * SIDE):
        count[o] = 0
    for j in range(16):
        target = owner[j, 0]
        to_x, to_z = target // 4, target % 4
        out[0, j] = to_z
        out[1, j] = count[to_z]
        count[to_z] = count[to_z] + 1
        out[2, j] = (to_x - x + 4) % 4
        out[3, j] = count[SIDE + to_x]
        count[SIDE + to_x] = count[SIDE + to_x] + 1
        atom = nu[j] // 4
        half = (nu[j] % 4) // 2
        out[4, j] = (z - atom % 4 + 4) % 4 + jnp.where(half == c, 0, SIDE)
        out[5, j] = (x - atom // 4 + 4) % 4
        out[6, j] = (nu[j] % 2) * 128


def plan(where, owner, nu):
    smem = pl.BlockSpec(memory_space=pltpu.SMEM)
    return pl.pallas_call(
        plan_kernel,
        in_specs=[smem] * 3,
        out_specs=smem,
        out_shape=jax.ShapeDtypeStruct((7, 16), jnp.int32),
        scratch_shapes=[pltpu.SMEM((2 * SIDE,), jnp.int32)],
        name="plan",
    )(where, owner, nu)


def transform_kernel(first, size, meta, live, tile_hbm, mask_ref, *refs):
    orb_hbm = refs[:8]
    a_main, a_extra, b_extra = refs[8:11]
    b_main = refs[11:15]
    tile, orb, result, tile_sem, orb_sem, a_sem, b_sem = refs[15:]

    def tile_copies(j):
        return [
            pltpu.make_async_copy(
                tile_hbm.at[j, pl.ds(start, size)], tile.at[j, pl.ds(h * size, size)], tile_sem.at[h, j]
            )
            for h, start in enumerate((first, 4 + first))
        ]

    def orb_copy(j, source):
        rows = pl.ds(pl.multiple_of(meta[6, j], 128), 128)
        return pltpu.make_async_copy(source.at[meta[5, j], rows], orb.at[j], orb_sem.at[j])

    def a_copy(j, target):
        return pltpu.make_async_copy(result.at[j, pl.ds(0, size)], target, a_sem.at[j])

    def b_copy(j, target):
        return pltpu.make_async_copy(result.at[j, pl.ds(size, size)], target, b_sem.at[j])

    def begin(j, carry):
        for copy in tile_copies(j):
            copy.start()
        for k, source in enumerate(orb_hbm):

            @pl.when(meta[4, j] == k)
            def _(source=source):
                orb_copy(j, source).start()

        return carry

    def work(j, carry):
        for copy in tile_copies(j):
            copy.wait()
        orb_copy(j, orb_hbm[0]).wait()
        masked = (tile[j] * mask_ref[j][None]).reshape(2 * size * 128, 128)
        product = jnp.dot(masked, orb[j], preferred_element_type=F32).astype(BF)
        result[j] = product.reshape(2 * size, 128, 128)
        group, entry = meta[0, j], meta[1, j]

        @pl.when(entry < MAIN)
        def _():
            a_copy(j, a_main.at[group, entry]).start()

        @pl.when(entry >= MAIN)
        def _():
            a_copy(j, a_extra.at[group, entry - MAIN]).start()

        piece, place = meta[2, j], meta[3, j]
        for s, target in enumerate(b_main):

            @pl.when(jnp.logical_and(piece == s, place < MAIN))
            def _(target=target):
                b_copy(j, target.at[place]).start()

        @pl.when(place >= MAIN)
        def _():
            b_copy(j, b_extra.at[piece, place - MAIN]).start()

        return carry

    def end(j, carry):
        a_copy(j, a_main.at[0, 0]).wait()
        b_copy(j, b_main[0].at[0]).wait()
        return carry

    lax.fori_loop(0, live[0], begin, 0)
    lax.fori_loop(0, live[0], work, 0)
    lax.fori_loop(0, live[0], end, 0)


def transform(first, size, meta, live, tiles, mask, orbitals):
    smem = pl.BlockSpec(memory_space=pltpu.SMEM)
    hbm = pl.BlockSpec(memory_space=pltpu.HBM)
    vmem = pl.BlockSpec(memory_space=pltpu.VMEM)
    sems = pltpu.SemaphoreType.DMA((16,))
    shapes = [(4, MAIN), (4, 8 - MAIN), (4, 8 - MAIN)] + [(MAIN,)] * 4
    return pl.pallas_call(
        functools.partial(transform_kernel, first, size),
        in_specs=[smem, smem, hbm, vmem] + [hbm] * 8,
        out_specs=[hbm] * 7,
        out_shape=[jax.ShapeDtypeStruct(shape + (size, 128, 128), BF) for shape in shapes],
        scratch_shapes=[
            pltpu.VMEM((16, 2 * size, 128, 128), BF),
            pltpu.VMEM((16, 128, 128), BF),
            pltpu.VMEM((16, 2 * size, 128, 128), BF),
            pltpu.SemaphoreType.DMA((2, 16)),
            sems,
            sems,
            sems,
        ],
        compiler_params=params(),
        cost_estimate=cost(2 * 16 * 2 * size * 128**3, 16 * 2 * size * 2**16),
        name="transform",
    )(meta, live, tiles, mask, *orbitals)


def collect_kernel(along_x, size, codes, source, place, mine, *refs):
    if along_x:
        main, extra, outs, rest = refs[:4], refs[4], refs[5:9], refs[9:]
    else:
        main, extra, outs, rest = [refs[0].at[k] for k in range(4)], refs[1], refs[2:3], refs[3:]
    buffer, acc, result, table, count, in_sem, out_sem = rest

    def arrival(k, q, origin):
        return pltpu.make_async_copy(origin, buffer.at[k, q], in_sem.at[k, q])

    def departure(j, target):
        return pltpu.make_async_copy(result.at[j], target, out_sem.at[j])

    for k in range(SIDE):
        for t in range(SIDE):
            count[t] = 0
            for r in range(CAP):
                table[(k * SIDE + t) * CAP + r] = 0
        row = source[k]

        def visit(slot, q, k=k, row=row):
            code = codes[row, slot]
            owner = code // 4
            fixed, free = (owner // 4, owner % 4) if along_x else (owner % 4, owner // 4)
            hit = jnp.logical_and(code >= 0, fixed == mine[0])

            @pl.when(hit)
            def _():
                rank = jnp.minimum(count[free], CAP - 1)
                table[(k * SIDE + free) * CAP + rank] = q * 4 + code % 4 + 1
                count[free] = rank + 1

            @pl.when(jnp.logical_and(hit, q < MAIN))
            def _():
                arrival(k, q, main[k].at[q]).start()

            @pl.when(jnp.logical_and(hit, q >= MAIN))
            def _():
                arrival(k, q, extra.at[k, q - MAIN]).start()

            return q + hit.astype(jnp.int32)

        lax.fori_loop(0, 16, visit, jnp.int32(0))

    for j in range(SIDE):
        acc[...] = jnp.zeros(acc.shape, F32)
        for k in range(SIDE):
            for r in range(CAP):
                code = table[(k * SIDE + j) * CAP + r]

                @pl.when(code > 0)
                def _(k=k, code=code):
                    q, sub = (code - 1) // 4, (code - 1) % 4
                    arrival(k, q, main[k].at[0]).wait()
                    acc[sub] += buffer[k, q].astype(F32)

        for s in range(4):
            result[j, :, s * 128 : (s + 1) * 128, :] = acc[s].astype(BF)
        if along_x:
            for s in range(SIDE):

                @pl.when(place[j] == s)
                def _(s=s, j=j):
                    departure(j, outs[s]).start()

        else:
            departure(j, outs[0].at[j]).start()
    for j in range(SIDE):
        departure(j, outs[0] if along_x else outs[0].at[0]).wait()


def collect(along_x, size, codes, source, place, mine, main, extra):
    smem = pl.BlockSpec(memory_space=pltpu.SMEM)
    hbm = pl.BlockSpec(memory_space=pltpu.HBM)
    out = (size, 512, 128)
    shapes = [jax.ShapeDtypeStruct(out, BF)] * 4 if along_x else [jax.ShapeDtypeStruct((4,) + out, BF)]
    return pl.pallas_call(
        functools.partial(collect_kernel, along_x, size),
        in_specs=[smem] * 4 + [hbm] * (len(main) + 1),
        out_specs=[hbm] * len(shapes),
        out_shape=shapes,
        scratch_shapes=[
            pltpu.VMEM((SIDE, 8, size, 128, 128), BF),
            pltpu.VMEM((4, size, 128, 128), F32),
            pltpu.VMEM((SIDE,) + out, BF),
            pltpu.SMEM((4 * SIDE * CAP,), jnp.int32),
            pltpu.SMEM((SIDE,), jnp.int32),
            pltpu.SemaphoreType.DMA((SIDE, 8)),
            pltpu.SemaphoreType.DMA((SIDE,)),
        ],
        compiler_params=params(),
        cost_estimate=cost(2**22, size * 3 * 2**19),
        name="collect",
    )(codes, source, place, mine, *main, extra)


def finish_kernel(size, first_ref, *refs):
    out_ref = refs[-1]
    for half in range(2):
        pieces = [first_ref[k] for k in range(4)] if half == 0 else [ref[...] for ref in refs[:4]]
        total = pieces[0].astype(F32)
        for piece in pieces[1:]:
            total += piece.astype(F32)
        for p in range(size):
            turned = total[p].T.astype(BF)
            out_ref[:, size * half + p] = turned.reshape(8, 16, 128)


def finish(size, first, pieces):
    return pl.pallas_call(
        functools.partial(finish_kernel, size),
        grid=(4,),
        in_specs=[pl.BlockSpec((4, size, 128, 128), lambda m: (0, 0, m, 0))]
        + [pl.BlockSpec((size, 128, 128), lambda m: (0, m, 0))] * 4,
        out_specs=pl.BlockSpec((8, 2 * size, 16, 128), lambda m: (0, 0, 0, m)),
        out_shape=jax.ShapeDtypeStruct((8, 2 * size, 16, 512), BF),
        compiler_params=params(),
        cost_estimate=cost(2**21, 5 * 2**20),
        name="finish",
    )(first, *pieces)


def product_kernel(has_add, zsel, psel, left_ref, f0, f1, f2, f3, *rest):
    out_ref = rest[-1]
    x2 = pl.program_id(0)
    for s, ref in enumerate((f0, f1, f2, f3)):

        @pl.when(psel[x2] == s)
        def _(ref=ref):
            value = jnp.dot(left_ref[0], ref[...], preferred_element_type=F32)
            if has_add:
                value += rest[0][0].astype(F32)
            out_ref[0] = value.astype(BF)


def product(zsel, psel, left, columns, add=None):
    whole = pl.BlockSpec((1024, 512), lambda x2, *_: (0, 0))
    tile = pl.BlockSpec((1, 512, 512), lambda x2, *_: (x2, 0, 0))
    specs = [pl.BlockSpec((1, 512, 1024), lambda x2, zsel, psel: (zsel[0], 0, 0))] + [whole] * 4
    operands = [left, *columns]
    if add is not None:
        specs.append(tile)
        operands.append(add)
    grid_spec = pltpu.PrefetchScalarGridSpec(
        num_scalar_prefetch=2, grid=(SIDE,), in_specs=specs, out_specs=tile
    )
    return pl.pallas_call(
        functools.partial(product_kernel, add is not None),
        grid_spec=grid_spec,
        out_shape=jax.ShapeDtypeStruct((SIDE, 512, 512), BF),
        compiler_params=params(),
        cost_estimate=cost(4 * 2 * 512 * 512 * 1024, 7 * 2**20),
        name="product",
    )(zsel, psel, *operands)


def per_device(
    three_index, pair_mask, pair_owner, pair_sub, pair_nu, live_count, coefficients, fit_matrix
):
    slots = three_index.shape[0]
    x, z, y, c = (lax.axis_index(name) for name in ("x", "z", "y", "c"))

    swapped_fit = lax.ppermute(fit_matrix, "c", [(0, 1), (1, 0)])
    pair_fit = jnp.where(
        c == 0,
        jnp.concatenate([fit_matrix, swapped_fit], 0),
        jnp.concatenate([swapped_fit, fit_matrix], 0),
    )
    fits = jnp.stack([pair_fit] + [shifted(pair_fit, "y", s) for s in (1, 2, 3)])
    fit = fits[(y - jnp.arange(4)) % 4].reshape(64, 64)

    alive = jnp.arange(slots) < live_count[0]
    code = jnp.where(alive, pair_owner[:, 0] * 4 + pair_sub, -1).astype(BF)
    half_blocks = lax.dynamic_slice_in_dim(coefficients, c * 256, 256, 0)
    code_rows = jnp.broadcast_to(jnp.pad(code, (0, 112))[None], (16, 128))
    sent = jnp.concatenate([half_blocks, code_rows], 0)
    swap = [(0, 1), (1, 0)]
    line = jnp.stack([sent] + [shifted(sent, "x", s) for s in (1, 2, 3)])
    halves = [line] + [shifted(line, "z", s) for s in (1, 2, 3)]
    orbitals = halves + [lax.ppermute(half, "c", swap) for half in halves]
    codes = jnp.concatenate([half[:, 256, :slots] for half in halves], 0).astype(jnp.int32)

    where = jnp.stack([x, z, c]).astype(jnp.int32)
    meta = plan(where, pair_owner, pair_nu)
    mask = jnp.repeat(jnp.repeat(pair_mask, 16, 1), 16, 2).astype(BF)
    mask, fit, meta = lax.optimization_barrier((mask, fit, meta))

    steps = jnp.arange(4, dtype=jnp.int32)
    to_x, to_z = codes // 16, codes // 4 % 4
    from_x, from_z = jnp.tile((x - steps) % 4, 4), jnp.repeat((z - steps) % 4, 4)

    def lengths(to, origin):
        hits = (codes[..., None] >= 0) & (to[..., None] == steps) & (to != origin[:, None])[..., None]
        return jnp.max(jnp.sum(hits.astype(jnp.int32), 1))

    overflow = jnp.maximum(lengths(to_x, from_x), lengths(to_z, from_z)) > MAIN

    size = 4 // CHUNKS

    def route(chunk):
        a_main, a_extra, b_extra, *b_main = transform(
            chunk * size, size, meta, live_count, three_index, mask, orbitals
        )
        a_got = lax.all_to_all(a_main, "z", 0, 0, tiled=True)
        b_got = [b_main[0]] + [shifted(b_main[s], "x", s) for s in (1, 2, 3)]

        def send_extra(a, b):
            moved = [b[:1]] + [shifted(b[s : s + 1], "x", s) for s in (1, 2, 3)]
            return lax.all_to_all(a, "z", 0, 0, tiled=True), jnp.concatenate(moved, 0)

        a_extra, b_extra = lax.cond(
            overflow, send_extra, lambda a, b: (a, b), a_extra, b_extra
        )
        (a_sum,) = collect(
            False, size, codes, (z - steps) % 4 * 4, steps, z[None], [a_got], a_extra
        )
        a_last = lax.all_to_all(a_sum, "x", 0, 0, tiled=True)
        b_sum = collect(True, size, codes, steps, (steps - z) % 4, x[None], b_got, b_extra)
        b_last = [b_sum[0]] + [shifted(b_sum[s], "z", s) for s in (1, 2, 3)]
        cut = finish(size, a_last, b_last)
        return lax.all_to_all(cut, ("y", "c"), 0, 0, tiled=True).reshape(-1, 512)

    (rows,) = [route(chunk) for chunk in range(CHUNKS)]

    spread = (jnp.arange(1024)[:, None] // 16 == jnp.arange(64)[None, :]).astype(BF)
    mixing = jnp.dot(jnp.dot(spread, fit, preferred_element_type=F32).astype(BF), spread.T)
    same = jnp.arange(1024)[:, None] % 16 == jnp.arange(1024)[None, :] % 16
    mixing = jnp.where(same, mixing, 0).astype(BF)

    fitted = jnp.dot(mixing, rows, preferred_element_type=F32).astype(BF)
    columns = [fitted] + [shifted(fitted, "x", s) for s in (1, 2, 3)]
    left = lax.all_to_all(
        jnp.broadcast_to(rows.T[None], (4, 512, 1024)), "z", 0, 0, tiled=True
    )

    psel = ((x - jnp.arange(4)) % 4).astype(jnp.int32)
    turns = [((z + t) % 2)[None] for t in range(2)]
    theirs = [product(2 * (1 - c) + turn, psel, left, columns) for turn in turns]
    theirs = [lax.ppermute(part, "c", swap) for part in theirs]
    got = []
    for t in range(2):
        partial = product(2 * c + turns[t], psel, left, columns, theirs[t])
        parts = lax.all_to_all(partial, "y", 0, 0, tiled=True)
        tile = jnp.sum(parts.astype(F32), 0).astype(BF)
        pairs = [
            (zz * 2 + k, (2 * k + (zz + t) % 2) * 2 + zz // 2) for zz in range(4) for k in range(2)
        ]
        got.append(lax.ppermute(tile, ("z", "c"), pairs).astype(F32))
    scale = 8192 ** (-0.5)
    even = z % 2 == 0
    first = jnp.where(even, got[0], got[1]) * scale
    second = jnp.where(even, got[1], got[0]) * scale
    return jnp.concatenate([first, second], 1)


def solution(mesh):
    grid = Mesh(mesh.devices.reshape(4, 4, 4, 2), ("x", "z", "y", "c"))
    atom, aux = ("x", "z"), ("y", "c")
    in_specs = (
        P(atom, aux, None, None),
        P(atom, None, None),
        P(atom, None),
        P(atom),
        P(atom),
        P(atom),
        P(atom, None),
        P(aux, None),
    )
    return jax.shard_map(
        per_device, mesh=grid, in_specs=in_specs, out_specs=P(atom, aux), check_vma=False
    )
```

time: 332 us -> 377 us (1.14)
  waiting for transfers between devices: 161 us -> 207 us
  blocking collectives: 46.3 us -> 20.4 us
  starting transfers between devices: 51.8 us -> 64.4 us
  Pallas kernels: 47.2 us -> 52.9 us
  other arithmetic: 6.57 us -> 11.7 us
    ppermute x12 -> x18, waiting for transfers between devices: 69.3 us -> 125 us  [shifted(): lax.ppermute(value, axis, [(i, (i + shift) % SIDE) for i in range(SIDE)])]
    all_to_all x2 -> x1, blocking collectives: 46.3 us -> 20.4 us  [route(): return lax.all_to_all(cut, ('y', 'c'), 0, 0, tiled=True).reshape(-1, 512)]
    ppermute x12 -> x18, starting transfers between devices: 13.7 us -> 24.7 us  [shifted(): lax.ppermute(value, axis, [(i, (i + shift) % SIDE) for i in range(SIDE)])]
    all_to_all x2, waiting for transfers between devices: 45.3 us -> 36.1 us  [the longest x1 36 us: route(): a_got = lax.all_to_all(a_main, 'z', 0, 0, tiled=True)]
    pallas_call x4, Pallas kernels: 25 us -> 29.4 us  [product(): pl.pallas_call(functools.partial(product_kernel, add is not None), grid_s...]
    unnamed x29 -> x47, local copies, waits for them, and re-layouts: 8.77 us -> 7.62 us
  transfers between devices with their start and end apart: 23 -> 32, of which waited for: 13 -> 15; matrix products, arithmetic and copies ran while one was open for 3% -> 4% of each run, Pallas kernels for 10% -> 8%
where the time goes in v3:
time: 377 us; the launch traced here: 376 us
  waiting for transfers between devices  207 us (55%)
  starting transfers between devices  64.4 us (17%)
  Pallas kernels  52.9 us (14%)
  blocking collectives  20.4 us (5%)
  local copies, waits for them, and re-layouts  14.3 us (4%)
  other arithmetic  11.7 us (3%)
    ppermute x18, waiting for transfers between devices, shifted(): lax.ppermute(value, axis, [(i, (i + shift) % SIDE) for i in range(SIDE)])  125 us
    all_to_all x2, waiting for transfers between devices, per_device(): parts = lax.all_to_all(partial, 'y', 0, 0, tiled=True)  38.5 us
    all_to_all x1, waiting for transfers between devices, route(): a_got = lax.all_to_all(a_main, 'z', 0, 0, tiled=True)  36 us
    pallas_call x4, Pallas kernels, product(): pl.pallas_call(functools.partial(product_kernel, add is not None), grid_s...  29.4 us
    ppermute x18, starting transfers between devices, shifted(): lax.ppermute(value, axis, [(i, (i + shift) % SIDE) for i in range(SIDE)])  24.7 us
    all_to_all x1, blocking collectives, route(): return lax.all_to_all(cut, ('y', 'c'), 0, 0, tiled=True).reshape(-1, 512)  20.4 us
    ppermute x2, starting transfers between devices, per_device(): got.append(lax.ppermute(tile, ('z', 'c'), pairs).astype(F32))  10.9 us
    pallas_call x2, Pallas kernels, collect(): pl.pallas_call(functools.partial(collect_kernel, along_x, size), in_specs...  10.1 us
  transfers between devices with their start and end apart: 32, of which 15 were waited for; matrix products, arithmetic and copies ran while one was open for 4% of the time, Pallas kernels for 8%

profile of v3, /device:TPU:1, one launch (start us, length us, event | category | flops | bytes accessed | tf_op | source)
XLA Modules:
  0.0 375.5 jit_solution(9054128728028942597)
XLA Ops:
  0.7 0.7 fusion.26
  1.4 3.4 collective-permute-start.5
  5.9 1.5 collective-permute-start.9
  7.5 1.0 collective-permute-done.9
  8.5 0.8 maximum_select_fusion.1
  9.3 2.7 collective-permute-start.12
  12.1 3.8 %collective-permute-start.8 = (bf16[4,272,128]{2,1,0:T(8,128)(2,1)S(1)}, bf16[4,272,128]{2,1,0:T(8,128)(2,1)S(1)}, u32[]{:S(2)}, u32[]{:S(2)}) collective-permute-start(bf16[4,272,128]{2,1,0:T(8,128)(2,1)S(1)} %pad_maximum_fusion.2.refs_0_), channel_id=1, source_target_pairs={{0,24},{8,0},{16,8},{24,16},{1,25},{9,1},{17,9},{25,17},{2,26},{10... | collective-permute-start | bytes 835592 | tf_op jit(solution)/shard_map/ppermute | solution.py:21
  15.9 0.7 collective-permute-start.6
  17.2 1.3 copy.17.owner
  18.5 0.8 convert_element_type.49
  20.1 2.0 plan.1.meta
  22.1 1.5 collective-permute-start.11
  24.0 0.8 maximum_select_fusion
  24.7 1.6 collective-permute-done.11
  26.4 1.2 collective-permute-done.10
  28.2 1.0 copy.18.mask_ref
  29.2 3.8 %collective-permute-start.13 = (bf16[4,272,128]{2,1,0:T(8,128)(2,1)S(1)}, bf16[4,272,128]{2,1,0:T(8,128)(2,1)S(1)}, u32[]{:S(2)}, u32[]{:S(2)}) collective-permute-start(bf16[4,272,128]{2,1,0:T(8,128)(2,1)S(1)} %pad_maximum_fusion.2.refs_0_), channel_id=1, source_target_pairs={{0,1},{1,0},{2,3},{3,2},{4,5},{5,4},{6,7},{7,6},{8,9},{9,8},{10,11... | collective-permute-start | bytes 835592 | tf_op jit(solution)/shard_map/ppermute | solution.py:344
  34.2 0.7 reduce_max.18
  34.9 0.7 reduce_max.19
  37.8 0.7 copy-done.19
  38.5 7.1 %transform.1 = (bf16[4,6,4,128,128]{4,3,2,1,0:T(8,128)(2,1)}, bf16[4,2,4,128,128]{4,3,2,1,0:T(8,128)(2,1)}, bf16[4,2,4,128,128]{4,3,2,1,0:T(8,128)(2,1)S(1)}, bf...) custom-call(s32[7,16]{1,0:T(8,128)} %plan.1.meta, ...), custom_call_target="tpu_custom_call" | custom-call | flops 536870912 | bytes 8388608 | tf_op jit(solution)/shard_map/transform/pallas_call | solution.py:145
  45.7 1.0 copy-done.7
  46.7 3.7 all-to-all-start.1
  51.6 36.0 %all-to-all-done.1.refs_0_ = bf16[4,6,4,128,128]{4,3,2,1,0:T(8,128)(2,1)S(1)} async-done(((bf16[4,6,4,128,128]{4,3,2,1,0:T(8,128)(2,1)}), bf16[4,6,4,128,128]{4,3,2,1,0:T(8,128)(2,1)S(1)}, u32[]{:S(2)}, u32[]{:S(2)}) %all-to-all-start.1) | async-done | bytes 3145760 | tf_op jit(solution)/shard_map/all_to_all | solution.py:368
  88.1 1.1 copy-done.5
  89.2 4.6 %collect.2 = bf16[4,4,512,128]{3,2,1,0:T(8,128)(2,1)} custom-call(s32[16,16]{1,0:T(8,128)} %fusion.33.codes, s32[4]{0:T(128)} %broadcast_multiply_fusion.source, s32[4]{0:T(128)} %iota.49.place, s32[1]{0:T(128)} %bitcast.7.mine, bf16[4,6,4,128,128]{4,3,2,1,0:T(8,128)(2,1)} %copy-done.5, bf16[4,2,4,128,128]{4,3,2,1,0:T(8,128)(2,1)} %get-tuple-element.36.refs_1_), custom_call_target="tpu_custom_call" | custom-call | flops 4194304 | bytes 6291456 | tf_op jit(solution)/shard_map/collect/pallas_call | solution.py:241
  93.9 3.8 all-to-all-start.2
  97.6 1.4 collective-permute-start.17
  99.1 2.4 collective-permute-start.18
  101.5 1.2 collective-permute-start.19
  103.2 36.2 %collective-permute-done.17.refs_1_ = bf16[6,4,128,128]{3,2,1,0:T(8,128)(2,1)} collective-permute-done((bf16[6,4,128,128]{3,2,1,0:T(8,128)(2,1)}, bf16[6,4,128,128]{3,2,1,0:T(8,128)(2,1)}, u32[]{:S(2)}, u32[]{:S(2)}) %collective-permute-start.17) | collective-permute-done | bytes 786464 | tf_op jit(solution)/shard_map/ppermute | solution.py:21
  139.4 17.2 %collective-permute-done.18.refs_2_ = bf16[6,4,128,128]{3,2,1,0:T(8,128)(2,1)} collective-permute-done((bf16[6,4,128,128]{3,2,1,0:T(8,128)(2,1)}, bf16[6,4,128,128]{3,2,1,0:T(8,128)(2,1)}, u32[]{:S(2)}, u32[]{:S(2)}) %collective-permute-start.18) | collective-permute-done | bytes 786464 | tf_op jit(solution)/shard_map/ppermute | solution.py:21
  157.2 5.5 %collect.3 = (bf16[4,512,128]{2,1,0:T(8,128)(2,1)}, bf16[4,512,128]{2,1,0:T(8,128)(2,1)}, bf16[4,512,128]{2,1,0:T(8,128)(2,1)}, bf16[4,512,128]{2,1,0:T(8,128)(2,1)}) custom-call(s32[16,16]{1,0:T(8,128)} %fusion.33.codes, s32[4]{0:T(128)} %iota.51.source, s32[4]{0:T(128)} %and_select_fusion.place, s32[1]{0:T(128)} %bitcast.16.mine, ...), custom_call_target="tpu_custom_call" | custom-call | flops 4194304 | bytes 6291456 | tf_op jit(solution)/shard_map/collect/pallas_call | solution.py:241
  162.8 2.1 collective-permute-start.21
  164.9 0.7 collective-permute-start.22
  165.6 10.4 %collective-permute-done.20.refs_1_ = bf16[4,512,128]{2,1,0:T(8,128)(2,1)S(1)} collective-permute-done((bf16[4,512,128]{2,1,0:T(8,128)(2,1)}, bf16[4,512,128]{2,1,0:T(8,128)(2,1)S(1)}, u32[]{:S(2)}, u32[]{:S(2)}) %collective-permute-start.20) | collective-permute-done | bytes 524320 | tf_op jit(solution)/shard_map/ppermute | solution.py:21
  176.0 10.2 %collective-permute-done.21.refs_2_ = bf16[4,512,128]{2,1,0:T(8,128)(2,1)S(1)} collective-permute-done((bf16[4,512,128]{2,1,0:T(8,128)(2,1)}, bf16[4,512,128]{2,1,0:T(8,128)(2,1)S(1)}, u32[]{:S(2)}, u32[]{:S(2)}) %collective-permute-start.21) | collective-permute-done | bytes 524320 | tf_op jit(solution)/shard_map/ppermute | solution.py:21
  186.2 2.5 collective-permute-done.22.refs_3_
  188.7 1.3 copy-done.6
  190.0 4.3 %finish.1 = bf16[8,8,16,512]{3,2,1,0:T(8,128)(2,1)} custom-call(bf16[4,4,512,128]{3,2,1,0:T(8,128)(2,1)} %copy-done.6, bf16[4,512,128]{2,1,0:T(8,128)(2,1)} %get-tuple-element.42.refs_0_, bf16[4,512,128]{2,1,0:T(8,128)(2,1)} %copy-done.11, bf16[4,512,128]{2,1,0:T(8,128)(2,1)} %copy-done.12, bf16[4,512,128]{2,1,0:T(8,128)(2,1)} %collective-permute-done.22.refs_3_), custom_call_target="tpu_custom_call" | custom-call | flops 2097152 | bytes 5242880 | tf_op jit(solution)/shard_map/finish/pallas_call | solution.py:274
  194.3 20.4 %all_to_all.34 = bf16[8,8,16,512]{3,2,1,0:T(8,128)(2,1)S(1)} all-to-all(bf16[8,8,16,512]{3,2,1,0:T(8,128)(2,1)} %finish.1), channel_id=1, replica_groups=mesh['x'=4,'z'=4,'y'=4,'c'=2] {'y','c'}, dimensions={0} | all-to-all | bytes 2097152 | tf_op jit(solution)/shard_map/all_to_all | solution.py:385
  215.2 2.6 broadcast_in_dim.26
  217.8 4.9 %all-to-all-start.4 = ((bf16[4,512,1024]{2,1,0:T(8,128)(2,1)}), bf16[4,512,1024]{2,1,0:T(8,128)(2,1)}, u32[]{:S(2)}, u32[]{:S(2)}) async-start(bf16[4,512,1024]{2,1,0:T(8,128)(2,1)} %broadcast_in_dim.26), calls=%async_computation.4 | async-start | bytes 8388608 | tf_op jit(solution)/shard_map/all_to_all | solution.py:396
  223.0 2.0 fusion.5.f0
  225.1 1.3 collective-permute-start.24
  226.4 1.7 collective-permute-start.25
  228.1 23.2 %collective-permute-done.23.f1 = bf16[1024,512]{1,0:T(8,128)(2,1)S(1)} collective-permute-done((bf16[1024,512]{1,0:T(8,128)(2,1)S(1)}, bf16[1024,512]{1,0:T(8,128)(2,1)S(1)}, u32[]{:S(2)}, u32[]{:S(2)}) %collective-permute-start.23) | collective-permute-done | bytes 1048608 | tf_op jit(solution)/shard_map/ppermute | solution.py:21
  251.4 19.8 %collective-permute-done.24.f2 = bf16[1024,512]{1,0:T(8,128)(2,1)S(1)} collective-permute-done((bf16[1024,512]{1,0:T(8,128)(2,1)S(1)}, bf16[1024,512]{1,0:T(8,128)(2,1)S(1)}, u32[]{:S(2)}, u32[]{:S(2)}) %collective-permute-start.24) | collective-permute-done | bytes 1048608 | tf_op jit(solution)/shard_map/ppermute | solution.py:21
  271.2 2.2 collective-permute-done.25.f3
  273.4 7.0 %product.6 = bf16[4,512,512]{2,1,0:T(8,128)(2,1)} custom-call(s32[1]{0:T(128)} %bitcast.22.zsel, s32[4]{0:T(128)} %copy-done.20, bf16[4,512,1024]{2,1,0:T(8,128)(2,1)} %all-to-all-done.4.left_ref, bf16[1024,512]{1,0:T(8,128)(2,1)} %copy-done.2, bf16[1024,512]{1,0:T(8,128)(2,1)} %copy-done.3, bf16[1024,512]{1,0:T(8,128)(2,1)} %copy-done.4, ...), custom_call_target="tpu_custom_call" | custom-call | flops 2147483648 | bytes 7340032 | tf_op jit(solution)/shard_map/product/pallas_call | solution.py:311
  280.4 2.2 collective-permute-start.28
  282.7 7.0 %product.4 = bf16[4,512,512]{2,1,0:T(8,128)(2,1)} custom-call(s32[1]{0:T(128)} %bitcast.20.zsel, s32[4]{0:T(128)} %copy-done.20, bf16[4,512,1024]{2,1,0:T(8,128)(2,1)} %all-to-all-done.4.left_ref, bf16[1024,512]{1,0:T(8,128)(2,1)} %copy-done.2, bf16[1024,512]{1,0:T(8,128)(2,1)} %copy-done.3, bf16[1024,512]{1,0:T(8,128)(2,1)} %copy-done.4, ...), custom_call_target="tpu_custom_call" | custom-call | flops 2147483648 | bytes 7340032 | tf_op jit(solution)/shard_map/product/pallas_call | solution.py:311
  289.7 1.3 copy-done.9
  291.0 7.7 %product.7 = bf16[4,512,512]{2,1,0:T(8,128)(2,1)} custom-call(s32[1]{0:T(128)} %bitcast.21.zsel, s32[4]{0:T(128)} %copy-done.20, bf16[4,512,1024]{2,1,0:T(8,128)(2,1)} %all-to-all-done.4.left_ref, bf16[1024,512]{1,0:T(8,128)(2,1)} %copy-done.2, bf16[1024,512]{1,0:T(8,128)(2,1)} %copy-done.3, bf16[1024,512]{1,0:T(8,128)(2,1)} %copy-done.4, ...), custom_call_target="tpu_custom_call" | custom-call | flops 2147483648 | bytes 7340032 | tf_op jit(solution)/shard_map/product/pallas_call | solution.py:311
  298.7 3.8 %all-to-all-start.6 = ((bf16[4,512,512]{2,1,0:T(8,128)(2,1)}), bf16[4,512,512]{2,1,0:T(8,128)(2,1)S(1)}, u32[]{:S(2)}, u32[]{:S(2)}) async-start(bf16[4,512,512]{2,1,0:T(8,128)(2,1)} %product.7), calls=%async_computation.6 | async-start | bytes 4194304 | tf_op jit(solution)/shard_map/all_to_all | solution.py:407
  302.6 7.6 %product.5 = bf16[4,512,512]{2,1,0:T(8,128)(2,1)} custom-call(s32[1]{0:T(128)} %bitcast.zsel, s32[4]{0:T(128)} %copy-done.20, bf16[4,512,1024]{2,1,0:T(8,128)(2,1)} %all-to-all-done.4.left_ref, bf16[1024,512]{1,0:T(8,128)(2,1)} %copy-done.2, bf16[1024,512]{1,0:T(8,128)(2,1)} %copy-done.3, bf16[1024,512]{1,0:T(8,128)(2,1)} %copy-done.4, ...), custom_call_target="tpu_custom_call" | custom-call | flops 2147483648 | bytes 7340032 | tf_op jit(solution)/shard_map/product/pallas_call | solution.py:311
  310.2 18.0 %all-to-all-done.6 = bf16[4,512,512]{2,1,0:T(8,128)(2,1)S(1)} async-done(((bf16[4,512,512]{2,1,0:T(8,128)(2,1)}), bf16[4,512,512]{2,1,0:T(8,128)(2,1)S(1)}, u32[]{:S(2)}, u32[]{:S(2)}) %all-to-all-start.6) | async-done | bytes 2097184 | tf_op jit(solution)/shard_map/all_to_all | solution.py:407
  328.2 4.5 %all-to-all-start.5 = ((bf16[4,512,512]{2,1,0:T(8,128)(2,1)}), bf16[4,512,512]{2,1,0:T(8,128)(2,1)}, u32[]{:S(2)}, u32[]{:S(2)}) async-start(bf16[4,512,512]{2,1,0:T(8,128)(2,1)} %product.5), calls=%async_computation.5 | async-start | bytes 4194304 | tf_op jit(solution)/shard_map/all_to_all | solution.py:407
  333.3 3.9 %collective-permute-start.29 = (bf16[512,512]{1,0:T(8,128)(2,1)S(1)}, bf16[512,512]{1,0:T(8,128)(2,1)S(1)}, u32[]{:S(2)}, u32[]{:S(2)}) collective-permute-start(bf16[512,512]{1,0:T(8,128)(2,1)S(1)} %reduce_sum.45), channel_id=1, source_target_pairs={{0,8},{1,24},{8,0},{9,16},{16,9},{17,25},{24,1},{25,17},{2,10},{3,... | collective-permute-start | bytes 1572872 | tf_op jit(solution)/shard_map/ppermute | solution.py:412
  337.3 20.5 %all-to-all-done.5 = bf16[4,512,512]{2,1,0:T(8,128)(2,1)} async-done(((bf16[4,512,512]{2,1,0:T(8,128)(2,1)}), bf16[4,512,512]{2,1,0:T(8,128)(2,1)}, u32[]{:S(2)}, u32[]{:S(2)}) %all-to-all-start.5) | async-done | bytes 2097184 | tf_op jit(solution)/shard_map/all_to_all | solution.py:407
  357.7 2.2 reduce_sum.44
  359.9 7.0 %collective-permute-start.27 = (bf16[512,512]{1,0:T(8,128)(2,1)S(1)}, bf16[512,512]{1,0:T(8,128)(2,1)S(1)}, u32[]{:S(2)}, u32[]{:S(2)}) collective-permute-start(bf16[512,512]{1,0:T(8,128)(2,1)S(1)} %reduce_sum.44), channel_id=1, source_target_pairs={{0,0},{1,16},{8,8},{9,24},{16,1},{17,17},{24,9},{25,25},{2,2},{3,1... | collective-permute-start | bytes 1572872 | tf_op jit(solution)/shard_map/ppermute | solution.py:412
  366.9 6.8 %collective-permute-done.27 = bf16[512,512]{1,0:T(8,128)(2,1)S(1)} collective-permute-done((bf16[512,512]{1,0:T(8,128)(2,1)S(1)}, bf16[512,512]{1,0:T(8,128)(2,1)S(1)}, u32[]{:S(2)}, u32[]{:S(2)}) %collective-permute-start.27) | collective-permute-done | bytes 524320 | tf_op jit(solution)/shard_map/ppermute | solution.py:412
  374.1 1.5 pad_maximum_fusion.1
  (106 shorter events, 10.4 us)
Async XLA Ops:
  0.0 1.4 copy-start
  1.4 10.6 %collective-permute-start.5 = (bf16[272,128]{1,0:T(8,128)(2,1)S(1)}, bf16[272,128]{1,0:T(8,128)(2,1)S(1)}, u32[]{:S(2)}, u32[]{:S(2)}) collective-permute-start(bf16[272,128]{1,0:T(8,128)(2,1)S(1)} %get-tuple-element.60), channel_id=1, source_target_pairs={{0,96},{32,0},{64,32},{96,64},{1,97},{33,1},{65,33},{97,65},{2,98}... | collective-permute-start | bytes 208904 | tf_op jit(solution)/shard_map/ppermute | solution.py:21
  4.8 7.2 %collective-permute-start.4 = (bf16[272,128]{1,0:T(8,128)(2,1)S(1)}, bf16[272,128]{1,0:T(8,128)(2,1)S(1)}, u32[]{:S(2)}, u32[]{:S(2)}) collective-permute-start(bf16[272,128]{1,0:T(8,128)(2,1)S(1)} %get-tuple-element.60), channel_id=1, source_target_pairs={{0,64},{32,96},{64,0},{96,32},{1,65},{33,97},{65,1},{97,33},{2,66}... | collective-permute-start | bytes 208904 | tf_op jit(solution)/shard_map/ppermute | solution.py:21
  5.3 6.7 %collective-permute-start.3 = (bf16[272,128]{1,0:T(8,128)(2,1)S(1)}, bf16[272,128]{1,0:T(8,128)(2,1)S(1)}, u32[]{:S(2)}, u32[]{:S(2)}) collective-permute-start(bf16[272,128]{1,0:T(8,128)(2,1)S(1)} %get-tuple-element.60), channel_id=1, source_target_pairs={{0,32},{32,64},{64,96},{96,0},{1,33},{33,65},{65,97},{97,1},{2,34}... | collective-permute-start | bytes 208904 | tf_op jit(solution)/shard_map/ppermute | solution.py:21
  5.9 2.5 collective-permute-start.9
  7.5 38.2 %copy-start.20 = (s32[4]{0:T(128)}, s32[4]{0:T(128)S(1)}, u32[]{:S(2)}) copy-start(s32[4]{0:T(128)S(1)} %and_select_fusion.3.psel) | copy-start | bytes 52
  9.3 14.3 %collective-permute-start.12 = (bf16[16,64]{1,0:T(8,128)(2,1)S(1)}, bf16[16,64]{1,0:T(8,128)(2,1)S(1)}, u32[]{:S(2)}, u32[]{:S(2)}) collective-permute-start(bf16[16,64]{1,0:T(8,128)(2,1)S(1)} %maximum_select_fusion.1), channel_id=1, source_target_pairs={{0,6},{2,0},{4,2},{6,4},{1,7},{3,1},{5,3},{7,5},{8,14},{10,8},{12,... | collective-permute-start | bytes 6152 | tf_op jit(solution)/shard_map/ppermute | solution.py:21
  12.0 24.9 %copy-start.10 = (bf16[4,272,128]{2,1,0:T(8,128)(2,1)}, bf16[4,272,128]{2,1,0:T(8,128)(2,1)S(1)}, u32[]{:S(2)}) copy-start(bf16[4,272,128]{2,1,0:T(8,128)(2,1)S(1)} %pad_maximum_fusion.2.refs_0_) | copy-start | bytes 835588
  12.1 21.0 %collective-permute-start.8 = (bf16[4,272,128]{2,1,0:T(8,128)(2,1)S(1)}, bf16[4,272,128]{2,1,0:T(8,128)(2,1)S(1)}, u32[]{:S(2)}, u32[]{:S(2)}) collective-permute-start(bf16[4,272,128]{2,1,0:T(8,128)(2,1)S(1)} %pad_maximum_fusion.2.refs_0_), channel_id=1, source_target_pairs={{0,24},{8,0},{16,8},{24,16},{1,25},{9,1},{17,9},{25,17},{2,26},{10... | collective-permute-start | bytes 835592 | tf_op jit(solution)/shard_map/ppermute | solution.py:21
  15.9 17.2 %collective-permute-start.7 = (bf16[4,272,128]{2,1,0:T(8,128)(2,1)S(1)}, bf16[4,272,128]{2,1,0:T(8,128)(2,1)S(1)}, u32[]{:S(2)}, u32[]{:S(2)}) collective-permute-start(bf16[4,272,128]{2,1,0:T(8,128)(2,1)S(1)} %pad_maximum_fusion.2.refs_0_), channel_id=1, source_target_pairs={{0,16},{8,24},{16,0},{24,8},{1,17},{9,25},{17,1},{25,9},{2,18},{10... | collective-permute-start | bytes 835592 | tf_op jit(solution)/shard_map/ppermute | solution.py:21
  15.9 17.3 %collective-permute-start.6 = (bf16[4,272,128]{2,1,0:T(8,128)(2,1)S(1)}, bf16[4,272,128]{2,1,0:T(8,128)(2,1)S(1)}, u32[]{:S(2)}, u32[]{:S(2)}) collective-permute-start(bf16[4,272,128]{2,1,0:T(8,128)(2,1)S(1)} %pad_maximum_fusion.2.refs_0_), channel_id=1, source_target_pairs={{0,8},{8,16},{16,24},{24,0},{1,9},{9,17},{17,25},{25,1},{2,10},{10... | collective-permute-start | bytes 835592 | tf_op jit(solution)/shard_map/ppermute | solution.py:21
  22.1 4.3 %collective-permute-start.11 = (bf16[16,64]{1,0:T(8,128)(2,1)S(1)}, bf16[16,64]{1,0:T(8,128)(2,1)S(1)}, u32[]{:S(2)}, u32[]{:S(2)}) collective-permute-start(bf16[16,64]{1,0:T(8,128)(2,1)S(1)} %maximum_select_fusion.1), channel_id=1, source_target_pairs={{0,4},{2,6},{4,0},{6,2},{1,5},{3,7},{5,1},{7,3},{8,12},{10,14},{12... | collective-permute-start | bytes 6152 | tf_op jit(solution)/shard_map/ppermute | solution.py:21
  23.6 4.0 %collective-permute-start.10 = (bf16[16,64]{1,0:T(8,128)(2,1)S(1)}, bf16[16,64]{1,0:T(8,128)(2,1)S(1)}, u32[]{:S(2)}, u32[]{:S(2)}) collective-permute-start(bf16[16,64]{1,0:T(8,128)(2,1)S(1)} %maximum_select_fusion.1), channel_id=1, source_target_pairs={{0,2},{2,4},{4,6},{6,0},{1,3},{3,5},{5,7},{7,1},{8,10},{10,12},{12... | collective-permute-start | bytes 6152 | tf_op jit(solution)/shard_map/ppermute | solution.py:21
  29.2 7.7 %collective-permute-start.13 = (bf16[4,272,128]{2,1,0:T(8,128)(2,1)S(1)}, bf16[4,272,128]{2,1,0:T(8,128)(2,1)S(1)}, u32[]{:S(2)}, u32[]{:S(2)}) collective-permute-start(bf16[4,272,128]{2,1,0:T(8,128)(2,1)S(1)} %pad_maximum_fusion.2.refs_0_), channel_id=1, source_target_pairs={{0,1},{1,0},{2,3},{3,2},{4,5},{5,4},{6,7},{7,6},{8,9},{9,8},{10,11... | collective-permute-start | bytes 835592 | tf_op jit(solution)/shard_map/ppermute | solution.py:344
  33.1 3.9 %copy-start.13 = (bf16[4,272,128]{2,1,0:T(8,128)(2,1)}, bf16[4,272,128]{2,1,0:T(8,128)(2,1)S(1)}, u32[]{:S(2)}) copy-start(bf16[4,272,128]{2,1,0:T(8,128)(2,1)S(1)} %collective-permute-done.8.refs_3_) | copy-start | bytes 835588
  33.1 3.9 %copy-start.14 = (bf16[4,272,128]{2,1,0:T(8,128)(2,1)}, bf16[4,272,128]{2,1,0:T(8,128)(2,1)S(1)}, u32[]{:S(2)}) copy-start(bf16[4,272,128]{2,1,0:T(8,128)(2,1)S(1)} %collective-permute-done.7.refs_2_) | copy-start | bytes 835588
  33.2 3.8 %copy-start.15 = (bf16[4,272,128]{2,1,0:T(8,128)(2,1)}, bf16[4,272,128]{2,1,0:T(8,128)(2,1)S(1)}, u32[]{:S(2)}) copy-start(bf16[4,272,128]{2,1,0:T(8,128)(2,1)S(1)} %collective-permute-done.6.refs_1_) | copy-start | bytes 835588
  33.2 3.7 collective-permute-start.14
  33.3 3.7 collective-permute-start.15
  33.8 3.2 collective-permute-start.16
  36.9 0.7 copy-start.16
  36.9 0.8 copy-start.17
  36.9 0.9 copy-start.18
  37.8 0.7 copy-start.19
  45.7 1.0 copy-start.7
  46.7 41.0 %all-to-all-start.1 = ((bf16[4,6,4,128,128]{4,3,2,1,0:T(8,128)(2,1)}), bf16[4,6,4,128,128]{4,3,2,1,0:T(8,128)(2,1)S(1)}, u32[]{:S(2)}, u32[]{:S(2)}) async-start(bf16[4,6,4,128,128]{4,3,2,1,0:T(8,128)(2,1)} %get-tuple-element.33), calls=%async_computation.1 | async-start | bytes 6291456 | tf_op jit(solution)/shard_map/all_to_all | solution.py:368
  87.6 1.6 copy-start.5
  93.9 63.3 %copy-start.8 = (bf16[4,2,4,128,128]{4,3,2,1,0:T(8,128)(2,1)S(1)}, bf16[4,2,4,128,128]{4,3,2,1,0:T(8,128)(2,1)}, u32[]{:S(2)}) copy-start(bf16[4,2,4,128,128]{4,3,2,1,0:T(8,128)(2,1)} %copy-done.7) | copy-start | bytes 3145732
  93.9 94.8 %all-to-all-start.2 = ((bf16[4,4,512,128]{3,2,1,0:T(8,128)(2,1)}), bf16[4,4,512,128]{3,2,1,0:T(8,128)(2,1)S(1)}, u32[]{:S(2)}, u32[]{:S(2)}) async-start(bf16[4,4,512,128]{3,2,1,0:T(8,128)(2,1)} %collect.2), calls=%async_computation.2 | async-start | bytes 4194304 | tf_op jit(solution)/shard_map/all_to_all | solution.py:381
  97.6 41.8 %collective-permute-start.17 = (bf16[6,4,128,128]{3,2,1,0:T(8,128)(2,1)}, bf16[6,4,128,128]{3,2,1,0:T(8,128)(2,1)}, u32[]{:S(2)}, u32[]{:S(2)}) collective-permute-start(bf16[6,4,128,128]{3,2,1,0:T(8,128)(2,1)} %get-tuple-element.38), channel_id=1, source_target_pairs={{0,32},{32,64},{64,96},{96,0},{1,33},{33,65},{65,97},{97,1},{2,34}... | collective-permute-start | bytes 2359304 | tf_op jit(solution)/shard_map/ppermute | solution.py:21
  99.1 57.5 %collective-permute-start.18 = (bf16[6,4,128,128]{3,2,1,0:T(8,128)(2,1)}, bf16[6,4,128,128]{3,2,1,0:T(8,128)(2,1)}, u32[]{:S(2)}, u32[]{:S(2)}) collective-permute-start(bf16[6,4,128,128]{3,2,1,0:T(8,128)(2,1)} %get-tuple-element.39), channel_id=1, source_target_pairs={{0,64},{32,96},{64,0},{96,32},{1,65},{33,97},{65,1},{97,33},{2,66}... | collective-permute-start | bytes 2359304 | tf_op jit(solution)/shard_map/ppermute | solution.py:21
  101.5 55.1 %collective-permute-start.19 = (bf16[6,4,128,128]{3,2,1,0:T(8,128)(2,1)}, bf16[6,4,128,128]{3,2,1,0:T(8,128)(2,1)}, u32[]{:S(2)}, u32[]{:S(2)}) collective-permute-start(bf16[6,4,128,128]{3,2,1,0:T(8,128)(2,1)} %get-tuple-element.40), channel_id=1, source_target_pairs={{0,96},{32,0},{64,32},{96,64},{1,97},{33,1},{65,33},{97,65},{2,98}... | collective-permute-start | bytes 2359304 | tf_op jit(solution)/shard_map/ppermute | solution.py:21
  162.7 13.3 %collective-permute-start.20 = (bf16[4,512,128]{2,1,0:T(8,128)(2,1)}, bf16[4,512,128]{2,1,0:T(8,128)(2,1)S(1)}, u32[]{:S(2)}, u32[]{:S(2)}) collective-permute-start(bf16[4,512,128]{2,1,0:T(8,128)(2,1)} %get-tuple-element.43), channel_id=1, source_target_pairs={{0,8},{8,16},{16,24},{24,0},{1,9},{9,17},{17,25},{25,1},{2,10},{10... | collective-permute-start | bytes 1572872 | tf_op jit(solution)/shard_map/ppermute | solution.py:21
  162.8 23.4 %collective-permute-start.21 = (bf16[4,512,128]{2,1,0:T(8,128)(2,1)}, bf16[4,512,128]{2,1,0:T(8,128)(2,1)S(1)}, u32[]{:S(2)}, u32[]{:S(2)}) collective-permute-start(bf16[4,512,128]{2,1,0:T(8,128)(2,1)} %get-tuple-element.44), channel_id=1, source_target_pairs={{0,16},{8,24},{16,0},{24,8},{1,17},{9,25},{17,1},{25,9},{2,18},{10... | collective-permute-start | bytes 1572872 | tf_op jit(solution)/shard_map/ppermute | solution.py:21
  164.9 23.7 %collective-permute-start.22 = (bf16[4,512,128]{2,1,0:T(8,128)(2,1)}, bf16[4,512,128]{2,1,0:T(8,128)(2,1)}, u32[]{:S(2)}, u32[]{:S(2)}) collective-permute-start(bf16[4,512,128]{2,1,0:T(8,128)(2,1)} %get-tuple-element.45), channel_id=1, source_target_pairs={{0,24},{8,0},{16,8},{24,16},{1,25},{9,1},{17,9},{25,17},{2,26},{10... | collective-permute-start | bytes 1572872 | tf_op jit(solution)/shard_map/ppermute | solution.py:21
  176.0 12.6 %copy-start.11 = (bf16[4,512,128]{2,1,0:T(8,128)(2,1)}, bf16[4,512,128]{2,1,0:T(8,128)(2,1)S(1)}, u32[]{:S(2)}) copy-start(bf16[4,512,128]{2,1,0:T(8,128)(2,1)S(1)} %collective-permute-done.20.refs_1_) | copy-start | bytes 1572868
  186.2 2.5 copy-start.12
  188.7 1.3 copy-start.6
  217.8 55.6 %all-to-all-start.4 = ((bf16[4,512,1024]{2,1,0:T(8,128)(2,1)}), bf16[4,512,1024]{2,1,0:T(8,128)(2,1)}, u32[]{:S(2)}, u32[]{:S(2)}) async-start(bf16[4,512,1024]{2,1,0:T(8,128)(2,1)} %broadcast_in_dim.26), calls=%async_computation.4 | async-start | bytes 8388608 | tf_op jit(solution)/shard_map/all_to_all | solution.py:396
  225.0 48.4 %copy-start.2 = (bf16[1024,512]{1,0:T(8,128)(2,1)}, bf16[1024,512]{1,0:T(8,128)(2,1)S(1)}, u32[]{:S(2)}) copy-start(bf16[1024,512]{1,0:T(8,128)(2,1)S(1)} %fusion.5.f0) | copy-start | bytes 3145732
  225.0 26.3 %collective-permute-start.23 = (bf16[1024,512]{1,0:T(8,128)(2,1)S(1)}, bf16[1024,512]{1,0:T(8,128)(2,1)S(1)}, u32[]{:S(2)}, u32[]{:S(2)}) collective-permute-start(bf16[1024,512]{1,0:T(8,128)(2,1)S(1)} %fusion.5.f0), channel_id=1, source_target_pairs={{0,32},{32,64},{64,96},{96,0},{1,33},{33,65},{65,97},{97,1},{2,34}... | collective-permute-start | bytes 3145736 | tf_op jit(solution)/shard_map/ppermute | solution.py:21
  225.1 46.1 %collective-permute-start.24 = (bf16[1024,512]{1,0:T(8,128)(2,1)S(1)}, bf16[1024,512]{1,0:T(8,128)(2,1)S(1)}, u32[]{:S(2)}, u32[]{:S(2)}) collective-permute-start(bf16[1024,512]{1,0:T(8,128)(2,1)S(1)} %fusion.5.f0), channel_id=1, source_target_pairs={{0,64},{32,96},{64,0},{96,32},{1,65},{33,97},{65,1},{97,33},{2,66}... | collective-permute-start | bytes 3145736 | tf_op jit(solution)/shard_map/ppermute | solution.py:21
  226.4 47.0 %collective-permute-start.25 = (bf16[1024,512]{1,0:T(8,128)(2,1)S(1)}, bf16[1024,512]{1,0:T(8,128)(2,1)}, u32[]{:S(2)}, u32[]{:S(2)}) collective-permute-start(bf16[1024,512]{1,0:T(8,128)(2,1)S(1)} %fusion.5.f0), channel_id=1, source_target_pairs={{0,96},{32,0},{64,32},{96,64},{1,97},{33,1},{65,33},{97,65},{2,98}... | collective-permute-start | bytes 3145736 | tf_op jit(solution)/shard_map/ppermute | solution.py:21
  251.3 22.1 %copy-start.3 = (bf16[1024,512]{1,0:T(8,128)(2,1)}, bf16[1024,512]{1,0:T(8,128)(2,1)S(1)}, u32[]{:S(2)}) copy-start(bf16[1024,512]{1,0:T(8,128)(2,1)S(1)} %collective-permute-done.23.f1) | copy-start | bytes 3145732
  271.2 2.2 copy-start.4
  280.4 9.2 %collective-permute-start.28 = (bf16[4,512,512]{2,1,0:T(8,128)(2,1)}, bf16[4,512,512]{2,1,0:T(8,128)(2,1)S(1)}, u32[]{:S(2)}, u32[]{:S(2)}) collective-permute-start(bf16[4,512,512]{2,1,0:T(8,128)(2,1)} %product.6), channel_id=1, source_target_pairs={{0,1},{1,0},{2,3},{3,2},{4,5},{5,4},{6,7},{7,6},{8,9},{9,8},{10,11... | collective-permute-start | bytes 6291464 | tf_op jit(solution)/shard_map/ppermute | solution.py:403
  289.7 12.9 %collective-permute-start.26 = (bf16[4,512,512]{2,1,0:T(8,128)(2,1)}, bf16[4,512,512]{2,1,0:T(8,128)(2,1)}, u32[]{:S(2)}, u32[]{:S(2)}) collective-permute-start(bf16[4,512,512]{2,1,0:T(8,128)(2,1)} %product.4), channel_id=1, source_target_pairs={{0,1},{1,0},{2,3},{3,2},{4,5},{5,4},{6,7},{7,6},{8,9},{9,8},{10,11... | collective-permute-start | bytes 6291464 | tf_op jit(solution)/shard_map/ppermute | solution.py:403
  289.7 1.3 copy-start.9
  298.7 29.5 %all-to-all-start.6 = ((bf16[4,512,512]{2,1,0:T(8,128)(2,1)}), bf16[4,512,512]{2,1,0:T(8,128)(2,1)S(1)}, u32[]{:S(2)}, u32[]{:S(2)}) async-start(bf16[4,512,512]{2,1,0:T(8,128)(2,1)} %product.7), calls=%async_computation.6 | async-start | bytes 4194304 | tf_op jit(solution)/shard_map/all_to_all | solution.py:407
  328.2 29.5 %all-to-all-start.5 = ((bf16[4,512,512]{2,1,0:T(8,128)(2,1)}), bf16[4,512,512]{2,1,0:T(8,128)(2,1)}, u32[]{:S(2)}, u32[]{:S(2)}) async-start(bf16[4,512,512]{2,1,0:T(8,128)(2,1)} %product.5), calls=%async_computation.5 | async-start | bytes 4194304 | tf_op jit(solution)/shard_map/all_to_all | solution.py:407
  333.3 33.6 %collective-permute-start.29 = (bf16[512,512]{1,0:T(8,128)(2,1)S(1)}, bf16[512,512]{1,0:T(8,128)(2,1)S(1)}, u32[]{:S(2)}, u32[]{:S(2)}) collective-permute-start(bf16[512,512]{1,0:T(8,128)(2,1)S(1)} %reduce_sum.45), channel_id=1, source_target_pairs={{0,8},{1,24},{8,0},{9,16},{16,9},{17,25},{24,1},{25,17},{2,10},{3,... | collective-permute-start | bytes 1572872 | tf_op jit(solution)/shard_map/ppermute | solution.py:412
  359.9 13.8 %collective-permute-start.27 = (bf16[512,512]{1,0:T(8,128)(2,1)S(1)}, bf16[512,512]{1,0:T(8,128)(2,1)S(1)}, u32[]{:S(2)}, u32[]{:S(2)}) collective-permute-start(bf16[512,512]{1,0:T(8,128)(2,1)S(1)} %reduce_sum.44), channel_id=1, source_target_pairs={{0,0},{1,16},{8,8},{9,24},{16,1},{17,17},{24,9},{25,25},{2,2},{3,1... | collective-permute-start | bytes 1572872 | tf_op jit(solution)/shard_map/ppermute | solution.py:412
  374.1 1.5 copy-start.1

commit v4 on v3

--- a/solution.py
+++ b/solution.py
@@ -14,15 +14,16 @@
 CHUNKS = 1
 BF = jnp.bfloat16
 F32 = jnp.float32
-VMEM = 60 * 1024 * 1024
+VMEM = 40 * 1024 * 1024
+MOST = 58 * 1024 * 1024
 
 
 def shifted(value, axis, shift):
     return lax.ppermute(value, axis, [(i, (i + shift) % SIDE) for i in range(SIDE)])
 
 
-def params():
-    return pltpu.CompilerParams(vmem_limit_bytes=VMEM)
+def params(limit=VMEM):
+    return pltpu.CompilerParams(vmem_limit_bytes=limit)
 
 
 def cost(flops, bytes_accessed):
@@ -44,8 +45,8 @@
         count[SIDE + to_x] = count[SIDE + to_x] + 1
         atom = nu[j] // 4
         half = (nu[j] % 4) // 2
-        out[4, j] = (z - atom % 4 + 4) % 4 + jnp.where(half == c, 0, SIDE)
-        out[5, j] = (x - atom // 4 + 4) % 4
+        out[4, j] = jnp.where(half == c, 0, 1)
+        out[5, j] = atom
         out[6, j] = (nu[j] % 2) * 128
 
 
@@ -62,10 +63,10 @@
 
 
 def transform_kernel(first, size, meta, live, tile_hbm, mask_ref, *refs):
-    orb_hbm = refs[:8]
-    a_main, a_extra, b_extra = refs[8:11]
-    b_main = refs[11:15]
-    tile, orb, result, tile_sem, orb_sem, a_sem, b_sem = refs[15:]
+    orb_hbm = refs[:2]
+    a_main, a_extra, b_extra = refs[2:5]
+    b_main = refs[5:9]
+    tile, orb, result, tile_sem, orb_sem, a_sem, b_sem = refs[9:]
 
     def tile_copies(j):
         return [
@@ -139,12 +140,13 @@
 def transform(first, size, meta, live, tiles, mask, orbitals):
     smem = pl.BlockSpec(memory_space=pltpu.SMEM)
     hbm = pl.BlockSpec(memory_space=pltpu.HBM)
+    anywhere = pl.BlockSpec(memory_space=pl.ANY)
     vmem = pl.BlockSpec(memory_space=pltpu.VMEM)
     sems = pltpu.SemaphoreType.DMA((16,))
     shapes = [(4, MAIN), (4, 8 - MAIN), (4, 8 - MAIN)] + [(MAIN,)] * 4
     return pl.pallas_call(
         functools.partial(transform_kernel, first, size),
-        in_specs=[smem, smem, hbm, vmem] + [hbm] * 8,
+        in_specs=[smem, smem, hbm, vmem] + [anywhere] * 2,
         out_specs=[hbm] * 7,
         out_shape=[jax.ShapeDtypeStruct(shape + (size, 128, 128), BF) for shape in shapes],
         scratch_shapes=[
@@ -156,7 +158,7 @@
             sems,
             sems,
         ],
-        compiler_params=params(),
+        compiler_params=params(MOST),
         cost_estimate=cost(2 * 16 * 2 * size * 128**3, 16 * 2 * size * 2**16),
         name="transform",
     )(meta, live, tiles, mask, *orbitals)
@@ -236,11 +238,12 @@
 def collect(along_x, size, codes, source, place, mine, main, extra):
     smem = pl.BlockSpec(memory_space=pltpu.SMEM)
     hbm = pl.BlockSpec(memory_space=pltpu.HBM)
+    anywhere = pl.BlockSpec(memory_space=pl.ANY)
     out = (size, 512, 128)
     shapes = [jax.ShapeDtypeStruct(out, BF)] * 4 if along_x else [jax.ShapeDtypeStruct((4,) + out, BF)]
     return pl.pallas_call(
         functools.partial(collect_kernel, along_x, size),
-        in_specs=[smem] * 4 + [hbm] * (len(main) + 1),
+        in_specs=[smem] * 4 + [anywhere] * (len(main) + 1),
         out_specs=[hbm] * len(shapes),
         out_shape=shapes,
         scratch_shapes=[
@@ -252,7 +255,7 @@
             pltpu.SemaphoreType.DMA((SIDE, 8)),
             pltpu.SemaphoreType.DMA((SIDE,)),
         ],
-        compiler_params=params(),
+        compiler_params=params(MOST),
         cost_estimate=cost(2**22, size * 3 * 2**19),
         name="collect",
     )(codes, source, place, mine, *main, extra)
@@ -339,19 +342,20 @@
     code_rows = jnp.broadcast_to(jnp.pad(code, (0, 112))[None], (16, 128))
     sent = jnp.concatenate([half_blocks, code_rows], 0)
     swap = [(0, 1), (1, 0)]
-    line = jnp.stack([sent] + [shifted(sent, "x", s) for s in (1, 2, 3)])
-    halves = [line] + [shifted(line, "z", s) for s in (1, 2, 3)]
-    orbitals = halves + [lax.ppermute(half, "c", swap) for half in halves]
-    codes = jnp.concatenate([half[:, 256, :slots] for half in halves], 0).astype(jnp.int32)
+    own = lax.all_to_all(
+        jnp.broadcast_to(sent[None], (16, 272, 128)), ("x", "z"), 0, 0, tiled=True
+    )
 
     where = jnp.stack([x, z, c]).astype(jnp.int32)
     meta = plan(where, pair_owner, pair_nu)
     mask = jnp.repeat(jnp.repeat(pair_mask, 16, 1), 16, 2).astype(BF)
-    mask, fit, meta = lax.optimization_barrier((mask, fit, meta))
+    own, mask, fit, meta = lax.optimization_barrier((own, mask, fit, meta))
+    orbitals = [own, lax.ppermute(own, "c", swap)]
+    codes = own[:, 256, :slots].astype(jnp.int32)
 
     steps = jnp.arange(4, dtype=jnp.int32)
     to_x, to_z = codes // 16, codes // 4 % 4
-    from_x, from_z = jnp.tile((x - steps) % 4, 4), jnp.repeat((z - steps) % 4, 4)
+    from_x, from_z = jnp.repeat(steps, 4), jnp.tile(steps, 4)
 
     def lengths(to, origin):
         hits = (codes[..., None] >= 0) & (to[..., None] == steps) & (to != origin[:, None])[..., None]
@@ -367,6 +371,7 @@
         )
         a_got = lax.all_to_all(a_main, "z", 0, 0, tiled=True)
         b_got = [b_main[0]] + [shifted(b_main[s], "x", s) for s in (1, 2, 3)]
+        a_got, *b_got = lax.optimization_barrier((a_got, *b_got))
 
         def send_extra(a, b):
             moved = [b[:1]] + [shifted(b[s : s + 1], "x", s) for s in (1, 2, 3)]
@@ -376,10 +381,12 @@
             overflow, send_extra, lambda a, b: (a, b), a_extra, b_extra
         )
         (a_sum,) = collect(
-            False, size, codes, (z - steps) % 4 * 4, steps, z[None], [a_got], a_extra
+            False, size, codes, x * 4 + steps, steps, z[None], [a_got], a_extra
         )
         a_last = lax.all_to_all(a_sum, "x", 0, 0, tiled=True)
-        b_sum = collect(True, size, codes, steps, (steps - z) % 4, x[None], b_got, b_extra)
+        b_sum = collect(
+            True, size, codes, (x - steps) % 4 * 4 + z, (steps - z) % 4, x[None], b_got, b_extra
+        )
         b_last = [b_sum[0]] + [shifted(b_sum[s], "z", s) for s in (1, 2, 3)]
         cut = finish(size, a_last, b_last)
         return lax.all_to_all(cut, ("y", "c"), 0, 0, tiled=True).reshape(-1, 512)

time: 377 us -> 311 us (0.82)
  waiting for transfers between devices: 207 us -> 151 us
  Pallas kernels: 52.9 us -> 43.9 us
    all_to_all x1, waiting for transfers between devices: 36 us -> 0.01 us  [route(): a_got = lax.all_to_all(a_main, 'z', 0, 0, tiled=True)]
    ppermute x18 -> x12, waiting for transfers between devices: 125 us -> 102 us  [shifted(): lax.ppermute(value, axis, [(i, (i + shift) % SIDE) for i in range(SIDE)])]
    all_to_all x0 -> x1, starting transfers between devices: none -> 8.43 us  [per_device(): lax.all_to_all(jnp.broadcast_to(sent[None], (16, 272, 128)), ('x', 'z'),...]
    ppermute x18 -> x12, starting transfers between devices: 24.7 us -> 16.3 us  [shifted(): lax.ppermute(value, axis, [(i, (i + shift) % SIDE) for i in range(SIDE)])]
    pallas_call x4, Pallas kernels: 29.4 us -> 23 us  [product(): pl.pallas_call(functools.partial(product_kernel, add is not None), grid_s...]
    unnamed x47 -> x31, local copies, waits for them, and re-layouts: 7.62 us -> 8.31 us
  transfers between devices with their start and end apart: 32 -> 24, of which waited for: 15 -> 13; matrix products, arithmetic and copies ran while one was open for 4% -> 4% of each run, Pallas kernels for 8% -> 8%
where the time goes in v4:
time: 311 us; the launch traced here: 309 us
  waiting for transfers between devices  151 us (49%)
  starting transfers between devices  62.5 us (20%)
  Pallas kernels  43.9 us (14%)
  blocking collectives  21.3 us (7%)
  local copies, waits for them, and re-layouts  15.9 us (5%)
  other arithmetic  10.4 us (3%)
    ppermute x12, waiting for transfers between devices, shifted(): lax.ppermute(value, axis, [(i, (i + shift) % SIDE) for i in range(SIDE)])  102 us
    all_to_all x2, waiting for transfers between devices, per_device(): parts = lax.all_to_all(partial, 'y', 0, 0, tiled=True)  37.9 us
    pallas_call x4, Pallas kernels, product(): pl.pallas_call(functools.partial(product_kernel, add is not None), grid_s...  23 us
    all_to_all x1, blocking collectives, route(): return lax.all_to_all(cut, ('y', 'c'), 0, 0, tiled=True).reshape(-1, 512)  21.3 us
    ppermute x12, starting transfers between devices, shifted(): lax.ppermute(value, axis, [(i, (i + shift) % SIDE) for i in range(SIDE)])  16.3 us
    ppermute x2, starting transfers between devices, per_device(): got.append(lax.ppermute(tile, ('z', 'c'), pairs).astype(F32))  10.9 us
    pallas_call x2, Pallas kernels, collect(): pl.pallas_call(functools.partial(collect_kernel, along_x, size), in_specs...  10.8 us
    all_to_all x1, starting transfers between devices, per_device(): lax.all_to_all(jnp.broadcast_to(sent[None], (16, 272, 128)), ('x', 'z'),...  8.43 us
  transfers between devices with their start and end apart: 24, of which 13 were waited for; matrix products, arithmetic and copies ran while one was open for 4% of the time, Pallas kernels for 8%

profile of v4, /device:TPU:1, one launch (start us, length us, event | category | flops | bytes accessed | tf_op | source)
XLA Modules:
  0.0 309.5 jit_solution(16337192945231351680)
XLA Ops:
  0.7 0.7 fusion.32
  1.5 1.1 broadcast_in_dim.21
  2.6 8.4 %all-to-all-start.1 = ((bf16[16,272,128]{2,1,0:T(8,128)(2,1)}), bf16[16,272,128]{2,1,0:T(8,128)(2,1)S(1)}, u32[]{:S(2)}, u32[]{:S(2)}) async-start(bf16[16,272,128]{2,1,0:T(8,128)(2,1)} %broadcast_in_dim.21), calls=%async_computation.1 | async-start | bytes 2228224 | tf_op jit(solution)/shard_map/all_to_all | solution.py:345
  11.0 1.0 collective-permute-start.3
  12.1 0.6 pad_add_fusion.where
  12.7 0.7 copy.26.owner
  13.9 1.8 plan.1.meta
  15.7 2.8 collective-permute-start.6
  18.9 0.7 collective-permute-start.4
  19.6 3.2 %collective-permute-done.5 = bf16[16,64]{1,0:T(8,128)(2,1)S(1)} collective-permute-done((bf16[16,64]{1,0:T(8,128)(2,1)S(1)}, bf16[16,64]{1,0:T(8,128)(2,1)S(1)}, u32[]{:S(2)}, u32[]{:S(2)}) %collective-permute-start.5) | collective-permute-done | bytes 2080 | tf_op jit(solution)/shard_map/ppermute | solution.py:22
  22.9 0.6 gather_fusion
  23.4 3.7 %all-to-all-done.1.refs_0_ = bf16[16,272,128]{2,1,0:T(8,128)(2,1)S(1)} async-done(((bf16[16,272,128]{2,1,0:T(8,128)(2,1)}), bf16[16,272,128]{2,1,0:T(8,128)(2,1)S(1)}, u32[]{:S(2)}, u32[]{:S(2)}) %all-to-all-start.1) | async-done | bytes 1114144 | tf_op jit(solution)/shard_map/all_to_all | solution.py:345
  27.2 3.5 %collective-permute-start.7 = (bf16[16,272,128]{2,1,0:T(8,128)(2,1)S(1)}, bf16[16,272,128]{2,1,0:T(8,128)(2,1)}, u32[]{:S(2)}, u32[]{:S(2)}) collective-permute-start(bf16[16,272,128]{2,1,0:T(8,128)(2,1)S(1)} %all-to-all-done.1.refs_0_), channel_id=1, source_target_pairs={{0,1},{1,0},{2,3},{3,2},{4,5},{5,4},{6,7},{7,6},{8,9},{9,8},{10,11... | collective-permute-start | bytes 3342344 | tf_op jit(solution)/shard_map/ppermute | solution.py:353
  31.1 1.2 copy.28.mask_ref
  32.6 0.6 reduce_max.18
  33.3 0.6 reduce_max.19
  35.1 7.0 %transform.1 = (bf16[4,6,4,128,128]{4,3,2,1,0:T(8,128)(2,1)}, bf16[4,2,4,128,128]{4,3,2,1,0:T(8,128)(2,1)}, bf16[4,2,4,128,128]{4,3,2,1,0:T(8,128)(2,1)S(1)}, bf...) custom-call(s32[7,16]{1,0:T(8,128)} %plan.1.meta, ...), custom_call_target="tpu_custom_call" | custom-call | flops 536870912 | bytes 8388608 | tf_op jit(solution)/shard_map/transform/pallas_call | solution.py:147
  42.2 1.0 copy-done.9
  43.2 3.7 %all-to-all-start.2 = ((bf16[4,6,4,128,128]{4,3,2,1,0:T(8,128)(2,1)}), bf16[4,6,4,128,128]{4,3,2,1,0:T(8,128)(2,1)S(1)}, u32[]{:S(2)}, u32[]{:S(2)}) async-start(bf16[4,6,4,128,128]{4,3,2,1,0:T(8,128)(2,1)} %get-tuple-element.40), calls=%async_computation.2 | async-start | bytes 6291456 | tf_op jit(solution)/shard_map/all_to_all | solution.py:372
  47.2 2.5 collective-permute-start.10
  49.7 0.5 iota_add_fusion.source
  50.2 1.3 fusion.31.codes
  51.5 33.1 %collective-permute-done.8.refs_1_ = bf16[6,4,128,128]{3,2,1,0:T(8,128)(2,1)} collective-permute-done((bf16[6,4,128,128]{3,2,1,0:T(8,128)(2,1)}, bf16[6,4,128,128]{3,2,1,0:T(8,128)(2,1)}, u32[]{:S(2)}, u32[]{:S(2)}) %collective-permute-start.8) | collective-permute-done | bytes 786464 | tf_op jit(solution)/shard_map/ppermute | solution.py:22
  84.8 0.6 iota.50.place
  85.4 1.1 copy-done.7
  86.5 5.3 %collect.2 = bf16[4,4,512,128]{3,2,1,0:T(8,128)(2,1)} custom-call(s32[16,16]{1,0:T(8,128)} %fusion.31.codes, s32[4]{0:T(128)} %iota_add_fusion.source, s32[4]{0:T(128)} %iota.50.place, s32[1]{0:T(128)} %bitcast.12.mine, bf16[4,6,4,128,128]{4,3,2,1,0:T(8,128)(2,1)} %copy-done.7, bf16[4,2,4,128,128]{4,3,2,1,0:T(8,128)(2,1)} %get-tuple-element.48.refs_1_), custom_call_target="tpu_custom_call" | custom-call | flops 4194304 | bytes 6291456 | tf_op jit(solution)/shard_map/collect/pallas_call | solution.py:244
  91.8 3.8 %all-to-all-start.3 = ((bf16[4,4,512,128]{3,2,1,0:T(8,128)(2,1)}), bf16[4,4,512,128]{3,2,1,0:T(8,128)(2,1)S(1)}, u32[]{:S(2)}, u32[]{:S(2)}) async-start(bf16[4,4,512,128]{3,2,1,0:T(8,128)(2,1)} %collect.2), calls=%async_computation.3 | async-start | bytes 4194304 | tf_op jit(solution)/shard_map/all_to_all | solution.py:386
  95.5 0.5 and_select_fusion
  96.1 5.5 %collect.3 = (bf16[4,512,128]{2,1,0:T(8,128)(2,1)}, bf16[4,512,128]{2,1,0:T(8,128)(2,1)}, bf16[4,512,128]{2,1,0:T(8,128)(2,1)}, bf16[4,512,128]{2,1,0:T(8,128)(2,1)}) custom-call(s32[16,16]{1,0:T(8,128)} %fusion.31.codes, s32[4]{0:T(128)} %get-tuple-element.75.source, s32[4]{0:T(128)} %get-tuple-element.74.place, s32[1]{0:T(128)} %bitcast.11.mine, ...), custom_call_target="tpu_custom_call" | custom-call | flops 4194304 | bytes 6291456 | tf_op jit(solution)/shard_map/collect/pallas_call | solution.py:244
  101.6 1.4 collective-permute-start.11
  103.0 2.5 collective-permute-start.12
  105.5 1.1 collective-permute-start.13
  106.6 8.7 %collective-permute-done.11.refs_1_ = bf16[4,512,128]{2,1,0:T(8,128)(2,1)S(1)} collective-permute-done((bf16[4,512,128]{2,1,0:T(8,128)(2,1)}, bf16[4,512,128]{2,1,0:T(8,128)(2,1)S(1)}, u32[]{:S(2)}, u32[]{:S(2)}) %collective-permute-start.11) | collective-permute-done | bytes 524320 | tf_op jit(solution)/shard_map/ppermute | solution.py:22
  115.3 12.1 %collective-permute-done.12.refs_2_ = bf16[4,512,128]{2,1,0:T(8,128)(2,1)S(1)} collective-permute-done((bf16[4,512,128]{2,1,0:T(8,128)(2,1)}, bf16[4,512,128]{2,1,0:T(8,128)(2,1)S(1)}, u32[]{:S(2)}, u32[]{:S(2)}) %collective-permute-start.12) | collective-permute-done | bytes 524320 | tf_op jit(solution)/shard_map/ppermute | solution.py:22
  127.9 0.8 copy-done.5
  128.7 1.0 copy-done.4
  129.7 1.0 copy-done.6
  130.7 1.3 finish.1
  132.0 21.3 %all_to_all.39 = bf16[8,8,16,512]{3,2,1,0:T(8,128)(2,1)S(1)} all-to-all(bf16[8,8,16,512]{3,2,1,0:T(8,128)(2,1)S(1)} %finish.1), channel_id=1, replica_groups=mesh['x'=4,'z'=4,'y'=4,'c'=2] {'y','c'}, dimensions={0} | all-to-all | bytes 2097152 | tf_op jit(solution)/shard_map/all_to_all | solution.py:392
  153.3 0.5 copy.29
  153.8 2.6 broadcast_in_dim.25
  156.4 4.9 %all-to-all-start.5 = ((bf16[4,512,1024]{2,1,0:T(8,128)(2,1)}), bf16[4,512,1024]{2,1,0:T(8,128)(2,1)}, u32[]{:S(2)}, u32[]{:S(2)}) async-start(bf16[4,512,1024]{2,1,0:T(8,128)(2,1)} %broadcast_in_dim.25), calls=%async_computation.5 | async-start | bytes 8388608 | tf_op jit(solution)/shard_map/all_to_all | solution.py:403
  161.7 2.0 fusion.5.f0
  163.7 1.7 collective-permute-start.14
  165.4 2.7 collective-permute-start.15
  168.3 21.0 %collective-permute-done.14.f1 = bf16[1024,512]{1,0:T(8,128)(2,1)S(1)} collective-permute-done((bf16[1024,512]{1,0:T(8,128)(2,1)S(1)}, bf16[1024,512]{1,0:T(8,128)(2,1)S(1)}, u32[]{:S(2)}, u32[]{:S(2)}) %collective-permute-start.14) | collective-permute-done | bytes 1048608 | tf_op jit(solution)/shard_map/ppermute | solution.py:22
  189.3 23.3 %collective-permute-done.15.f2 = bf16[1024,512]{1,0:T(8,128)(2,1)S(1)} collective-permute-done((bf16[1024,512]{1,0:T(8,128)(2,1)S(1)}, bf16[1024,512]{1,0:T(8,128)(2,1)S(1)}, u32[]{:S(2)}, u32[]{:S(2)}) %collective-permute-start.15) | collective-permute-done | bytes 1048608 | tf_op jit(solution)/shard_map/ppermute | solution.py:22
  212.6 5.9 %product.6 = bf16[4,512,512]{2,1,0:T(8,128)(2,1)} custom-call(s32[1]{0:T(128)} %bitcast.20.zsel, s32[4]{0:T(128)S(1)} %and_select_fusion.2.psel, bf16[4,512,1024]{2,1,0:T(8,128)(2,1)} %all-to-all-done.5.left_ref, bf16[1024,512]{1,0:T(8,128)(2,1)S(1)} %fusion.5.f0, bf16[1024,512]{1,0:T(8,128)(2,1)S(1)} %collective-permute-done.14.f1, ...), custom_call_target="tpu_custom_call" | custom-call | flops 2147483648 | bytes 7340032 | tf_op jit(solution)/shard_map/product/pallas_call | solution.py:314
  218.5 2.0 collective-permute-start.19
  220.5 5.9 %product.4 = bf16[4,512,512]{2,1,0:T(8,128)(2,1)} custom-call(s32[1]{0:T(128)} %bitcast.18.zsel, s32[4]{0:T(128)S(1)} %and_select_fusion.2.psel, bf16[4,512,1024]{2,1,0:T(8,128)(2,1)} %all-to-all-done.5.left_ref, bf16[1024,512]{1,0:T(8,128)(2,1)S(1)} %fusion.5.f0, bf16[1024,512]{1,0:T(8,128)(2,1)S(1)} %collective-permute-done.14.f1, ...), custom_call_target="tpu_custom_call" | custom-call | flops 2147483648 | bytes 7340032 | tf_op jit(solution)/shard_map/product/pallas_call | solution.py:314
  226.5 5.6 %product.7 = bf16[4,512,512]{2,1,0:T(8,128)(2,1)S(1)} custom-call(s32[1]{0:T(128)} %bitcast.19.zsel, s32[4]{0:T(128)S(1)} %and_select_fusion.2.psel, bf16[4,512,1024]{2,1,0:T(8,128)(2,1)} %all-to-all-done.5.left_ref, bf16[1024,512]{1,0:T(8,128)(2,1)S(1)} %fusion.5.f0, bf16[1024,512]{1,0:T(8,128)(2,1)S(1)} %collective-permute-done.14.f1, ...), custom_call_target="tpu_custom_call" | custom-call | flops 2147483648 | bytes 7340032 | tf_op jit(solution)/shard_map/product/pallas_call | solution.py:314
  232.1 1.3 copy-done.3
  233.4 4.5 %all-to-all-start.7 = ((bf16[4,512,512]{2,1,0:T(8,128)(2,1)}), bf16[4,512,512]{2,1,0:T(8,128)(2,1)}, u32[]{:S(2)}, u32[]{:S(2)}) async-start(bf16[4,512,512]{2,1,0:T(8,128)(2,1)} %copy-done.3), calls=%async_computation.7 | async-start | bytes 4194304 | tf_op jit(solution)/shard_map/all_to_all | solution.py:414
  237.9 5.6 %product.5 = bf16[4,512,512]{2,1,0:T(8,128)(2,1)S(1)} custom-call(s32[1]{0:T(128)} %bitcast.zsel, s32[4]{0:T(128)S(1)} %and_select_fusion.2.psel, bf16[4,512,1024]{2,1,0:T(8,128)(2,1)} %all-to-all-done.5.left_ref, bf16[1024,512]{1,0:T(8,128)(2,1)S(1)} %fusion.5.f0, bf16[1024,512]{1,0:T(8,128)(2,1)S(1)} %collective-permute-done.14.f1, ...), custom_call_target="tpu_custom_call" | custom-call | flops 2147483648 | bytes 7340032 | tf_op jit(solution)/shard_map/product/pallas_call | solution.py:314
  243.5 1.3 copy-done.2
  244.8 19.0 %all-to-all-done.7 = bf16[4,512,512]{2,1,0:T(8,128)(2,1)} async-done(((bf16[4,512,512]{2,1,0:T(8,128)(2,1)}), bf16[4,512,512]{2,1,0:T(8,128)(2,1)}, u32[]{:S(2)}, u32[]{:S(2)}) %all-to-all-start.7) | async-done | bytes 2097184 | tf_op jit(solution)/shard_map/all_to_all | solution.py:414
  263.8 3.6 %all-to-all-start.6 = ((bf16[4,512,512]{2,1,0:T(8,128)(2,1)}), bf16[4,512,512]{2,1,0:T(8,128)(2,1)S(1)}, u32[]{:S(2)}, u32[]{:S(2)}) async-start(bf16[4,512,512]{2,1,0:T(8,128)(2,1)} %copy-done.2), calls=%async_computation.6 | async-start | bytes 4194304 | tf_op jit(solution)/shard_map/all_to_all | solution.py:414
  267.5 2.2 reduce_sum.45
  269.6 3.9 %collective-permute-start.20 = (bf16[512,512]{1,0:T(8,128)(2,1)S(1)}, bf16[512,512]{1,0:T(8,128)(2,1)S(1)}, u32[]{:S(2)}, u32[]{:S(2)}) collective-permute-start(bf16[512,512]{1,0:T(8,128)(2,1)S(1)} %reduce_sum.45), channel_id=1, source_target_pairs={{0,8},{1,24},{8,0},{9,16},{16,9},{17,25},{24,1},{25,17},{2,10},{3,... | collective-permute-start | bytes 1572872 | tf_op jit(solution)/shard_map/ppermute | solution.py:419
  273.6 18.8 %all-to-all-done.6 = bf16[4,512,512]{2,1,0:T(8,128)(2,1)S(1)} async-done(((bf16[4,512,512]{2,1,0:T(8,128)(2,1)}), bf16[4,512,512]{2,1,0:T(8,128)(2,1)S(1)}, u32[]{:S(2)}, u32[]{:S(2)}) %all-to-all-start.6) | async-done | bytes 2097184 | tf_op jit(solution)/shard_map/all_to_all | solution.py:414
  292.4 1.2 reduce_sum.44
  293.7 7.0 %collective-permute-start.18 = (bf16[512,512]{1,0:T(8,128)(2,1)}, bf16[512,512]{1,0:T(8,128)(2,1)S(1)}, u32[]{:S(2)}, u32[]{:S(2)}) collective-permute-start(bf16[512,512]{1,0:T(8,128)(2,1)} %reduce_sum.44), channel_id=1, source_target_pairs={{0,0},{1,16},{8,8},{9,24},{16,1},{17,17},{24,9},{25,25},{2,2},{3,1... | collective-permute-start | bytes 1572872 | tf_op jit(solution)/shard_map/ppermute | solution.py:419
  300.7 7.0 %collective-permute-done.18 = bf16[512,512]{1,0:T(8,128)(2,1)S(1)} collective-permute-done((bf16[512,512]{1,0:T(8,128)(2,1)}, bf16[512,512]{1,0:T(8,128)(2,1)S(1)}, u32[]{:S(2)}, u32[]{:S(2)}) %collective-permute-start.18) | collective-permute-done | bytes 524320 | tf_op jit(solution)/shard_map/ppermute | solution.py:419
  308.0 1.5 pad_maximum_fusion.1
  (69 shorter events, 3.9 us)
Async XLA Ops:
  0.0 1.4 copy-start
  0.0 12.7 %copy-start.14 = (s32[16,1]{0,1:T(1,128)S(1)}, s32[16,1]{0,1:T(1,128)}, u32[]{:S(2)}) copy-start(s32[16,1]{0,1:T(1,128)} %param.12) | copy-start | bytes 196
  0.0 11.0 %copy-start.13 = (bf16[8,64]{1,0:T(8,128)(2,1)S(1)}, bf16[8,64]{1,0:T(8,128)(2,1)}, u32[]{:S(2)}) copy-start(bf16[8,64]{1,0:T(8,128)(2,1)} %param.17) | copy-start | bytes 3076
  0.0 13.4 %copy-start.12 = (s32[16,8,8]{0,2,1:T(8,128)S(1)}, s32[16,8,8]{0,2,1:T(8,128)}, u32[]{:S(2)}) copy-start(s32[16,8,8]{0,2,1:T(8,128)} %param.11) | copy-start | bytes 12292
  2.6 24.5 %all-to-all-start.1 = ((bf16[16,272,128]{2,1,0:T(8,128)(2,1)}), bf16[16,272,128]{2,1,0:T(8,128)(2,1)S(1)}, u32[]{:S(2)}, u32[]{:S(2)}) async-start(bf16[16,272,128]{2,1,0:T(8,128)(2,1)} %broadcast_in_dim.21), calls=%async_computation.1 | async-start | bytes 2228224 | tf_op jit(solution)/shard_map/all_to_all | solution.py:345
  11.0 4.7 %collective-permute-start.3 = (bf16[8,64]{1,0:T(8,128)(2,1)S(1)}, bf16[8,64]{1,0:T(8,128)(2,1)S(1)}, u32[]{:S(2)}, u32[]{:S(2)}) collective-permute-start(bf16[8,64]{1,0:T(8,128)(2,1)S(1)} %copy-done.13), channel_id=1, source_target_pairs={{0,1},{1,0},{2,3},{3,2},{4,5},{5,4},{6,7},{7,6},{8,9},{9,8},{10,11... | collective-permute-start | bytes 3080 | tf_op jit(solution)/shard_map/ppermute | solution.py:330
  15.7 3.9 %collective-permute-start.6 = (bf16[16,64]{1,0:T(8,128)(2,1)S(1)}, bf16[16,64]{1,0:T(8,128)(2,1)S(1)}, u32[]{:S(2)}, u32[]{:S(2)}) collective-permute-start(bf16[16,64]{1,0:T(8,128)(2,1)S(1)} %maximum_select_fusion.1), channel_id=1, source_target_pairs={{0,6},{2,0},{4,2},{6,4},{1,7},{3,1},{5,3},{7,5},{8,14},{10,8},{12,... | collective-permute-start | bytes 6152 | tf_op jit(solution)/shard_map/ppermute | solution.py:22
  18.5 4.3 %collective-permute-start.5 = (bf16[16,64]{1,0:T(8,128)(2,1)S(1)}, bf16[16,64]{1,0:T(8,128)(2,1)S(1)}, u32[]{:S(2)}, u32[]{:S(2)}) collective-permute-start(bf16[16,64]{1,0:T(8,128)(2,1)S(1)} %maximum_select_fusion.1), channel_id=1, source_target_pairs={{0,4},{2,6},{4,0},{6,2},{1,5},{3,7},{5,1},{7,3},{8,12},{10,14},{12... | collective-permute-start | bytes 6152 | tf_op jit(solution)/shard_map/ppermute | solution.py:22
  18.9 4.0 %collective-permute-start.4 = (bf16[16,64]{1,0:T(8,128)(2,1)S(1)}, bf16[16,64]{1,0:T(8,128)(2,1)S(1)}, u32[]{:S(2)}, u32[]{:S(2)}) collective-permute-start(bf16[16,64]{1,0:T(8,128)(2,1)S(1)} %maximum_select_fusion.1), channel_id=1, source_target_pairs={{0,2},{2,4},{4,6},{6,0},{1,3},{3,5},{5,7},{7,1},{8,10},{10,12},{12... | collective-permute-start | bytes 6152 | tf_op jit(solution)/shard_map/ppermute | solution.py:22
  27.1 8.0 %copy-start.8 = (bf16[16,272,128]{2,1,0:T(8,128)(2,1)}, bf16[16,272,128]{2,1,0:T(8,128)(2,1)S(1)}, u32[]{:S(2)}) copy-start(bf16[16,272,128]{2,1,0:T(8,128)(2,1)S(1)} %all-to-all-done.1.refs_0_) | copy-start | bytes 3342340
  27.2 7.9 %collective-permute-start.7 = (bf16[16,272,128]{2,1,0:T(8,128)(2,1)S(1)}, bf16[16,272,128]{2,1,0:T(8,128)(2,1)}, u32[]{:S(2)}, u32[]{:S(2)}) collective-permute-start(bf16[16,272,128]{2,1,0:T(8,128)(2,1)S(1)} %all-to-all-done.1.refs_0_), channel_id=1, source_target_pairs={{0,1},{1,0},{2,3},{3,2},{4,5},{5,4},{6,7},{7,6},{8,9},{9,8},{10,11... | collective-permute-start | bytes 3342344 | tf_op jit(solution)/shard_map/ppermute | solution.py:353
  31.1 4.0 %copy-start.11 = (bf16[16,272,128]{2,0,1:T(8,128)(2,1)}, bf16[16,272,128]{2,0,1:T(8,128)(2,1)S(1)}, u32[]{:S(2)}) copy-start(bf16[16,272,128]{2,0,1:T(8,128)(2,1)S(1)} %copy.27) | copy-start | bytes 3342340
  42.2 1.0 copy-start.9
  43.2 41.6 %all-to-all-start.2 = ((bf16[4,6,4,128,128]{4,3,2,1,0:T(8,128)(2,1)}), bf16[4,6,4,128,128]{4,3,2,1,0:T(8,128)(2,1)S(1)}, u32[]{:S(2)}, u32[]{:S(2)}) async-start(bf16[4,6,4,128,128]{4,3,2,1,0:T(8,128)(2,1)} %get-tuple-element.40), calls=%async_computation.2 | async-start | bytes 6291456 | tf_op jit(solution)/shard_map/all_to_all | solution.py:372
  46.9 37.6 %collective-permute-start.8 = (bf16[6,4,128,128]{3,2,1,0:T(8,128)(2,1)}, bf16[6,4,128,128]{3,2,1,0:T(8,128)(2,1)}, u32[]{:S(2)}, u32[]{:S(2)}) collective-permute-start(bf16[6,4,128,128]{3,2,1,0:T(8,128)(2,1)} %get-tuple-element.42), channel_id=1, source_target_pairs={{0,32},{32,64},{64,96},{96,0},{1,33},{33,65},{65,97},{97,1},{2,34}... | collective-permute-start | bytes 2359304 | tf_op jit(solution)/shard_map/ppermute | solution.py:22
  47.0 37.5 %collective-permute-start.9 = (bf16[6,4,128,128]{3,2,1,0:T(8,128)(2,1)}, bf16[6,4,128,128]{3,2,1,0:T(8,128)(2,1)}, u32[]{:S(2)}, u32[]{:S(2)}) collective-permute-start(bf16[6,4,128,128]{3,2,1,0:T(8,128)(2,1)} %get-tuple-element.43), channel_id=1, source_target_pairs={{0,64},{32,96},{64,0},{96,32},{1,65},{33,97},{65,1},{97,33},{2,66}... | collective-permute-start | bytes 2359304 | tf_op jit(solution)/shard_map/ppermute | solution.py:22
  47.2 37.6 %collective-permute-start.10 = (bf16[6,4,128,128]{3,2,1,0:T(8,128)(2,1)}, bf16[6,4,128,128]{3,2,1,0:T(8,128)(2,1)}, u32[]{:S(2)}, u32[]{:S(2)}) collective-permute-start(bf16[6,4,128,128]{3,2,1,0:T(8,128)(2,1)} %get-tuple-element.44), channel_id=1, source_target_pairs={{0,96},{32,0},{64,32},{96,64},{1,97},{33,1},{65,33},{97,65},{2,98}... | collective-permute-start | bytes 2359304 | tf_op jit(solution)/shard_map/ppermute | solution.py:22
  84.8 1.6 copy-start.7
  91.8 4.3 %copy-start.10 = (bf16[4,2,4,128,128]{4,3,2,1,0:T(8,128)(2,1)S(1)}, bf16[4,2,4,128,128]{4,3,2,1,0:T(8,128)(2,1)}, u32[]{:S(2)}) copy-start(bf16[4,2,4,128,128]{4,3,2,1,0:T(8,128)(2,1)} %copy-done.9) | copy-start | bytes 3145732
  91.8 36.9 %all-to-all-start.3 = ((bf16[4,4,512,128]{3,2,1,0:T(8,128)(2,1)}), bf16[4,4,512,128]{3,2,1,0:T(8,128)(2,1)S(1)}, u32[]{:S(2)}, u32[]{:S(2)}) async-start(bf16[4,4,512,128]{3,2,1,0:T(8,128)(2,1)} %collect.2), calls=%async_computation.3 | async-start | bytes 4194304 | tf_op jit(solution)/shard_map/all_to_all | solution.py:386
  101.6 13.8 %collective-permute-start.11 = (bf16[4,512,128]{2,1,0:T(8,128)(2,1)}, bf16[4,512,128]{2,1,0:T(8,128)(2,1)S(1)}, u32[]{:S(2)}, u32[]{:S(2)}) collective-permute-start(bf16[4,512,128]{2,1,0:T(8,128)(2,1)} %get-tuple-element.55), channel_id=1, source_target_pairs={{0,8},{8,16},{16,24},{24,0},{1,9},{9,17},{17,25},{25,1},{2,10},{10... | collective-permute-start | bytes 1572872 | tf_op jit(solution)/shard_map/ppermute | solution.py:22
  103.0 24.5 %collective-permute-start.12 = (bf16[4,512,128]{2,1,0:T(8,128)(2,1)}, bf16[4,512,128]{2,1,0:T(8,128)(2,1)S(1)}, u32[]{:S(2)}, u32[]{:S(2)}) collective-permute-start(bf16[4,512,128]{2,1,0:T(8,128)(2,1)} %get-tuple-element.56), channel_id=1, source_target_pairs={{0,16},{8,24},{16,0},{24,8},{1,17},{9,25},{17,1},{25,9},{2,18},{10... | collective-permute-start | bytes 1572872 | tf_op jit(solution)/shard_map/ppermute | solution.py:22
  105.5 22.4 %collective-permute-start.13 = (bf16[4,512,128]{2,1,0:T(8,128)(2,1)}, bf16[4,512,128]{2,1,0:T(8,128)(2,1)S(1)}, u32[]{:S(2)}, u32[]{:S(2)}) collective-permute-start(bf16[4,512,128]{2,1,0:T(8,128)(2,1)} %get-tuple-element.57), channel_id=1, source_target_pairs={{0,24},{8,0},{16,8},{24,16},{1,25},{9,1},{17,9},{25,17},{2,26},{10... | collective-permute-start | bytes 1572872 | tf_op jit(solution)/shard_map/ppermute | solution.py:22
  127.9 0.8 copy-start.5
  128.7 1.0 copy-start.4
  129.7 1.0 copy-start.6
  156.4 56.2 %all-to-all-start.5 = ((bf16[4,512,1024]{2,1,0:T(8,128)(2,1)}), bf16[4,512,1024]{2,1,0:T(8,128)(2,1)}, u32[]{:S(2)}, u32[]{:S(2)}) async-start(bf16[4,512,1024]{2,1,0:T(8,128)(2,1)} %broadcast_in_dim.25), calls=%async_computation.5 | async-start | bytes 8388608 | tf_op jit(solution)/shard_map/all_to_all | solution.py:403
  163.7 25.7 %collective-permute-start.14 = (bf16[1024,512]{1,0:T(8,128)(2,1)S(1)}, bf16[1024,512]{1,0:T(8,128)(2,1)S(1)}, u32[]{:S(2)}, u32[]{:S(2)}) collective-permute-start(bf16[1024,512]{1,0:T(8,128)(2,1)S(1)} %fusion.5.f0), channel_id=1, source_target_pairs={{0,32},{32,64},{64,96},{96,0},{1,33},{33,65},{65,97},{97,1},{2,34}... | collective-permute-start | bytes 3145736 | tf_op jit(solution)/shard_map/ppermute | solution.py:22
  165.4 47.3 %collective-permute-start.15 = (bf16[1024,512]{1,0:T(8,128)(2,1)S(1)}, bf16[1024,512]{1,0:T(8,128)(2,1)S(1)}, u32[]{:S(2)}, u32[]{:S(2)}) collective-permute-start(bf16[1024,512]{1,0:T(8,128)(2,1)S(1)} %fusion.5.f0), channel_id=1, source_target_pairs={{0,64},{32,96},{64,0},{96,32},{1,65},{33,97},{65,1},{97,33},{2,66}... | collective-permute-start | bytes 3145736 | tf_op jit(solution)/shard_map/ppermute | solution.py:22
  168.0 44.6 %collective-permute-start.16 = (bf16[1024,512]{1,0:T(8,128)(2,1)S(1)}, bf16[1024,512]{1,0:T(8,128)(2,1)}, u32[]{:S(2)}, u32[]{:S(2)}) collective-permute-start(bf16[1024,512]{1,0:T(8,128)(2,1)S(1)} %fusion.5.f0), channel_id=1, source_target_pairs={{0,96},{32,0},{64,32},{96,64},{1,97},{33,1},{65,33},{97,65},{2,98}... | collective-permute-start | bytes 3145736 | tf_op jit(solution)/shard_map/ppermute | solution.py:22
  218.5 7.9 %collective-permute-start.19 = (bf16[4,512,512]{2,1,0:T(8,128)(2,1)}, bf16[4,512,512]{2,1,0:T(8,128)(2,1)}, u32[]{:S(2)}, u32[]{:S(2)}) collective-permute-start(bf16[4,512,512]{2,1,0:T(8,128)(2,1)} %product.6), channel_id=1, source_target_pairs={{0,1},{1,0},{2,3},{3,2},{4,5},{5,4},{6,7},{7,6},{8,9},{9,8},{10,11... | collective-permute-start | bytes 6291464 | tf_op jit(solution)/shard_map/ppermute | solution.py:410
  226.4 11.4 %collective-permute-start.17 = (bf16[4,512,512]{2,1,0:T(8,128)(2,1)}, bf16[4,512,512]{2,1,0:T(8,128)(2,1)}, u32[]{:S(2)}, u32[]{:S(2)}) collective-permute-start(bf16[4,512,512]{2,1,0:T(8,128)(2,1)} %product.4), channel_id=1, source_target_pairs={{0,1},{1,0},{2,3},{3,2},{4,5},{5,4},{6,7},{7,6},{8,9},{9,8},{10,11... | collective-permute-start | bytes 6291464 | tf_op jit(solution)/shard_map/ppermute | solution.py:410
  232.0 1.3 copy-start.3
  233.4 30.5 %all-to-all-start.7 = ((bf16[4,512,512]{2,1,0:T(8,128)(2,1)}), bf16[4,512,512]{2,1,0:T(8,128)(2,1)}, u32[]{:S(2)}, u32[]{:S(2)}) async-start(bf16[4,512,512]{2,1,0:T(8,128)(2,1)} %copy-done.3), calls=%async_computation.7 | async-start | bytes 4194304 | tf_op jit(solution)/shard_map/all_to_all | solution.py:414
  243.5 1.4 copy-start.2
  263.8 28.6 %all-to-all-start.6 = ((bf16[4,512,512]{2,1,0:T(8,128)(2,1)}), bf16[4,512,512]{2,1,0:T(8,128)(2,1)S(1)}, u32[]{:S(2)}, u32[]{:S(2)}) async-start(bf16[4,512,512]{2,1,0:T(8,128)(2,1)} %copy-done.2), calls=%async_computation.6 | async-start | bytes 4194304 | tf_op jit(solution)/shard_map/all_to_all | solution.py:414
  269.6 31.0 %collective-permute-start.20 = (bf16[512,512]{1,0:T(8,128)(2,1)S(1)}, bf16[512,512]{1,0:T(8,128)(2,1)S(1)}, u32[]{:S(2)}, u32[]{:S(2)}) collective-permute-start(bf16[512,512]{1,0:T(8,128)(2,1)S(1)} %reduce_sum.45), channel_id=1, source_target_pairs={{0,8},{1,24},{8,0},{9,16},{16,9},{17,25},{24,1},{25,17},{2,10},{3,... | collective-permute-start | bytes 1572872 | tf_op jit(solution)/shard_map/ppermute | solution.py:419
  293.7 14.0 %collective-permute-start.18 = (bf16[512,512]{1,0:T(8,128)(2,1)}, bf16[512,512]{1,0:T(8,128)(2,1)S(1)}, u32[]{:S(2)}, u32[]{:S(2)}) collective-permute-start(bf16[512,512]{1,0:T(8,128)(2,1)} %reduce_sum.44), channel_id=1, source_target_pairs={{0,0},{1,16},{8,8},{9,24},{16,1},{17,17},{24,9},{25,25},{2,2},{3,1... | collective-permute-start | bytes 1572872 | tf_op jit(solution)/shard_map/ppermute | solution.py:419
  308.0 1.5 copy-start.1

commit v5 on v4

--- a/solution.py
+++ b/solution.py
@@ -11,7 +11,6 @@
 CAP = 2
 SIDE = 4
 MAIN = 6
-CHUNKS = 1
 BF = jnp.bfloat16
 F32 = jnp.float32
 VMEM = 40 * 1024 * 1024
@@ -287,38 +286,111 @@
     )(first, *pieces)
 
 
-def product_kernel(has_add, zsel, psel, left_ref, f0, f1, f2, f3, *rest):
-    out_ref = rest[-1]
-    x2 = pl.program_id(0)
-    for s, ref in enumerate((f0, f1, f2, f3)):
-
-        @pl.when(psel[x2] == s)
-        def _(ref=ref):
-            value = jnp.dot(left_ref[0], ref[...], preferred_element_type=F32)
-            if has_add:
-                value += rest[0][0].astype(F32)
-            out_ref[0] = value.astype(BF)
-
-
-def product(zsel, psel, left, columns, add=None):
-    whole = pl.BlockSpec((1024, 512), lambda x2, *_: (0, 0))
-    tile = pl.BlockSpec((1, 512, 512), lambda x2, *_: (x2, 0, 0))
-    specs = [pl.BlockSpec((1, 512, 1024), lambda x2, zsel, psel: (zsel[0], 0, 0))] + [whole] * 4
-    operands = [left, *columns]
-    if add is not None:
-        specs.append(tile)
-        operands.append(add)
-    grid_spec = pltpu.PrefetchScalarGridSpec(
-        num_scalar_prefetch=2, grid=(SIDE,), in_specs=specs, out_specs=tile
-    )
+def product_kernel(rows_cut, columns_cut, has_add, filled, zsel, way, *refs):
+    refs, count = list(refs), len(columns_cut)
+
+    def halves(cut):
+        if cut:
+            return refs.pop(0), refs.pop(0)
+        ref = refs.pop(0)
+        half = ref.shape[0] // 2
+        return ref.at[pl.ds(0, half)], ref.at[pl.ds(half, half)]
+
+    rows_hbm = [halves(cut) for cut in rows_cut]
+    columns_hbm = [halves(cut) for cut in columns_cut]
+    if has_add:
+        add_hbm, refs = refs[0], refs[1 + filled :]
+        outs, refs = refs[:SIDE], refs[SIDE:]
+    else:
+        outs, refs = refs[:1], refs[1:]
+    left, right, result, left_sem, right_sem, out_sem, *more = refs
+
+    def left_copy(h, source):
+        return pltpu.make_async_copy(source[h], left.at[pl.ds(256 * h, 256)], left_sem.at[h])
+
+    def right_copy(h, n):
+        return pltpu.make_async_copy(
+            columns_hbm[n][h], right.at[n, pl.ds(512 * h, 512)], right_sem.at[h, n]
+        )
+
+    def out_copy(n, target):
+        return pltpu.make_async_copy(result.at[n], target, out_sem.at[n])
+
+    def add_copy(n):
+        return pltpu.make_async_copy(add_hbm.at[n], more[0].at[n], more[1].at[n])
+
+    for k, source in enumerate(rows_hbm):
+
+        @pl.when(zsel[0] == k)
+        def _(source=source):
+            for h in range(2):
+                left_copy(h, source).start()
+
+    for n in range(count):
+        for h in range(2):
+            right_copy(h, n).start()
+        if has_add:
+            add_copy(n).start()
+    for h in range(2):
+        left_copy(h, rows_hbm[0]).wait()
+    for n in range(count):
+        for h in range(2):
+            right_copy(h, n).wait()
+        value = jnp.dot(left[...], right[n], preferred_element_type=F32)
+        if has_add:
+            add_copy(n).wait()
+            value += more[0][n].astype(F32)
+        result[n] = value.astype(BF)
+        if has_add:
+            for s in range(SIDE):
+
+                @pl.when(way[n] == s)
+                def _(n=n, s=s):
+                    out_copy(n, outs[s]).start()
+
+        else:
+            out_copy(n, outs[0].at[n]).start()
+    for n in range(count):
+        out_copy(n, outs[0] if has_add else outs[0].at[0]).wait()
+
+
+def product(zsel, way, rows, columns, add=None, fill=()):
+    smem = pl.BlockSpec(memory_space=pltpu.SMEM)
+    anywhere = pl.BlockSpec(memory_space=pl.ANY)
+    has_add, count = add is not None, len(columns)
+    tiles = (count, 512, 512)
+    sems = pltpu.SemaphoreType.DMA((count,))
+    scratch = [
+        pltpu.VMEM((512, 1024), BF),
+        pltpu.VMEM((count, 1024, 512), BF),
+        pltpu.VMEM(tiles, BF),
+        pltpu.SemaphoreType.DMA((2,)),
+        pltpu.SemaphoreType.DMA((2, count)),
+        sems,
+    ]
+    cuts = [[isinstance(array, tuple) for array in arrays] for arrays in (rows, columns)]
+    operands = []
+    for array in [*rows, *columns]:
+        operands += array if isinstance(array, tuple) else (array,)
+    aliases = {}
+    if has_add:
+        aliases = {3 + len(operands) + n: n for n in range(len(fill))}
+        operands += [add, *fill]
+        scratch += [pltpu.VMEM(tiles, BF), sems]
+        out_shape = [jax.ShapeDtypeStruct((512, 512), BF)] * SIDE
+    else:
+        out_shape = [jax.ShapeDtypeStruct(tiles, BF)]
     return pl.pallas_call(
-        functools.partial(product_kernel, add is not None),
-        grid_spec=grid_spec,
-        out_shape=jax.ShapeDtypeStruct((SIDE, 512, 512), BF),
-        compiler_params=params(),
-        cost_estimate=cost(4 * 2 * 512 * 512 * 1024, 7 * 2**20),
+        functools.partial(product_kernel, *cuts, has_add, len(fill)),
+        in_specs=[smem] * 2 + [anywhere] * len(operands),
+        out_specs=[anywhere] * len(out_shape),
+        out_shape=out_shape,
+        scratch_shapes=scratch,
+        input_output_aliases=aliases,
+        compiler_params=params(MOST),
+        cost_estimate=cost(count * 2 * 512 * 512 * 1024, (1 + 2 * count) * 2**20),
         name="product",
-    )(zsel, psel, *operands)
+    )(zsel, way, *operands)
 
 
 def per_device(
@@ -363,64 +435,79 @@
 
     overflow = jnp.maximum(lengths(to_x, from_x), lengths(to_z, from_z)) > MAIN
 
-    size = 4 // CHUNKS
-
-    def route(chunk):
-        a_main, a_extra, b_extra, *b_main = transform(
-            chunk * size, size, meta, live_count, three_index, mask, orbitals
-        )
-        a_got = lax.all_to_all(a_main, "z", 0, 0, tiled=True)
-        b_got = [b_main[0]] + [shifted(b_main[s], "x", s) for s in (1, 2, 3)]
-        a_got, *b_got = lax.optimization_barrier((a_got, *b_got))
-
-        def send_extra(a, b):
-            moved = [b[:1]] + [shifted(b[s : s + 1], "x", s) for s in (1, 2, 3)]
-            return lax.all_to_all(a, "z", 0, 0, tiled=True), jnp.concatenate(moved, 0)
-
-        a_extra, b_extra = lax.cond(
-            overflow, send_extra, lambda a, b: (a, b), a_extra, b_extra
-        )
-        (a_sum,) = collect(
-            False, size, codes, x * 4 + steps, steps, z[None], [a_got], a_extra
-        )
-        a_last = lax.all_to_all(a_sum, "x", 0, 0, tiled=True)
-        b_sum = collect(
-            True, size, codes, (x - steps) % 4 * 4 + z, (steps - z) % 4, x[None], b_got, b_extra
-        )
-        b_last = [b_sum[0]] + [shifted(b_sum[s], "z", s) for s in (1, 2, 3)]
-        cut = finish(size, a_last, b_last)
-        return lax.all_to_all(cut, ("y", "c"), 0, 0, tiled=True).reshape(-1, 512)
-
-    (rows,) = [route(chunk) for chunk in range(CHUNKS)]
-
-    spread = (jnp.arange(1024)[:, None] // 16 == jnp.arange(64)[None, :]).astype(BF)
+    size = 4
+
+    spot = jnp.arange(1024)
+    spread = (spot[:, None] // 16 == jnp.arange(64)[None, :]).astype(BF)
     mixing = jnp.dot(jnp.dot(spread, fit, preferred_element_type=F32).astype(BF), spread.T)
-    same = jnp.arange(1024)[:, None] % 16 == jnp.arange(1024)[None, :] % 16
+    same = spot[:, None] % 16 == spot[None, :] % 16
     mixing = jnp.where(same, mixing, 0).astype(BF)
 
+    a_main, a_extra, b_extra, *b_main = transform(
+        0, size, meta, live_count, three_index, mask, orbitals
+    )
+    a_got = lax.all_to_all(a_main, "z", 0, 0, tiled=True)
+    b_got = [b_main[0]] + [shifted(b_main[s], "x", s) for s in (1, 2, 3)]
+    a_got, *b_got = lax.optimization_barrier((a_got, *b_got))
+
+    def send_extra(a, b):
+        moved = [b[:1]] + [shifted(b[s : s + 1], "x", s) for s in (1, 2, 3)]
+        return lax.all_to_all(a, "z", 0, 0, tiled=True), jnp.concatenate(moved, 0)
+
+    a_extra, b_extra = lax.cond(overflow, send_extra, lambda a, b: (a, b), a_extra, b_extra)
+    (a_sum,) = collect(False, size, codes, x * 4 + steps, steps, z[None], [a_got], a_extra)
+    a_last = lax.all_to_all(a_sum, "x", 0, 0, tiled=True)
+    b_sum = collect(
+        True, size, codes, (x - steps) % 4 * 4 + z, (steps - z) % 4, x[None], b_got, b_extra
+    )
+    b_last = [b_sum[0]] + [shifted(b_sum[s], "z", s) for s in (1, 2, 3)]
+
+    cut = finish(size, a_last, b_last)
+    rows = lax.all_to_all(cut, ("y", "c"), 0, 0, tiled=True).reshape(1024, 512)
+    turned = rows.T
+    beside = [shifted(turned, "z", s) for s in (1, 3)]
     fitted = jnp.dot(mixing, rows, preferred_element_type=F32).astype(BF)
-    columns = [fitted] + [shifted(fitted, "x", s) for s in (1, 2, 3)]
-    left = lax.all_to_all(
-        jnp.broadcast_to(rows.T[None], (4, 512, 1024)), "z", 0, 0, tiled=True
-    )
-
-    psel = ((x - jnp.arange(4)) % 4).astype(jnp.int32)
-    turns = [((z + t) % 2)[None] for t in range(2)]
-    theirs = [product(2 * (1 - c) + turn, psel, left, columns) for turn in turns]
-    theirs = [lax.ppermute(part, "c", swap) for part in theirs]
-    got = []
-    for t in range(2):
-        partial = product(2 * c + turns[t], psel, left, columns, theirs[t])
-        parts = lax.all_to_all(partial, "y", 0, 0, tiled=True)
-        tile = jnp.sum(parts.astype(F32), 0).astype(BF)
+    early = [fitted] + [shifted(fitted, "x", s) for s in (1, 3)]
+    *beside, early_next, early_last = lax.optimization_barrier((*beside, early[1], early[2]))
+    early = [fitted, early_next, early_last]
+    onward = (early[1][:512], early[2][512:], beside[0][:256], beside[1][256:])
+    *onward, early[0] = lax.optimization_barrier((*onward, fitted))
+    late = [(shifted(onward[0], "x", 1), shifted(onward[1], "x", 3))]
+    across = [turned, (shifted(onward[2], "z", 1), shifted(onward[3], "z", 3))]
+
+    def choose(owner, turn):
+        return ((z - 2 * owner - turn) % 4 // 2)[None]
+
+    way = ((x - y - jnp.array([0, 1, 3, 2])) % 4).astype(jnp.int32)
+    turn = (z + 1) % 2
+    other, mine = choose(1 - c, turn), choose(c, turn)
+    (part,) = product(other, way, beside, early)
+    part = lax.ppermute(part, "c", swap)
+    tiles = product(mine, way[:3], beside, early, part)
+    *tiles, top, bottom, low, high = lax.optimization_barrier((*tiles, *late[0], *across[1]))
+    late, across = [(top, bottom)], [turned, (low, high)]
+    (part,) = product(other, way, beside, late)
+    part = lax.ppermute(part, "c", swap)
+    odd = product(mine, way[3:], beside, late, part, tiles)
+
+    turn = z % 2
+    other, mine = choose(1 - c, turn), choose(c, turn)
+    other, *odd = lax.optimization_barrier((other, *odd))
+    (part,) = product(other, way, across, early + late)
+    part = lax.ppermute(part, "c", swap)
+    even = product(mine, way, across, early + late, part)
+    got = [None, None]
+    for t, tiles in ((1, odd), (0, even)):
+        parts = [tiles[0]] + [shifted(tiles[s], "y", s) for s in (1, 2, 3)]
+        tile = sum(part.astype(F32) for part in parts).astype(BF)
         pairs = [
             (zz * 2 + k, (2 * k + (zz + t) % 2) * 2 + zz // 2) for zz in range(4) for k in range(2)
         ]
-        got.append(lax.ppermute(tile, ("z", "c"), pairs).astype(F32))
+        got[t] = lax.ppermute(tile, ("z", "c"), pairs).astype(F32)
     scale = 8192 ** (-0.5)
-    even = z % 2 == 0
-    first = jnp.where(even, got[0], got[1]) * scale
-    second = jnp.where(even, got[1], got[0]) * scale
+    level = z % 2 == 0
+    first = jnp.where(level, got[0], got[1]) * scale
+    second = jnp.where(level, got[1], got[0]) * scale
     return jnp.concatenate([first, second], 1)
 
 

time: 311 us -> 300 us (0.965)
  blocking collectives: 21.3 us -> 0 us
  Pallas kernels: 43.9 us -> 53.1 us
  waiting for transfers between devices: 151 us -> 142 us
  starting transfers between devices: 62.5 us -> 68.9 us
    all_to_all x5 -> x3, waiting for transfers between devices: 37.9 us -> 14.7 us  [the longest x1 14.7 us: per_device(): rows = lax.all_to_all(cut, ('y', 'c'), 0, 0, tiled=True).reshape(1024, 512)]
    all_to_all x1 -> x0, blocking collectives: 21.3 us -> none  [route(): return lax.all_to_all(cut, ('y', 'c'), 0, 0, tiled=True).reshape(-1, 512)]
    ppermute x12 -> x23, waiting for transfers between devices: 102 us -> 114 us  [shifted(): lax.ppermute(value, axis, [(i, (i + shift) % SIDE) for i in range(SIDE)])]
    ppermute x12 -> x23, starting transfers between devices: 16.3 us -> 27.7 us  [shifted(): lax.ppermute(value, axis, [(i, (i + shift) % SIDE) for i in range(SIDE)])]
    pallas_call x4 -> x6, Pallas kernels: 23 us -> 33.8 us  [product(): pl.pallas_call(functools.partial(product_kernel, *cuts, has_add, len(fill...]
    all_to_all x5 -> x3, starting transfers between devices: 20.4 us -> 13.7 us  [the longest x1 5.92 us: per_device(): rows = lax.all_to_all(cut, ('y', 'c'), 0, 0, tiled=True).reshape(1024, 512)]
    slice x0 -> x5, local copies, waits for them, and re-layouts: none -> 5.41 us  [the longest x4 4.78 us: per_device(): onward = (early[1][:512], early[2][512:], beside[0][:256], beside[1][256:])]
    reduce_sum x2 -> x0, other arithmetic: 3.42 us -> none  [per_device(): tile = jnp.sum(parts.astype(F32), 0).astype(BF)]
  transfers between devices with their start and end apart: 24 -> 34, of which waited for: 13 -> 22; matrix products, arithmetic and copies ran while one was open for 4% -> 5% of each run, Pallas kernels for 8% -> 7%
where the time goes in v5:
time: 300 us; the launch traced here: 298 us
  waiting for transfers between devices  142 us (47%)
  starting transfers between devices  68.9 us (23%)
  Pallas kernels  53.1 us (18%)
  local copies, waits for them, and re-layouts  19 us (6%)
  other arithmetic  9.48 us (3%)
  matrix products  3.31 us (1%)
    ppermute x23, waiting for transfers between devices, shifted(): lax.ppermute(value, axis, [(i, (i + shift) % SIDE) for i in range(SIDE)])  114 us
    pallas_call x6, Pallas kernels, product(): pl.pallas_call(functools.partial(product_kernel, *cuts, has_add, len(fill...  33.8 us
    ppermute x23, starting transfers between devices, shifted(): lax.ppermute(value, axis, [(i, (i + shift) % SIDE) for i in range(SIDE)])  27.7 us
    all_to_all x1, waiting for transfers between devices, per_device(): rows = lax.all_to_all(cut, ('y', 'c'), 0, 0, tiled=True).reshape(1024, 512)  14.7 us
    pallas_call x2, Pallas kernels, collect(): pl.pallas_call(functools.partial(collect_kernel, along_x, size), in_specs...  11.1 us
    ppermute x2, starting transfers between devices, per_device(): got[t] = lax.ppermute(tile, ('z', 'c'), pairs).astype(F32)  9.94 us
    all_to_all x1, starting transfers between devices, per_device(): lax.all_to_all(jnp.broadcast_to(sent[None], (16, 272, 128)), ('x', 'z'),...  8.43 us
    unnamed x57, local copies, waits for them, and re-layouts  7.79 us
  transfers between devices with their start and end apart: 34, of which 22 were waited for; matrix products, arithmetic and copies ran while one was open for 5% of the time, Pallas kernels for 7%

profile of v5, /device:TPU:1, one launch (start us, length us, event | category | flops | bytes accessed | tf_op | source)
XLA Modules:
  0.0 298.0 jit_solution(5164786206304502378)
XLA Ops:
  1.5 1.1 broadcast_in_dim.29
  2.6 8.4 %all-to-all-start.1 = ((bf16[16,272,128]{2,1,0:T(8,128)(2,1)}), bf16[16,272,128]{2,1,0:T(8,128)(2,1)S(1)}, u32[]{:S(2)}, u32[]{:S(2)}) async-start(bf16[16,272,128]{2,1,0:T(8,128)(2,1)} %broadcast_in_dim.29), calls=%async_computation.1 | async-start | bytes 2228224 | tf_op jit(solution)/shard_map/all_to_all | solution.py:417
  11.0 1.0 collective-permute-start.3
  13.9 1.8 plan.1.meta
  15.7 2.8 collective-permute-start.6
  19.6 3.2 %collective-permute-done.5 = bf16[16,64]{1,0:T(8,128)(2,1)S(1)} collective-permute-done((bf16[16,64]{1,0:T(8,128)(2,1)S(1)}, bf16[16,64]{1,0:T(8,128)(2,1)S(1)}, u32[]{:S(2)}, u32[]{:S(2)}) %collective-permute-start.5) | collective-permute-done | bytes 2080 | tf_op jit(solution)/shard_map/ppermute | solution.py:21
  23.4 3.7 %all-to-all-done.1.refs_0_ = bf16[16,272,128]{2,1,0:T(8,128)(2,1)S(1)} async-done(((bf16[16,272,128]{2,1,0:T(8,128)(2,1)}), bf16[16,272,128]{2,1,0:T(8,128)(2,1)S(1)}, u32[]{:S(2)}, u32[]{:S(2)}) %all-to-all-start.1) | async-done | bytes 1114144 | tf_op jit(solution)/shard_map/all_to_all | solution.py:417
  27.2 3.5 %collective-permute-start.7 = (bf16[16,272,128]{2,1,0:T(8,128)(2,1)S(1)}, bf16[16,272,128]{2,1,0:T(8,128)(2,1)}, u32[]{:S(2)}, u32[]{:S(2)}) collective-permute-start(bf16[16,272,128]{2,1,0:T(8,128)(2,1)S(1)} %all-to-all-done.1.refs_0_), channel_id=1, source_target_pairs={{0,1},{1,0},{2,3},{3,2},{4,5},{5,4},{6,7},{7,6},{8,9},{9,8},{10,11... | collective-permute-start | bytes 3342344 | tf_op jit(solution)/shard_map/ppermute | solution.py:425
  31.1 1.2 copy.33.mask_ref
  35.1 4.1 %transform.1 = (bf16[4,6,4,128,128]{4,3,2,1,0:T(8,128)(2,1)}, bf16[4,2,4,128,128]{4,3,2,1,0:T(8,128)(2,1)}, bf16[4,2,4,128,128]{4,3,2,1,0:T(8,128)(2,1)S(1)}, bf...) custom-call(s32[7,16]{1,0:T(8,128)} %plan.1.meta, ...), custom_call_target="tpu_custom_call" | custom-call | flops 536870912 | bytes 8388608 | tf_op jit(solution)/shard_map/transform/pallas_call | solution.py:146
  39.3 1.0 copy-done.12
  40.3 4.0 %all-to-all-start.2 = ((bf16[4,6,4,128,128]{4,3,2,1,0:T(8,128)(2,1)}), bf16[4,6,4,128,128]{4,3,2,1,0:T(8,128)(2,1)S(1)}, u32[]{:S(2)}, u32[]{:S(2)}) async-start(bf16[4,6,4,128,128]{4,3,2,1,0:T(8,128)(2,1)} %get-tuple-element.74), calls=%async_computation.2 | async-start | bytes 6291456 | tf_op jit(solution)/shard_map/all_to_all | solution.py:449
  44.3 1.6 collective-permute-start.8
  45.9 2.6 collective-permute-start.9
  49.4 1.3 fusion.31.codes
  50.7 14.6 %collective-permute-done.8.refs_1_ = bf16[6,4,128,128]{3,2,1,0:T(8,128)(2,1)} collective-permute-done((bf16[6,4,128,128]{3,2,1,0:T(8,128)(2,1)}, bf16[6,4,128,128]{3,2,1,0:T(8,128)(2,1)}, u32[]{:S(2)}, u32[]{:S(2)}) %collective-permute-start.8) | collective-permute-done | bytes 786464 | tf_op jit(solution)/shard_map/ppermute | solution.py:21
  65.3 18.0 %collective-permute-done.9.refs_2_ = bf16[6,4,128,128]{3,2,1,0:T(8,128)(2,1)} collective-permute-done((bf16[6,4,128,128]{3,2,1,0:T(8,128)(2,1)}, bf16[6,4,128,128]{3,2,1,0:T(8,128)(2,1)}, u32[]{:S(2)}, u32[]{:S(2)}) %collective-permute-start.9) | collective-permute-done | bytes 786464 | tf_op jit(solution)/shard_map/ppermute | solution.py:21
  83.9 1.1 copy-done.8
  84.9 5.3 %collect.2 = bf16[4,4,512,128]{3,2,1,0:T(8,128)(2,1)} custom-call(s32[16,16]{1,0:T(8,128)} %fusion.31.codes, s32[4]{0:T(128)} %iota_add_fusion.source, s32[4]{0:T(128)} %iota.46.place, s32[1]{0:T(128)} %bitcast.12.mine, bf16[4,6,4,128,128]{4,3,2,1,0:T(8,128)(2,1)} %copy-done.8, bf16[4,2,4,128,128]{4,3,2,1,0:T(8,128)(2,1)} %get-tuple-element.82.refs_1_), custom_call_target="tpu_custom_call" | custom-call | flops 4194304 | bytes 6291456 | tf_op jit(solution)/shard_map/collect/pallas_call | solution.py:243
  90.2 3.8 %all-to-all-start.3 = ((bf16[4,4,512,128]{3,2,1,0:T(8,128)(2,1)}), bf16[4,4,512,128]{3,2,1,0:T(8,128)(2,1)S(1)}, u32[]{:S(2)}, u32[]{:S(2)}) async-start(bf16[4,4,512,128]{3,2,1,0:T(8,128)(2,1)} %collect.2), calls=%async_computation.3 | async-start | bytes 4194304 | tf_op jit(solution)/shard_map/all_to_all | solution.py:459
  94.6 5.9 %collect.3 = (bf16[4,512,128]{2,1,0:T(8,128)(2,1)}, bf16[4,512,128]{2,1,0:T(8,128)(2,1)}, bf16[4,512,128]{2,1,0:T(8,128)(2,1)}, bf16[4,512,128]{2,1,0:T(8,128)(2,1)}) custom-call(s32[16,16]{1,0:T(8,128)} %fusion.31.codes, s32[4]{0:T(128)} %get-tuple-element.143.source, s32[4]{0:T(128)} %get-tuple-element.142.place, s32[1]{0:T(128)} %bitcast.11.mine, ...), custom_call_target="tpu_custom_call" | custom-call | flops 4194304 | bytes 6291456 | tf_op jit(solution)/shard_map/collect/pallas_call | solution.py:243
  101.3 2.2 collective-permute-start.12
  103.6 1.5 collective-permute-start.13
  105.1 9.6 %collective-permute-done.11.refs_1_ = bf16[4,512,128]{2,1,0:T(8,128)(2,1)S(1)} collective-permute-done((bf16[4,512,128]{2,1,0:T(8,128)(2,1)}, bf16[4,512,128]{2,1,0:T(8,128)(2,1)S(1)}, u32[]{:S(2)}, u32[]{:S(2)}) %collective-permute-start.11) | collective-permute-done | bytes 524320 | tf_op jit(solution)/shard_map/ppermute | solution.py:21
  114.6 11.2 %collective-permute-done.12.refs_2_ = bf16[4,512,128]{2,1,0:T(8,128)(2,1)S(1)} collective-permute-done((bf16[4,512,128]{2,1,0:T(8,128)(2,1)}, bf16[4,512,128]{2,1,0:T(8,128)(2,1)S(1)}, u32[]{:S(2)}, u32[]{:S(2)}) %collective-permute-start.12) | collective-permute-done | bytes 524320 | tf_op jit(solution)/shard_map/ppermute | solution.py:21
  127.5 1.0 copy-done.2
  128.6 1.0 copy-done.4
  129.6 2.3 finish.1
  131.9 5.9 %all-to-all-start.4 = ((bf16[8,8,16,512]{3,2,1,0:T(8,128)(2,1)}), bf16[8,8,16,512]{3,2,1,0:T(8,128)(2,1)S(1)}, u32[]{:S(2)}, u32[]{:S(2)}) async-start(bf16[8,8,16,512]{3,2,1,0:T(8,128)(2,1)} %finish.1), calls=%async_computation.4 | async-start | bytes 2097152 | tf_op jit(solution)/shard_map/all_to_all | solution.py:466
  138.2 14.7 %all-to-all-done.4 = bf16[8,8,16,512]{3,2,1,0:T(8,128)(2,1)S(1)} async-done(((bf16[8,8,16,512]{3,2,1,0:T(8,128)(2,1)}), bf16[8,8,16,512]{3,2,1,0:T(8,128)(2,1)S(1)}, u32[]{:S(2)}, u32[]{:S(2)}) %all-to-all-start.4) | async-done | bytes 1048608 | tf_op jit(solution)/shard_map/all_to_all | solution.py:466
  152.9 1.3 copy.34
  154.2 2.3 collective-permute-start.15
  156.5 2.9 fusion.5.refs_2_.refs_3_
  159.5 2.0 collective-permute-start.17
  162.1 16.4 %collective-permute-done.15.refs_1_ = bf16[512,1024]{1,0:T(8,128)(2,1)S(1)} collective-permute-done((bf16[512,1024]{1,0:T(8,128)(2,1)}, bf16[512,1024]{1,0:T(8,128)(2,1)S(1)}, u32[]{:S(2)}, u32[]{:S(2)}) %collective-permute-start.15) | collective-permute-done | bytes 1048608 | tf_op jit(solution)/shard_map/ppermute | solution.py:21
  178.5 3.1 %collective-permute-done.14.refs_0_ = bf16[512,1024]{1,0:T(8,128)(2,1)} collective-permute-done((bf16[512,1024]{1,0:T(8,128)(2,1)}, bf16[512,1024]{1,0:T(8,128)(2,1)}, u32[]{:S(2)}, u32[]{:S(2)}) %collective-permute-start.14) | collective-permute-done | bytes 1048608 | tf_op jit(solution)/shard_map/ppermute | solution.py:21
  181.6 1.7 collective-permute-done.17.refs_4_.refs_5_
  183.2 2.9 collective-permute-done.16.refs_3_.refs_4_
  186.2 2.2 slice.37
  190.9 5.7 %product.6 = bf16[3,512,512]{2,1,0:T(8,128)(2,1)} custom-call(s32[1]{0:T(128)} %bitcast.19.zsel, s32[4]{0:T(128)} %and_select_fusion.3.way, bf16[512,1024]{1,0:T(8,128)(2,1)} %collective-permute-done.14.refs_0_, bf16[512,1024]{1,0:T(8,128)(2,1)} %copy-done.7, bf16[1024,512]{1,0:T(8,128)(2,1)} %fusion.5.refs_2_.refs_3_, bf16[1024,512]{1,0:T(8,128)(2,1)} %copy-done.6, ...), custom_call_target="tpu_custom_call" | custom-call | flops 1610612736 | bytes 7340032 | tf_op jit(solution)/shard_map/product/pallas_call | solution.py:383
  196.6 2.1 collective-permute-start.18
  198.8 2.7 collective-permute-start.20
  202.3 1.8 collective-permute-start.22
  204.1 5.9 %product.7 = (bf16[512,512]{1,0:T(8,128)(2,1)}, bf16[512,512]{1,0:T(8,128)(2,1)}, bf16[512,512]{1,0:T(8,128)(2,1)}, bf16[512,512]{1,0:T(8,128)(2,1)}) custom-call(s32[1]{0:T(128)} %bitcast.18.zsel, s32[3]{0:T(128)} %bitcast.49, bf16[512,1024]{1,0:T(8,128)(2,1)} %collective-permute-done.14.refs_0_, bf16[512,1024]{1,0:T(8,128)(2,1)} %copy-done.7, ...), custom_call_target="tpu_custom_call" | custom-call | flops 1610612736 | bytes 7340032 | tf_op jit(solution)/shard_map/product/pallas_call | solution.py:383
  210.0 3.6 %collective-permute-done.19.refs_2_.refs_6_ = bf16[512,512]{1,0:T(8,128)(2,1)S(1)} collective-permute-done((bf16[512,512]{1,0:T(8,128)(2,1)}, bf16[512,512]{1,0:T(8,128)(2,1)S(1)}, u32[]{:S(2)}, u32[]{:S(2)}) %collective-permute-start.19) | collective-permute-done | bytes 524320 | tf_op jit(solution)/shard_map/ppermute | solution.py:21
  213.7 2.0 collective-permute-done.21.refs_1_
  215.7 3.7 %product.8 = bf16[1,512,512]{2,1,0:T(8,128)(2,1)} custom-call(s32[1]{0:T(128)} %bitcast.19.zsel, s32[4]{0:T(128)} %and_select_fusion.3.way, bf16[512,1024]{1,0:T(8,128)(2,1)} %collective-permute-done.14.refs_0_, bf16[512,1024]{1,0:T(8,128)(2,1)} %copy-done.7, bf16[512,512]{1,0:T(8,128)(2,1)} %copy-done.10, bf16[512,512]{1,0:T(8,128)(2,1)} %copy-done.11), custom_call_target="tpu_custom_call" | custom-call | flops 536870912 | bytes 3145728 | tf_op jit(solution)/shard_map/product/pallas_call | solution.py:383
  219.5 1.6 collective-permute-start.23
  221.7 1.1 collective-permute-done.23.refs_4_
  223.6 3.9 %product.9 = (bf16[512,512]{1,0:T(8,128)(2,1)}, bf16[512,512]{1,0:T(8,128)(2,1)}, bf16[512,512]{1,0:T(8,128)(2,1)}, bf16[512,512]{1,0:T(8,128)(2,1)}) custom-call(s32[1]{0:T(128)} %bitcast.18.zsel, s32[1]{0:T(128)} %slice.39.way, ...), custom_call_target="tpu_custom_call", output_to_operand_aliasing={{0}: (7, {}), {1}: (8, {}), {2}: (9, {}), {3}: (10, {})} | custom-call | flops 536870912 | bytes 3145728 | tf_op jit(solution)/shard_map/product/pallas_call | solution.py:383
  227.5 6.6 %product.10 = bf16[4,512,512]{2,1,0:T(8,128)(2,1)} custom-call(s32[1]{0:T(128)} %bitcast.20.zsel, s32[4]{0:T(128)} %and_select_fusion.3.way, bf16[512,1024]{1,0:T(8,128)(2,1)} %bitcast.17.refs_0_, bf16[256,1024]{1,0:T(8,128)(2,1)} %copy-done.15, bf16[256,1024]{1,0:T(8,128)(2,1)} %copy-done.16, bf16[1024,512]{1,0:T(8,128)(2,1)} %fusion.5.refs_2_.refs_3_, ...), custom_call_target="tpu_custom_call" | custom-call | flops 2147483648 | bytes 9437184 | tf_op jit(solution)/shard_map/product/pallas_call | solution.py:383
  234.1 1.0 collective-permute-start.24
  235.3 1.8 collective-permute-start.30
  237.8 1.3 collective-permute-done.24.refs_8_
  239.1 1.3 copy-done.14
  240.4 8.1 %product.11 = (bf16[512,512]{1,0:T(8,128)(2,1)}, bf16[512,512]{1,0:T(8,128)(2,1)}, bf16[512,512]{1,0:T(8,128)(2,1)}, bf16[512,512]{1,0:T(8,128)(2,1)}) custom-call(s32[1]{0:T(128)} %bitcast.zsel, s32[4]{0:T(128)} %and_select_fusion.3.way, bf16[512,1024]{1,0:T(8,128)(2,1)} %bitcast.17.refs_0_, bf16[256,1024]{1,0:T(8,128)(2,1)} %copy-done.15, ...), custom_call_target="tpu_custom_call" | custom-call | flops 2147483648 | bytes 9437184 | tf_op jit(solution)/shard_map/product/pallas_call | solution.py:383
  248.8 1.8 collective-permute-start.26
  250.5 10.2 %collective-permute-done.29 = bf16[512,512]{1,0:T(8,128)(2,1)} collective-permute-done((bf16[512,512]{1,0:T(8,128)(2,1)S(1)}, bf16[512,512]{1,0:T(8,128)(2,1)}, u32[]{:S(2)}, u32[]{:S(2)}) %collective-permute-start.29) | collective-permute-done | bytes 524320 | tf_op jit(solution)/shard_map/ppermute | solution.py:21
  261.4 1.6 add_convert_fusion
  263.0 4.6 %collective-permute-start.32 = (bf16[512,512]{1,0:T(8,128)(2,1)S(1)}, bf16[512,512]{1,0:T(8,128)(2,1)S(1)}, u32[]{:S(2)}, u32[]{:S(2)}) collective-permute-start(bf16[512,512]{1,0:T(8,128)(2,1)S(1)} %add_convert_fusion), channel_id=1, source_target_pairs={{0,8},{1,24},{8,0},{9,16},{16,9},{17,25},{24,1},{25,17},{2,10},{3,... | collective-permute-start | bytes 1572872 | tf_op jit(solution)/shard_map/ppermute | solution.py:506
  267.7 15.8 %collective-permute-done.25 = bf16[512,512]{1,0:T(8,128)(2,1)S(1)} collective-permute-done((bf16[512,512]{1,0:T(8,128)(2,1)}, bf16[512,512]{1,0:T(8,128)(2,1)S(1)}, u32[]{:S(2)}, u32[]{:S(2)}) %collective-permute-start.25) | collective-permute-done | bytes 524320 | tf_op jit(solution)/shard_map/ppermute | solution.py:21
  284.1 5.3 %collective-permute-start.28 = (bf16[512,512]{1,0:T(8,128)(2,1)S(1)}, bf16[512,512]{1,0:T(8,128)(2,1)S(1)}, u32[]{:S(2)}, u32[]{:S(2)}) collective-permute-start(bf16[512,512]{1,0:T(8,128)(2,1)S(1)} %add_convert_fusion.1), channel_id=1, source_target_pairs={{0,0},{1,16},{8,8},{9,24},{16,1},{17,17},{24,9},{25,25},{2,2},{3,1... | collective-permute-start | bytes 1572872 | tf_op jit(solution)/shard_map/ppermute | solution.py:506
  289.4 6.8 %collective-permute-done.28 = bf16[512,512]{1,0:T(8,128)(2,1)S(1)} collective-permute-done((bf16[512,512]{1,0:T(8,128)(2,1)S(1)}, bf16[512,512]{1,0:T(8,128)(2,1)S(1)}, u32[]{:S(2)}, u32[]{:S(2)}) %collective-permute-start.28) | collective-permute-done | bytes 524320 | tf_op jit(solution)/shard_map/ppermute | solution.py:506
  296.6 1.5 pad_maximum_fusion.1
  (120 shorter events, 19.7 us)
Async XLA Ops:
  0.0 1.4 copy-start
  0.0 12.7 %copy-start.26 = (s32[16,1]{0,1:T(1,128)S(1)}, s32[16,1]{0,1:T(1,128)}, u32[]{:S(2)}) copy-start(s32[16,1]{0,1:T(1,128)} %param.13) | copy-start | bytes 196
  0.0 11.0 %copy-start.25 = (bf16[8,64]{1,0:T(8,128)(2,1)S(1)}, bf16[8,64]{1,0:T(8,128)(2,1)}, u32[]{:S(2)}) copy-start(bf16[8,64]{1,0:T(8,128)(2,1)} %param.18) | copy-start | bytes 3076
  0.0 13.3 %copy-start.23 = (s32[16,8,8]{0,2,1:T(8,128)S(1)}, s32[16,8,8]{0,2,1:T(8,128)}, u32[]{:S(2)}) copy-start(s32[16,8,8]{0,2,1:T(8,128)} %param.12) | copy-start | bytes 12292
  2.6 24.5 %all-to-all-start.1 = ((bf16[16,272,128]{2,1,0:T(8,128)(2,1)}), bf16[16,272,128]{2,1,0:T(8,128)(2,1)S(1)}, u32[]{:S(2)}, u32[]{:S(2)}) async-start(bf16[16,272,128]{2,1,0:T(8,128)(2,1)} %broadcast_in_dim.29), calls=%async_computation.1 | async-start | bytes 2228224 | tf_op jit(solution)/shard_map/all_to_all | solution.py:417
  11.0 4.7 %collective-permute-start.3 = (bf16[8,64]{1,0:T(8,128)(2,1)S(1)}, bf16[8,64]{1,0:T(8,128)(2,1)S(1)}, u32[]{:S(2)}, u32[]{:S(2)}) collective-permute-start(bf16[8,64]{1,0:T(8,128)(2,1)S(1)} %copy-done.25), channel_id=1, source_target_pairs={{0,1},{1,0},{2,3},{3,2},{4,5},{5,4},{6,7},{7,6},{8,9},{9,8},{10,11... | collective-permute-start | bytes 3080 | tf_op jit(solution)/shard_map/ppermute | solution.py:402
  15.7 3.9 %collective-permute-start.6 = (bf16[16,64]{1,0:T(8,128)(2,1)S(1)}, bf16[16,64]{1,0:T(8,128)(2,1)S(1)}, u32[]{:S(2)}, u32[]{:S(2)}) collective-permute-start(bf16[16,64]{1,0:T(8,128)(2,1)S(1)} %maximum_select_fusion.1), channel_id=1, source_target_pairs={{0,6},{2,0},{4,2},{6,4},{1,7},{3,1},{5,3},{7,5},{8,14},{10,8},{12,... | collective-permute-start | bytes 6152 | tf_op jit(solution)/shard_map/ppermute | solution.py:21
  18.5 4.3 %collective-permute-start.5 = (bf16[16,64]{1,0:T(8,128)(2,1)S(1)}, bf16[16,64]{1,0:T(8,128)(2,1)S(1)}, u32[]{:S(2)}, u32[]{:S(2)}) collective-permute-start(bf16[16,64]{1,0:T(8,128)(2,1)S(1)} %maximum_select_fusion.1), channel_id=1, source_target_pairs={{0,4},{2,6},{4,0},{6,2},{1,5},{3,7},{5,1},{7,3},{8,12},{10,14},{12... | collective-permute-start | bytes 6152 | tf_op jit(solution)/shard_map/ppermute | solution.py:21
  18.9 4.0 %collective-permute-start.4 = (bf16[16,64]{1,0:T(8,128)(2,1)S(1)}, bf16[16,64]{1,0:T(8,128)(2,1)S(1)}, u32[]{:S(2)}, u32[]{:S(2)}) collective-permute-start(bf16[16,64]{1,0:T(8,128)(2,1)S(1)} %maximum_select_fusion.1), channel_id=1, source_target_pairs={{0,2},{2,4},{4,6},{6,0},{1,3},{3,5},{5,7},{7,1},{8,10},{10,12},{12... | collective-permute-start | bytes 6152 | tf_op jit(solution)/shard_map/ppermute | solution.py:21
  27.1 8.0 %copy-start.9 = (bf16[16,272,128]{2,1,0:T(8,128)(2,1)}, bf16[16,272,128]{2,1,0:T(8,128)(2,1)S(1)}, u32[]{:S(2)}) copy-start(bf16[16,272,128]{2,1,0:T(8,128)(2,1)S(1)} %all-to-all-done.1.refs_0_) | copy-start | bytes 3342340
  27.2 7.9 %collective-permute-start.7 = (bf16[16,272,128]{2,1,0:T(8,128)(2,1)S(1)}, bf16[16,272,128]{2,1,0:T(8,128)(2,1)}, u32[]{:S(2)}, u32[]{:S(2)}) collective-permute-start(bf16[16,272,128]{2,1,0:T(8,128)(2,1)S(1)} %all-to-all-done.1.refs_0_), channel_id=1, source_target_pairs={{0,1},{1,0},{2,3},{3,2},{4,5},{5,4},{6,7},{7,6},{8,9},{9,8},{10,11... | collective-permute-start | bytes 3342344 | tf_op jit(solution)/shard_map/ppermute | solution.py:425
  31.1 4.0 %copy-start.18 = (bf16[16,272,128]{2,0,1:T(8,128)(2,1)}, bf16[16,272,128]{2,0,1:T(8,128)(2,1)S(1)}, u32[]{:S(2)}) copy-start(bf16[16,272,128]{2,0,1:T(8,128)(2,1)S(1)} %copy.32) | copy-start | bytes 3342340
  39.3 1.0 copy-start.12
  40.3 43.1 %all-to-all-start.2 = ((bf16[4,6,4,128,128]{4,3,2,1,0:T(8,128)(2,1)}), bf16[4,6,4,128,128]{4,3,2,1,0:T(8,128)(2,1)S(1)}, u32[]{:S(2)}, u32[]{:S(2)}) async-start(bf16[4,6,4,128,128]{4,3,2,1,0:T(8,128)(2,1)} %get-tuple-element.74), calls=%async_computation.2 | async-start | bytes 6291456 | tf_op jit(solution)/shard_map/all_to_all | solution.py:449
  44.3 21.1 %collective-permute-start.8 = (bf16[6,4,128,128]{3,2,1,0:T(8,128)(2,1)}, bf16[6,4,128,128]{3,2,1,0:T(8,128)(2,1)}, u32[]{:S(2)}, u32[]{:S(2)}) collective-permute-start(bf16[6,4,128,128]{3,2,1,0:T(8,128)(2,1)} %get-tuple-element.76), channel_id=1, source_target_pairs={{0,32},{32,64},{64,96},{96,0},{1,33},{33,65},{65,97},{97,1},{2,34}... | collective-permute-start | bytes 2359304 | tf_op jit(solution)/shard_map/ppermute | solution.py:21
  45.9 37.5 %collective-permute-start.9 = (bf16[6,4,128,128]{3,2,1,0:T(8,128)(2,1)}, bf16[6,4,128,128]{3,2,1,0:T(8,128)(2,1)}, u32[]{:S(2)}, u32[]{:S(2)}) collective-permute-start(bf16[6,4,128,128]{3,2,1,0:T(8,128)(2,1)} %get-tuple-element.77), channel_id=1, source_target_pairs={{0,64},{32,96},{64,0},{96,32},{1,65},{33,97},{65,1},{97,33},{2,66}... | collective-permute-start | bytes 2359304 | tf_op jit(solution)/shard_map/ppermute | solution.py:21
  48.4 34.9 %collective-permute-start.10 = (bf16[6,4,128,128]{3,2,1,0:T(8,128)(2,1)}, bf16[6,4,128,128]{3,2,1,0:T(8,128)(2,1)}, u32[]{:S(2)}, u32[]{:S(2)}) collective-permute-start(bf16[6,4,128,128]{3,2,1,0:T(8,128)(2,1)} %get-tuple-element.78), channel_id=1, source_target_pairs={{0,96},{32,0},{64,32},{96,64},{1,97},{33,1},{65,33},{97,65},{2,98}... | collective-permute-start | bytes 2359304 | tf_op jit(solution)/shard_map/ppermute | solution.py:21
  83.3 1.6 copy-start.8
  90.2 4.4 %copy-start.13 = (bf16[4,2,4,128,128]{4,3,2,1,0:T(8,128)(2,1)S(1)}, bf16[4,2,4,128,128]{4,3,2,1,0:T(8,128)(2,1)}, u32[]{:S(2)}) copy-start(bf16[4,2,4,128,128]{4,3,2,1,0:T(8,128)(2,1)} %copy-done.12) | copy-start | bytes 3145732
  90.2 37.3 %all-to-all-start.3 = ((bf16[4,4,512,128]{3,2,1,0:T(8,128)(2,1)}), bf16[4,4,512,128]{3,2,1,0:T(8,128)(2,1)S(1)}, u32[]{:S(2)}, u32[]{:S(2)}) async-start(bf16[4,4,512,128]{3,2,1,0:T(8,128)(2,1)} %collect.2), calls=%async_computation.3 | async-start | bytes 4194304 | tf_op jit(solution)/shard_map/all_to_all | solution.py:459
  100.5 14.1 %collective-permute-start.11 = (bf16[4,512,128]{2,1,0:T(8,128)(2,1)}, bf16[4,512,128]{2,1,0:T(8,128)(2,1)S(1)}, u32[]{:S(2)}, u32[]{:S(2)}) collective-permute-start(bf16[4,512,128]{2,1,0:T(8,128)(2,1)} %get-tuple-element.89), channel_id=1, source_target_pairs={{0,8},{8,16},{16,24},{24,0},{1,9},{9,17},{17,25},{25,1},{2,10},{10... | collective-permute-start | bytes 1572872 | tf_op jit(solution)/shard_map/ppermute | solution.py:21
  101.3 24.5 %collective-permute-start.12 = (bf16[4,512,128]{2,1,0:T(8,128)(2,1)}, bf16[4,512,128]{2,1,0:T(8,128)(2,1)S(1)}, u32[]{:S(2)}, u32[]{:S(2)}) collective-permute-start(bf16[4,512,128]{2,1,0:T(8,128)(2,1)} %get-tuple-element.90), channel_id=1, source_target_pairs={{0,16},{8,24},{16,0},{24,8},{1,17},{9,25},{17,1},{25,9},{2,18},{10... | collective-permute-start | bytes 1572872 | tf_op jit(solution)/shard_map/ppermute | solution.py:21
  103.6 23.1 %collective-permute-start.13 = (bf16[4,512,128]{2,1,0:T(8,128)(2,1)}, bf16[4,512,128]{2,1,0:T(8,128)(2,1)S(1)}, u32[]{:S(2)}, u32[]{:S(2)}) collective-permute-start(bf16[4,512,128]{2,1,0:T(8,128)(2,1)} %get-tuple-element.91), channel_id=1, source_target_pairs={{0,24},{8,0},{16,8},{24,16},{1,25},{9,1},{17,9},{25,17},{2,26},{10... | collective-permute-start | bytes 1572872 | tf_op jit(solution)/shard_map/ppermute | solution.py:21
  126.7 0.8 copy-start.3
  127.5 1.0 copy-start.2
  128.6 1.0 copy-start.4
  131.9 21.0 %all-to-all-start.4 = ((bf16[8,8,16,512]{3,2,1,0:T(8,128)(2,1)}), bf16[8,8,16,512]{3,2,1,0:T(8,128)(2,1)S(1)}, u32[]{:S(2)}, u32[]{:S(2)}) async-start(bf16[8,8,16,512]{3,2,1,0:T(8,128)(2,1)} %finish.1), calls=%async_computation.4 | async-start | bytes 2097152 | tf_op jit(solution)/shard_map/all_to_all | solution.py:466
  154.2 7.3 %copy-start.27 = (s32[4]{0:T(128)S(1)}, s32[4]{0:T(128)}, u32[]{:S(2)}) copy-start(s32[4]{0:T(128)} %constant.197) | copy-start | bytes 52
  154.2 24.3 %collective-permute-start.15 = (bf16[512,1024]{1,0:T(8,128)(2,1)}, bf16[512,1024]{1,0:T(8,128)(2,1)S(1)}, u32[]{:S(2)}, u32[]{:S(2)}) collective-permute-start(bf16[512,1024]{1,0:T(8,128)(2,1)} %bitcast.17.refs_0_), channel_id=1, source_target_pairs={{0,24},{8,0},{16,8},{24,16},{1,25},{9,1},{17,9},{25,17},{2,26},{10... | collective-permute-start | bytes 3145736 | tf_op jit(solution)/shard_map/ppermute | solution.py:21
  156.5 25.0 %collective-permute-start.14 = (bf16[512,1024]{1,0:T(8,128)(2,1)}, bf16[512,1024]{1,0:T(8,128)(2,1)}, u32[]{:S(2)}, u32[]{:S(2)}) collective-permute-start(bf16[512,1024]{1,0:T(8,128)(2,1)} %bitcast.17.refs_0_), channel_id=1, source_target_pairs={{0,8},{8,16},{16,24},{24,0},{1,9},{9,17},{17,25},{25,1},{2,10},{10... | collective-permute-start | bytes 3145736 | tf_op jit(solution)/shard_map/ppermute | solution.py:21
  159.5 23.8 %collective-permute-start.17 = (bf16[1024,512]{1,0:T(8,128)(2,1)}, bf16[1024,512]{1,0:T(8,128)(2,1)S(1)}, u32[]{:S(2)}, u32[]{:S(2)}) collective-permute-start(bf16[1024,512]{1,0:T(8,128)(2,1)} %fusion.5.refs_2_.refs_3_), channel_id=1, source_target_pairs={{0,96},{32,0},{64,32},{96,64},{1,97},{33,1},{65,33},{97,65},{2,98}... | collective-permute-start | bytes 3145736 | tf_op jit(solution)/shard_map/ppermute | solution.py:21
  161.5 24.6 %collective-permute-start.16 = (bf16[1024,512]{1,0:T(8,128)(2,1)}, bf16[1024,512]{1,0:T(8,128)(2,1)S(1)}, u32[]{:S(2)}, u32[]{:S(2)}) collective-permute-start(bf16[1024,512]{1,0:T(8,128)(2,1)} %fusion.5.refs_2_.refs_3_), channel_id=1, source_target_pairs={{0,32},{32,64},{64,96},{96,0},{1,33},{33,65},{65,97},{97,1},{2,34}... | collective-permute-start | bytes 3145736 | tf_op jit(solution)/shard_map/ppermute | solution.py:21
  178.5 12.5 %copy-start.7 = (bf16[512,1024]{1,0:T(8,128)(2,1)}, bf16[512,1024]{1,0:T(8,128)(2,1)S(1)}, u32[]{:S(2)}) copy-start(bf16[512,1024]{1,0:T(8,128)(2,1)S(1)} %collective-permute-done.15.refs_1_) | copy-start | bytes 3145732
  183.2 7.7 %copy-start.5 = (bf16[1024,512]{1,0:T(8,128)(2,1)}, bf16[1024,512]{1,0:T(8,128)(2,1)S(1)}, u32[]{:S(2)}) copy-start(bf16[1024,512]{1,0:T(8,128)(2,1)S(1)} %collective-permute-done.17.refs_4_.refs_5_) | copy-start | bytes 3145732
  186.2 4.8 %copy-start.6 = (bf16[1024,512]{1,0:T(8,128)(2,1)}, bf16[1024,512]{1,0:T(8,128)(2,1)S(1)}, u32[]{:S(2)}) copy-start(bf16[1024,512]{1,0:T(8,128)(2,1)S(1)} %collective-permute-done.16.refs_3_.refs_4_) | copy-start | bytes 3145732
  196.6 7.5 %collective-permute-start.18 = (bf16[3,512,512]{2,1,0:T(8,128)(2,1)}, bf16[3,512,512]{2,1,0:T(8,128)(2,1)}, u32[]{:S(2)}, u32[]{:S(2)}) collective-permute-start(bf16[3,512,512]{2,1,0:T(8,128)(2,1)} %product.6), channel_id=1, source_target_pairs={{0,1},{1,0},{2,3},{3,2},{4,5},{5,4},{6,7},{7,6},{8,9},{9,8},{10,11... | collective-permute-start | bytes 4718600 | tf_op jit(solution)/shard_map/ppermute | solution.py:485
  198.8 14.9 %collective-permute-start.19 = (bf16[512,512]{1,0:T(8,128)(2,1)}, bf16[512,512]{1,0:T(8,128)(2,1)S(1)}, u32[]{:S(2)}, u32[]{:S(2)}) collective-permute-start(bf16[512,512]{1,0:T(8,128)(2,1)} %slice.35), channel_id=1, source_target_pairs={{0,32},{32,64},{64,96},{96,0},{1,33},{33,65},{65,97},{97,1},{2,34}... | collective-permute-start | bytes 1572872 | tf_op jit(solution)/shard_map/ppermute | solution.py:21
  198.8 14.9 %collective-permute-start.20 = (bf16[512,512]{1,0:T(8,128)(2,1)}, bf16[512,512]{1,0:T(8,128)(2,1)S(1)}, u32[]{:S(2)}, u32[]{:S(2)}) collective-permute-start(bf16[512,512]{1,0:T(8,128)(2,1)} %slice.36), channel_id=1, source_target_pairs={{0,96},{32,0},{64,32},{96,64},{1,97},{33,1},{65,33},{97,65},{2,98}... | collective-permute-start | bytes 1572872 | tf_op jit(solution)/shard_map/ppermute | solution.py:21
  201.4 14.3 %collective-permute-start.21 = (bf16[256,1024]{1,0:T(8,128)(2,1)}, bf16[256,1024]{1,0:T(8,128)(2,1)S(1)}, u32[]{:S(2)}, u32[]{:S(2)}) collective-permute-start(bf16[256,1024]{1,0:T(8,128)(2,1)} %slice.37), channel_id=1, source_target_pairs={{0,8},{8,16},{16,24},{24,0},{1,9},{9,17},{17,25},{25,1},{2,10},{10... | collective-permute-start | bytes 1572872 | tf_op jit(solution)/shard_map/ppermute | solution.py:21
  202.3 13.4 %collective-permute-start.22 = (bf16[256,1024]{1,0:T(8,128)(2,1)}, bf16[256,1024]{1,0:T(8,128)(2,1)S(1)}, u32[]{:S(2)}, u32[]{:S(2)}) collective-permute-start(bf16[256,1024]{1,0:T(8,128)(2,1)} %slice.38), channel_id=1, source_target_pairs={{0,24},{8,0},{16,8},{24,16},{1,25},{9,1},{17,9},{25,17},{2,26},{10... | collective-permute-start | bytes 1572872 | tf_op jit(solution)/shard_map/ppermute | solution.py:21
  210.0 11.0 %copy-start.24 = (s32[4]{0:T(128)S(1)}, s32[4]{0:T(128)}, u32[]{:S(2)}) copy-start(s32[4]{0:T(128)} %and_select_fusion.3.way) | copy-start | bytes 52
  213.7 2.1 copy-start.10
  213.7 2.1 copy-start.11
  215.7 11.8 %copy-start.15 = (bf16[256,1024]{1,0:T(8,128)(2,1)}, bf16[256,1024]{1,0:T(8,128)(2,1)S(1)}, u32[]{:S(2)}) copy-start(bf16[256,1024]{1,0:T(8,128)(2,1)S(1)} %collective-permute-done.21.refs_1_) | copy-start | bytes 1572868
  215.7 11.8 %copy-start.16 = (bf16[256,1024]{1,0:T(8,128)(2,1)}, bf16[256,1024]{1,0:T(8,128)(2,1)S(1)}, u32[]{:S(2)}) copy-start(bf16[256,1024]{1,0:T(8,128)(2,1)S(1)} %collective-permute-done.22.refs_2_) | copy-start | bytes 1572868
  219.5 3.3 %collective-permute-start.23 = (bf16[1,512,512]{2,1,0:T(8,128)(2,1)}, bf16[1,512,512]{2,1,0:T(8,128)(2,1)S(1)}, u32[]{:S(2)}, u32[]{:S(2)}) collective-permute-start(bf16[1,512,512]{2,1,0:T(8,128)(2,1)} %product.8), channel_id=1, source_target_pairs={{0,1},{1,0},{2,3},{3,2},{4,5},{5,4},{6,7},{7,6},{8,9},{9,8},{10,11... | collective-permute-start | bytes 1572872 | tf_op jit(solution)/shard_map/ppermute | solution.py:490
  222.8 0.8 copy-start.21
  227.5 7.6 %copy-start.19 = (bf16[512,512]{1,0:T(8,128)(2,1)S(1)}, bf16[512,512]{1,0:T(8,128)(2,1)}, u32[]{:S(2)}) copy-start(bf16[512,512]{1,0:T(8,128)(2,1)} %get-tuple-element.124) | copy-start | bytes 1572868
  227.5 7.8 %copy-start.20 = (bf16[512,512]{1,0:T(8,128)(2,1)S(1)}, bf16[512,512]{1,0:T(8,128)(2,1)}, u32[]{:S(2)}) copy-start(bf16[512,512]{1,0:T(8,128)(2,1)} %get-tuple-element.125) | copy-start | bytes 1572868
  234.1 5.0 %collective-permute-start.24 = (bf16[4,512,512]{2,1,0:T(8,128)(2,1)}, bf16[4,512,512]{2,1,0:T(8,128)(2,1)S(1)}, u32[]{:S(2)}, u32[]{:S(2)}) collective-permute-start(bf16[4,512,512]{2,1,0:T(8,128)(2,1)} %product.10), channel_id=1, source_target_pairs={{0,1},{1,0},{2,3},{3,2},{4,5},{5,4},{6,7},{7,6},{8,9},{9,8},{10,11... | collective-permute-start | bytes 6291464 | tf_op jit(solution)/shard_map/ppermute | solution.py:497
  235.1 25.7 %collective-permute-start.29 = (bf16[512,512]{1,0:T(8,128)(2,1)S(1)}, bf16[512,512]{1,0:T(8,128)(2,1)}, u32[]{:S(2)}, u32[]{:S(2)}) collective-permute-start(bf16[512,512]{1,0:T(8,128)(2,1)S(1)} %copy-done.19), channel_id=1, source_target_pairs={{0,2},{2,4},{4,6},{6,0},{1,3},{3,5},{5,7},{7,1},{8,10},{10,12},{12... | collective-permute-start | bytes 1572872 | tf_op jit(solution)/shard_map/ppermute | solution.py:21
  235.3 25.4 %collective-permute-start.30 = (bf16[512,512]{1,0:T(8,128)(2,1)S(1)}, bf16[512,512]{1,0:T(8,128)(2,1)}, u32[]{:S(2)}, u32[]{:S(2)}) collective-permute-start(bf16[512,512]{1,0:T(8,128)(2,1)S(1)} %copy-done.20), channel_id=1, source_target_pairs={{0,4},{2,6},{4,0},{6,2},{1,5},{3,7},{5,1},{7,3},{8,12},{10,14},{12... | collective-permute-start | bytes 1572872 | tf_op jit(solution)/shard_map/ppermute | solution.py:21
  237.1 24.3 %collective-permute-start.31 = (bf16[512,512]{1,0:T(8,128)(2,1)}, bf16[512,512]{1,0:T(8,128)(2,1)}, u32[]{:S(2)}, u32[]{:S(2)}) collective-permute-start(bf16[512,512]{1,0:T(8,128)(2,1)} %get-tuple-element.126), channel_id=1, source_target_pairs={{0,6},{2,0},{4,2},{6,4},{1,7},{3,1},{5,3},{7,5},{8,14},{10,8},{12,... | collective-permute-start | bytes 1572872 | tf_op jit(solution)/shard_map/ppermute | solution.py:21
  239.1 1.3 copy-start.14
  240.4 21.0 %copy-start.17 = (bf16[512,512]{1,0:T(8,128)(2,1)S(1)}, bf16[512,512]{1,0:T(8,128)(2,1)}, u32[]{:S(2)}) copy-start(bf16[512,512]{1,0:T(8,128)(2,1)} %get-tuple-element.123) | copy-start | bytes 1572868
  248.4 35.4 %copy-start.22 = (bf16[512,512]{1,0:T(8,128)(2,1)S(1)}, bf16[512,512]{1,0:T(8,128)(2,1)}, u32[]{:S(2)}) copy-start(bf16[512,512]{1,0:T(8,128)(2,1)} %get-tuple-element.119) | copy-start | bytes 1572868
  248.5 35.0 %collective-permute-start.25 = (bf16[512,512]{1,0:T(8,128)(2,1)}, bf16[512,512]{1,0:T(8,128)(2,1)S(1)}, u32[]{:S(2)}, u32[]{:S(2)}) collective-permute-start(bf16[512,512]{1,0:T(8,128)(2,1)} %get-tuple-element.120), channel_id=1, source_target_pairs={{0,2},{2,4},{4,6},{6,0},{1,3},{3,5},{5,7},{7,1},{8,10},{10,12},{12... | collective-permute-start | bytes 1572872 | tf_op jit(solution)/shard_map/ppermute | solution.py:21
  248.8 34.7 %collective-permute-start.26 = (bf16[512,512]{1,0:T(8,128)(2,1)}, bf16[512,512]{1,0:T(8,128)(2,1)S(1)}, u32[]{:S(2)}, u32[]{:S(2)}) collective-permute-start(bf16[512,512]{1,0:T(8,128)(2,1)} %get-tuple-element.121), channel_id=1, source_target_pairs={{0,4},{2,6},{4,0},{6,2},{1,5},{3,7},{5,1},{7,3},{8,12},{10,14},{12... | collective-permute-start | bytes 1572872 | tf_op jit(solution)/shard_map/ppermute | solution.py:21
  260.8 23.1 %collective-permute-start.27 = (bf16[512,512]{1,0:T(8,128)(2,1)}, bf16[512,512]{1,0:T(8,128)(2,1)S(1)}, u32[]{:S(2)}, u32[]{:S(2)}) collective-permute-start(bf16[512,512]{1,0:T(8,128)(2,1)} %get-tuple-element.122), channel_id=1, source_target_pairs={{0,6},{2,0},{4,2},{6,4},{1,7},{3,1},{5,3},{7,5},{8,14},{10,8},{12,... | collective-permute-start | bytes 1572872 | tf_op jit(solution)/shard_map/ppermute | solution.py:21
  263.0 26.4 %collective-permute-start.32 = (bf16[512,512]{1,0:T(8,128)(2,1)S(1)}, bf16[512,512]{1,0:T(8,128)(2,1)S(1)}, u32[]{:S(2)}, u32[]{:S(2)}) collective-permute-start(bf16[512,512]{1,0:T(8,128)(2,1)S(1)} %add_convert_fusion), channel_id=1, source_target_pairs={{0,8},{1,24},{8,0},{9,16},{16,9},{17,25},{24,1},{25,17},{2,10},{3,... | collective-permute-start | bytes 1572872 | tf_op jit(solution)/shard_map/ppermute | solution.py:506
  284.1 12.2 %collective-permute-start.28 = (bf16[512,512]{1,0:T(8,128)(2,1)S(1)}, bf16[512,512]{1,0:T(8,128)(2,1)S(1)}, u32[]{:S(2)}, u32[]{:S(2)}) collective-permute-start(bf16[512,512]{1,0:T(8,128)(2,1)S(1)} %add_convert_fusion.1), channel_id=1, source_target_pairs={{0,0},{1,16},{8,8},{9,24},{16,1},{17,17},{24,9},{25,25},{2,2},{3,1... | collective-permute-start | bytes 1572872 | tf_op jit(solution)/shard_map/ppermute | solution.py:506
  296.6 1.5 copy-start.1
